TPU v7x, 32 devices: a whole 2x2x4 slice. The times are simulated.
32 devices in a mesh: dp: 4 (over z), ctx: 8 (over y, x, core).
Axes of the slice: x: 2, y: 2, z: 4, core: 2. Of those that a mesh axis runs over, the one named last changes fastest.
Arguments:
- source_picture_sequence: bfloat16 [4, 32, 8, 8, 16, 128], P('dp', 'ctx'), may hold values from -6 to 6
- slot_assignment: int32 [32], replicated, may hold values from 0 to 31, as said below
- segment_piece_counts: int32 [4], replicated, may hold values from 1 to 16, 32 in all
- logit_scaling: float32 [4], replicated, may hold values from 1 to 16
- filter_tap_coefficients: bfloat16 [3456, 256], replicated, may hold values from -0.109375 to 0.109375
- triple_linear_matrix: bfloat16 [256, 768], replicated, may hold values from -0.375 to 0.375
- final_linear_matrix: bfloat16 [256, 256], replicated, may hold values from -0.375 to 0.375
- upstream_gradient: bfloat16 [4, 32, 4, 128, 256], P('dp', 'ctx'), may hold values from -6 to 6
Outputs:
- latents: bfloat16 [4, 32, 4, 128, 256], P('dp', 'ctx')
- conv_grad: float32 [3456, 256], P('ctx')
Inputs may be any that keep to these rules, and one draw needn't show every extreme that they name: `slot_assignment`: A permutation of the span numbers; entry i names the span at slot i, held by device i // 4. Each quarter of the span numbers, in order, fills one of the 4 positions on every device. The spans that follow one device's spans lie on at most two devices, at most two on any one device, and so do the spans that precede them; in every draw some device has two spans followed by spans on one other device.
All inputs are finite; a program needn't handle non-finite values.
Results may differ from a plain program's by a relative error of at most 0.0058.
Values may be sent and summed in bfloat16 or wider, within the bound.
No kernel may reach another device: no remote copies, remote signals or barrier semaphores. Data moves between devices by JAX's collectives and lax.ppermute only.
A program may use at most 128 MiB of HBM per device.

v0:
```python
import jax
import jax.numpy as jnp
from jax import lax
from jax.sharding import PartitionSpec as P

masked_score = -1e30


def clip_marks(segment_piece_counts, span_ids):
    clip_ends = jnp.cumsum(segment_piece_counts, dtype=jnp.int32)
    clip_starts = clip_ends - segment_piece_counts
    clip_index = jnp.sum(
        (span_ids[:, None] >= clip_ends[None, :]).astype(jnp.int32), axis=1, dtype=jnp.int32
    )
    opening = jnp.any(span_ids[:, None] == clip_starts[None, :], axis=1)
    return (clip_index, opening)


def locate(span_ids, slot_assignment):
    slot_ids = jnp.arange(slot_assignment.shape[0], dtype=jnp.int32)
    matches = slot_assignment[None, :] == span_ids[:, None]
    return jnp.sum(jnp.where(matches, slot_ids[None, :], 0), axis=1, dtype=jnp.int32)


def conv_patches(frames):
    span_total, unused_len, rows_h, cols_w, channel_in = frames.shape
    padded = jnp.pad(frames, ((0, 0), (0, 0), (1, 1), (1, 1), (0, 0)))
    tap_list = []
    for step_t in range(3):
        for step_h in range(3):
            for step_w in range(3):
                tap_list.append(
                    padded[
                        :,
                        step_t : step_t + 7 : 2,
                        step_h : step_h + rows_h,
                        step_w : step_w + cols_w,
                        :,
                    ]
                )
    return jnp.concatenate(tap_list, axis=-1).reshape(-1, 27 * channel_in)


def timewise_softmax_mixing(
    grid_tile_entries, logit_scaling, triple_linear_matrix, final_linear_matrix, allowance_pattern
):
    channel_width = grid_tile_entries.shape[-1]
    channel_group_index = logit_scaling.shape[0]
    head_size = channel_width // channel_group_index
    values32 = grid_tile_entries.astype(jnp.float32)
    normed = (
        values32 * lax.rsqrt(jnp.mean(values32 * values32, axis=-1, keepdims=True) + 1e-06)
    ).astype(jnp.bfloat16)
    projected = jnp.einsum(
        "gac,cd->gad", normed, triple_linear_matrix, preferred_element_type=jnp.float32
    )
    head_shape = grid_tile_entries.shape[:2] + (channel_group_index, head_size)
    queries = projected[..., :channel_width].reshape(head_shape)
    keys_all = projected[..., channel_width : 2 * channel_width].reshape(head_shape)
    head_values = projected[..., 2 * channel_width :].reshape(head_shape).astype(jnp.bfloat16)
    queries = queries * lax.rsqrt(jnp.sum(queries * queries, axis=-1, keepdims=True) + 1e-06)
    keys_all = keys_all * lax.rsqrt(jnp.sum(keys_all * keys_all, axis=-1, keepdims=True) + 1e-06)
    affinity_logits = jnp.einsum(
        "gahd,gbhd->ghab", queries, keys_all, precision=lax.Precision.HIGHEST
    )
    affinity_logits = affinity_logits * logit_scaling[None, :, None, None]
    affinity_logits = jnp.where(allowance_pattern[None, None], affinity_logits, masked_score)
    highest = jnp.max(affinity_logits, axis=-1, keepdims=True)
    weights = jnp.exp(affinity_logits - highest)
    probabilities = (weights / jnp.sum(weights, axis=-1, keepdims=True)).astype(jnp.bfloat16)
    mixed_heads = jnp.einsum(
        "ghab,gbhd->gahd", probabilities, head_values, preferred_element_type=jnp.float32
    )
    mixed_heads = mixed_heads.astype(jnp.bfloat16).reshape(grid_tile_entries.shape)
    branch = jnp.einsum(
        "gac,cd->gad", mixed_heads, final_linear_matrix, preferred_element_type=jnp.float32
    )
    return (values32 + branch).astype(jnp.bfloat16)


def per_device(
    source_picture_sequence,
    slot_assignment,
    segment_piece_counts,
    logit_scaling,
    filter_tap_coefficients,
    triple_linear_matrix,
    final_linear_matrix,
    upstream_gradient,
):
    my_index = lax.axis_index("ctx")
    local_frames = source_picture_sequence[0]
    slot_count = local_frames.shape[0]
    my_spans = lax.dynamic_slice_in_dim(slot_assignment, my_index * slot_count, slot_count)
    unused_clip, opening = clip_marks(segment_piece_counts, my_spans)
    pred_slot = locate(jnp.maximum(my_spans - 1, 0), slot_assignment)
    tails = local_frames[:, 6:]
    shard_rows = lax.all_gather(tails, "ctx", axis=0, tiled=True)
    inside = (pred_slot >= 0) & (pred_slot < shard_rows.shape[0])
    chosen = shard_rows[jnp.clip(pred_slot, 0, shard_rows.shape[0] - 1)]
    previous = jnp.where(inside[:, None, None, None, None], chosen, jnp.zeros_like(tails))
    previous = jnp.where(opening[:, None, None, None, None], jnp.zeros_like(previous), previous)
    patches = conv_patches(jnp.concatenate([previous, local_frames], axis=1))
    channels = filter_tap_coefficients.shape[1]
    cell_count = local_frames.shape[2] * local_frames.shape[3]
    conv_out = jnp.dot(patches, filter_tap_coefficients, preferred_element_type=jnp.float32).astype(
        jnp.bfloat16
    )
    conv_out = conv_out.reshape(slot_count, 4, cell_count, channels)
    grad_rows = upstream_gradient[0].reshape(-1, channels)
    grad_share = lax.psum_scatter(
        jnp.dot(patches.T, grad_rows, preferred_element_type=jnp.float32),
        "ctx",
        scatter_dimension=0,
        tiled=True,
    )
    conv_grad = lax.psum(grad_share, "dp")
    gathered = lax.all_to_all(conv_out, "ctx", split_axis=2, concat_axis=0, tiled=True)
    frame_total = gathered.shape[0] * 4
    cells_dev = gathered.shape[2]
    location_entry_count = jnp.transpose(
        gathered.reshape(frame_total, cells_dev, channels), (1, 0, 2)
    )
    clip_all, unused_open = clip_marks(segment_piece_counts, slot_assignment)
    frame_clip = jnp.repeat(clip_all, 4)
    frame_time = (slot_assignment[:, None] * 4 + jnp.arange(4, dtype=jnp.int32)[None, :]).reshape(
        -1
    )
    allowance_pattern = (frame_clip[:, None] == frame_clip[None, :]) & (
        frame_time[None, :] <= frame_time[:, None]
    )
    cell_group = 1
    for unused_bit in range(12):
        if (
            cell_group * 2 <= cells_dev
            and cells_dev % (cell_group * 2) == 0
            and (cell_group * frame_total < 512)
        ):
            cell_group = cell_group * 2
    block_list = location_entry_count.reshape(
        cells_dev // cell_group, cell_group, frame_total, channels
    )
    blended_result = lax.map(
        lambda grid_tile_entries: timewise_softmax_mixing(
            grid_tile_entries,
            logit_scaling,
            triple_linear_matrix,
            final_linear_matrix,
            allowance_pattern,
        ),
        block_list,
    )
    blended_result = jnp.transpose(
        blended_result.reshape(cells_dev, frame_total, channels), (1, 0, 2)
    ).reshape(gathered.shape)
    latents = lax.all_to_all(blended_result, "ctx", split_axis=0, concat_axis=2, tiled=True)
    return (latents[None], conv_grad)


def solution(mesh):
    placed = (
        P("dp", "ctx", None, None, None, None),
        P(),
        P(),
        P(),
        P(),
        P(),
        P(),
        P("dp", "ctx", None, None, None),
    )
    return jax.shard_map(
        per_device,
        mesh=mesh,
        in_specs=placed,
        out_specs=(P("dp", "ctx", None, None, None), P("ctx", None)),
        check_vma=False,
    )
```

profile of v0, /device:TPU:0, one launch (start us, length us, event | category | flops | bytes accessed | tf_op | source)
XLA Modules:
  0.0 218.2 jit_solution(16532643515650054417)
XLA Ops:
  14.1 27.0 %all-gather.2.cloned.1.call-done = bf16[32,2,8,16,128]{4,3,2,1,0:T(8,128)(2,1)} async-done(((bf16[4,2,8,16,128]{4,3,2,1,0:T(8,128)(2,1)}), bf16[32,2,8,16,128]{4,3,2,1,0:T(8,128)(2,1)}) %all-gather.2.cloned.1.call-update) | async-done | bytes 2097168 | tf_op jit(solution)/shard_map/all_gather | solution.py:98
  41.1 2.2 %gather_fusion = bf16[4,2,8,16,128]{4,3,2,1,0:T(8,128)(2,1)S(1)} fusion(bf16[32,2,8,16,128]{4,3,2,1,0:T(8,128)(2,1)} %all-gather.2.cloned.1.call-done, s32[1024]{0:T(1024)S(1)} %pad_clamp_fusion), kind=kCustom, calls=%fused_computation | custom fusion | bytes 524304 | tf_op jit(solution)/shard_map/gather | solution.py:100
  43.4 2.0 fusion.30
  52.4 4.2 %convolution_convert_fusion.1 = bf16[2048,256]{1,0:T(8,128)(2,1)S(1)} fusion(bf16[2048,3456]{1,0:T(8,128)(2,1)S(1)} %bitcast.105, bf16[3456,256]{1,0:T(8,128)(2,1)S(1)} %copy-done), kind=kOutput, calls=%fused_computation.45 | convolution fusion | flops 3624402944 | bytes 16973824 | tf_op jit(solution)/shard_map/dot_general | solution.py:106
  59.2 3.6 %all-to-all-start = ((bf16[4,4,128,256]{3,1,0,2:T(4,128)(2,1)}), bf16[4,4,128,256]{3,1,0,2:T(4,128)(2,1)S(1)}, u32[]{:S(2)}, u32[]{:S(2)}) async-start(bf16[4,4,128,256]{3,1,0,2:T(4,128)(2,1)} %copy.64), calls=%async_computation | async-start | bytes 2097152 | tf_op jit(solution)/shard_map/all_to_all | solution.py:118
  63.0 10.9 %fusion.35 = f32[3456,256]{1,0:T(8,128)} fusion(bf16[2048,3456]{1,0:T(8,128)(2,1)} %bitcast.106, bf16[2048,256]{1,0:T(8,128)(2,1)} %bitcast.107), kind=kOutput, calls=%fused_computation.90 | convolution fusion | flops 3623878656 | bytes 18743296 | tf_op jit(solution)/shard_map/dot_general | solution.py:112
  74.0 4.1 %all-to-all-done = bf16[4,4,128,256]{3,1,0,2:T(4,128)(2,1)S(1)} async-done(((bf16[4,4,128,256]{3,1,0,2:T(4,128)(2,1)}), bf16[4,4,128,256]{3,1,0,2:T(4,128)(2,1)S(1)}, u32[]{:S(2)}, u32[]{:S(2)}) %all-to-all-start) | async-done | bytes 1048608 | tf_op jit(solution)/shard_map/all_to_all | solution.py:118
  79.9 81.9 %while.11 = (s32[]{:T(128)}, bf16[4,4,128,256]{3,2,1,0:T(8,128)(2,1)}, bf16[4,4,128,256]{3,2,1,0:T(8,128)(2,1)}, bf16[256,768]{1,0:T(8,128)(2,1)}, f32[4]{0:T(12...) while((s32[]{:T(128)}, ...), condition=%wide.region_10.11_spmd.clone, body=%wide.region_4.10_spmd.clone.sunk | while | flops 507300608 | bytes 18737292 | solution.py:143
  83.7 2.1 copy.77
  87.0 2.1 copy.78
  90.3 3.1 %fusion.71 = f32[4,4,128,128]{2,3,1,0:T(8,128)S(1)} fusion(f32[4]{0:T(128)S(1)} %get-tuple-element.185, f32[4,128,4,64]{1,3,2,0:T(8,128)} %bitcast.92, f32[4,128,4,64]{1,3,2,0:T(8,128)} %bitcast.93, pred[128,128]{0,1:T(8,128)(4,1)S(1)} %compare_and_fusion.3, f32[4,128,4]{1,2,0:T(4,128)S(1)} %get-tuple-element.161, ...), kind=kOutput, calls=%fused_computation.6.clone.1 | convolution fusion | flops 202113024 | bytes 2129936 | tf_op jit(solution)/shard_map/while/body/eval_jaxpr/gahd,gbhd->ghab/dot_general | solution.py:63
  96.5 2.4 %convolution_convert_fusion.3 = bf16[4,4,64,128]{3,2,1,0:T(8,128)(2,1)S(1)} fusion(bf16[4,128,4,64]{1,3,2,0:T(8,128)(2,1)S(1)} %bitcast.95, f32[4,4,128]{2,1,0:T(4,128)S(1)} %fusion.72, f32[4,4,128,128]{2,3,1,0:T(8,128)} %copy-done.1), kind=kOutput, calls=%fused_computation.8.clone.1 | convolution fusion | flops 34474112 | bytes 1581056 | tf_op jit(solution)/shard_map/while/body/eval_jaxpr/ghab,gbhd->gahd/dot_general | solution.py:71
  98.9 1.9 fusion.73
  104.5 2.1 copy.77
  107.7 2.1 copy.78
  111.0 3.1 %fusion.71 = f32[4,4,128,128]{2,3,1,0:T(8,128)S(1)} fusion(f32[4]{0:T(128)S(1)} %get-tuple-element.185, f32[4,128,4,64]{1,3,2,0:T(8,128)} %bitcast.92, f32[4,128,4,64]{1,3,2,0:T(8,128)} %bitcast.93, pred[128,128]{0,1:T(8,128)(4,1)S(1)} %compare_and_fusion.3, f32[4,128,4]{1,2,0:T(4,128)S(1)} %get-tuple-element.161, ...), kind=kOutput, calls=%fused_computation.6.clone.1 | convolution fusion | flops 202113024 | bytes 2129936 | tf_op jit(solution)/shard_map/while/body/eval_jaxpr/gahd,gbhd->ghab/dot_general | solution.py:63
  117.2 2.1 convolution_convert_fusion.3
  119.2 1.9 fusion.73
  124.9 2.1 copy.77
  128.0 2.0 copy.78
  131.3 3.1 %fusion.71 = f32[4,4,128,128]{2,3,1,0:T(8,128)S(1)} fusion(f32[4]{0:T(128)S(1)} %get-tuple-element.185, f32[4,128,4,64]{1,3,2,0:T(8,128)} %bitcast.92, f32[4,128,4,64]{1,3,2,0:T(8,128)} %bitcast.93, pred[128,128]{0,1:T(8,128)(4,1)S(1)} %compare_and_fusion.3, f32[4,128,4]{1,2,0:T(4,128)S(1)} %get-tuple-element.161, ...), kind=kOutput, calls=%fused_computation.6.clone.1 | convolution fusion | flops 202113024 | bytes 2129936 | tf_op jit(solution)/shard_map/while/body/eval_jaxpr/gahd,gbhd->ghab/dot_general | solution.py:63
  137.5 2.1 convolution_convert_fusion.3
  139.6 1.9 fusion.73
  145.2 2.1 copy.77
  148.4 2.0 copy.78
  151.6 3.1 %fusion.71 = f32[4,4,128,128]{2,3,1,0:T(8,128)S(1)} fusion(f32[4]{0:T(128)S(1)} %get-tuple-element.185, f32[4,128,4,64]{1,3,2,0:T(8,128)} %bitcast.92, f32[4,128,4,64]{1,3,2,0:T(8,128)} %bitcast.93, pred[128,128]{0,1:T(8,128)(4,1)S(1)} %compare_and_fusion.3, f32[4,128,4]{1,2,0:T(4,128)S(1)} %get-tuple-element.161, ...), kind=kOutput, calls=%fused_computation.6.clone.1 | convolution fusion | flops 202113024 | bytes 2129936 | tf_op jit(solution)/shard_map/while/body/eval_jaxpr/gahd,gbhd->ghab/dot_general | solution.py:63
  157.8 2.1 convolution_convert_fusion.3
  159.9 1.9 fusion.73
  161.8 2.8 %copy.68 = bf16[16,128,256]{2,0,1:T(8,128)(2,1)} copy(bf16[16,128,256]{2,1,0:T(8,128)(2,1)} %bitcast.102) | data formatting | bytes 2097152 | tf_op jit(solution)/shard_map/reshape | solution.py:154
  164.6 3.6 %all-to-all-start.1 = ((bf16[32,4,16,256]{3,2,1,0:T(8,128)(2,1)}), bf16[32,4,16,256]{3,2,1,0:T(8,128)(2,1)S(1)}, u32[]{:S(2)}, u32[]{:S(2)}) async-start(bf16[32,4,16,256]{3,2,1,0:T(8,128)(2,1)} %bitcast.97), calls=%async_computation.1 | async-start | bytes 2097152 | tf_op jit(solution)/shard_map/all_to_all | solution.py:156
  168.9 14.6 %all-to-all-done.1 = bf16[32,4,16,256]{3,2,1,0:T(8,128)(2,1)S(1)} async-done(((bf16[32,4,16,256]{3,2,1,0:T(8,128)(2,1)}), bf16[32,4,16,256]{3,2,1,0:T(8,128)(2,1)S(1)}, u32[]{:S(2)}, u32[]{:S(2)}) %all-to-all-start.1) | async-done | bytes 1048608 | tf_op jit(solution)/shard_map/all_to_all | solution.py:156
  184.6 25.2 %all-reduce.3.cloned.1.call-done = f32[432,256]{1,0:T(8,128)} async-done(((f32[432,256]{1,0:T(8,128)}), f32[432,256]{1,0:T(8,128)}) %all-reduce.3.cloned.1.call-update) | async-done | bytes 442384 | tf_op jit(solution)/shard_map/psum | solution.py:117
  (117 shorter events, 58.6 us)
Async XLA Ops:
  7.2 45.2 %copy-start = (bf16[3456,256]{1,0:T(8,128)(2,1)S(1)}, bf16[3456,256]{1,0:T(8,128)(2,1)}, u32[]{:S(2)}) copy-start(bf16[3456,256]{1,0:T(8,128)(2,1)} %param.14) | copy-start | bytes 5308420
  7.2 33.9 %all-gather.2.cloned.1.call-start = ((), (), s32[]{:S(2)}) async-start(), calls=%async_computation.3 | async-start | bytes 2359296 | tf_op jit(solution)/shard_map/all_gather | solution.py:98
  52.4 5.1 %copy-start.3 = (bf16[4,4,8,16,3456]{4,3,2,1,0:T(8,128)(2,1)}, bf16[4,4,8,16,3456]{4,3,2,1,0:T(8,128)(2,1)S(1)}, u32[]{:S(2)}) copy-start(bf16[4,4,8,16,3456]{4,3,2,1,0:T(8,128)(2,1)S(1)} %slice_dynamic-update-slice_fusion) | copy-start | bytes 42467332
  59.2 18.9 %all-to-all-start = ((bf16[4,4,128,256]{3,1,0,2:T(4,128)(2,1)}), bf16[4,4,128,256]{3,1,0,2:T(4,128)(2,1)S(1)}, u32[]{:S(2)}, u32[]{:S(2)}) async-start(bf16[4,4,128,256]{3,1,0,2:T(4,128)(2,1)} %copy.64), calls=%async_computation | async-start | bytes 2097152 | tf_op jit(solution)/shard_map/all_to_all | solution.py:118
  62.8 105.5 %reduce-scatter.2.cloned.1.call-start = ((), (), s32[]{:S(2)}) async-start(), calls=%async_computation.4 | async-start | bytes 3981312 | tf_op jit(solution)/shard_map/reduce_scatter | solution.py:111
  63.0 16.9 %copy-start.2 = (bf16[256,256]{1,0:T(8,128)(2,1)S(1)}, bf16[256,256]{1,0:T(8,128)(2,1)}, u32[]{:S(2)}) copy-start(bf16[256,256]{1,0:T(8,128)(2,1)} %param.16) | copy-start | bytes 393220
  63.0 16.9 %copy-start.4 = (f32[4]{0:T(128)S(1)}, f32[4]{0:T(128)}, u32[]{:S(2)}) copy-start(f32[4]{0:T(128)} %param.13) | copy-start | bytes 52
  93.4 1.0 copy-start.1
  114.0 1.0 copy-start.1
  134.4 1.0 copy-start.1
  154.7 1.0 copy-start.1
  164.6 18.9 %all-to-all-start.1 = ((bf16[32,4,16,256]{3,2,1,0:T(8,128)(2,1)}), bf16[32,4,16,256]{3,2,1,0:T(8,128)(2,1)S(1)}, u32[]{:S(2)}, u32[]{:S(2)}) async-start(bf16[32,4,16,256]{3,2,1,0:T(8,128)(2,1)} %bitcast.97), calls=%async_computation.1 | async-start | bytes 2097152 | tf_op jit(solution)/shard_map/all_to_all | solution.py:156
  168.2 41.7 %all-reduce.3.cloned.1.call-start = ((), (), s32[]{:S(2)}) async-start(), calls=%async_computation.5 | async-start | bytes 884736 | tf_op jit(solution)/shard_map/psum | solution.py:117
Sparse Core Ops, SparseCore 0:
  10.5 30.5 all-gather.1
  74.1 49.2 reduce-scatter.1
  171.4 38.4 all-reduce.2
where the time goes:
time: 220 us; the launch traced here: 218 us
  waiting for transfers between devices  71.7 us (33%)
  local copies, waits for them, and re-layouts  53.6 us (24%)
  matrix products  49.7 us (23%)
  other arithmetic  21.6 us (10%)
  between operations  14.1 us (6%)
  starting transfers between devices  7.41 us (3%)
    all_gather x1, waiting for transfers between devices, per_device(): shard_rows = lax.all_gather(tails, 'ctx', axis=0, tiled=True)  27 us
    psum x1, waiting for transfers between devices, per_device(): conv_grad = lax.psum(grad_share, 'dp')  25.2 us
    all_to_all x1, waiting for transfers between devices, per_device(): lax.all_to_all(blended_result, 'ctx', split_axis=0, concat_axis=2, tiled=...  14.6 us
    slice x8, local copies, waits for them, and re-layouts, timewise_softmax_mixing(): queries = projected[..., :channel_width].reshape(head_shape)  12.6 us
    dot_general x4, matrix products, timewise_softmax_mixing(): jnp.einsum('gahd,gbhd->ghab', queries, keys_all, precision=lax.Precision....  12.3 us
    dot_general x1, matrix products, per_device(): jnp.dot(patches.T, grad_rows, preferred_element_type=jnp.float32)  10.9 us
    unnamed x36, local copies, waits for them, and re-layouts  10.5 us
    dot_general x4, matrix products, timewise_softmax_mixing(): jnp.einsum('ghab,gbhd->gahd', probabilities, head_values, preferred_eleme...  8.58 us
  transfers between devices with their start and end apart: 5, of which 4 were waited for; matrix products, arithmetic and copies ran while one was open for 45% of the time, Pallas kernels for 0%

commit v1 on v0

v1 whole, which is shorter than its diff:
```python
import functools

import jax
import jax.numpy as jnp
from jax import lax
from jax.experimental import pallas as pl
from jax.experimental.pallas import tpu as pltpu
from jax.sharding import PartitionSpec as P

BF = jnp.bfloat16
F32 = jnp.float32
VMEM_LIMIT = 56 * 1024 * 1024
ROWS, COLS, CIN, COUT = 8, 16, 128, 256
SLOTS, STEPS = 4, 4
FRAMES = SLOTS * STEPS
TAPS = [(h, w) for h in range(3) for w in range(3)]
TAP_SETS = [TAPS[0:2], TAPS[2:4], TAPS[4:6], TAPS[6:8], TAPS[8:9]]


def iota(shape, axis):
    return lax.broadcasted_iota(jnp.int32, shape, axis)


def dot(a, b):
    return jnp.dot(a, b, preferred_element_type=F32)


def dot_t(a, b):
    return lax.dot_general(a, b, (((1,), (1,)), ((), ())), preferred_element_type=F32)


def swap_matrix(outer, inner):
    total = outer * inner
    i, j = iota((total, total), 0), iota((total, total), 1)
    return ((i % outer == j // inner) & (i // outer == j % inner)).astype(F32).astype(BF)


def params(**kw):
    return pltpu.CompilerParams(vmem_limit_bytes=VMEM_LIMIT, **kw)


def cost(flops, nbytes):
    return pl.CostEstimate(flops=flops, bytes_accessed=nbytes, transcendentals=0)


VMEM = pl.BlockSpec(memory_space=pltpu.VMEM)
SMEM = pl.BlockSpec(memory_space=pltpu.SMEM)


def fill_slots(assign, slot_of):
    def body(i, carry):
        slot_of[assign[i]] = i
        return carry

    lax.fori_loop(0, assign.shape[0], body, 0)


def is_opening(span, counts):
    start, found = jnp.int32(0), jnp.int32(0)
    for k in range(counts.shape[0]):
        found = jnp.where(span == start, jnp.int32(1), found)
        start = start + counts[k]
    return found


def lay_out_taps(x_ref, prev, padded):
    padded[...] = jnp.zeros_like(padded)
    swap = swap_matrix(FRAMES, COLS)

    def tile(s, f, r):
        return x_ref[s, f, r] if f >= 0 else prev(s, f, r)

    for r in range(0, ROWS, 2):
        for kt in range(3):
            cols = [
                jnp.concatenate([tile(s, 2 * t - 2 + kt, rr) for s in range(SLOTS) for t in range(STEPS)], axis=0)
                for rr in (r, r + 1)
            ]
            turned = dot(swap, jnp.concatenate(cols, axis=1)).astype(BF)
            for n in range(2):
                part = turned[:, n * CIN : (n + 1) * CIN].reshape(COLS, FRAMES, CIN)
                padded[r + n + 1, 1 : COLS + 1, :, kt * CIN : (kt + 1) * CIN] = part


def tap_block(padded, taps):
    blocks = [padded[h : h + ROWS, w : w + COLS].reshape(ROWS * COLS * FRAMES, 3 * CIN) for h, w in taps]
    return blocks[0] if len(blocks) == 1 else jnp.concatenate(blocks, axis=1)


def tap_rows(kt, h, w):
    at = ((kt * 3 + h) * 3 + w) * CIN
    return slice(at, at + CIN)


def conv_kernel(cells, x_ref, w_ref, out_ref, padded, edge):
    lay_out_taps(x_ref, lambda s, f, r: jnp.zeros((COLS, CIN), BF), padded)
    total = None
    for taps in TAP_SETS:
        rows = jnp.concatenate([w_ref[tap_rows(kt, h, w), :] for h, w in taps for kt in range(3)], axis=0)
        term = dot(tap_block(padded, taps), rows)
        total = term if total is None else total + term
    main = cells * FRAMES
    out_ref[:, :main, :] = total.astype(BF).reshape(out_ref.shape[0], main, COUT)
    wide = SLOTS * COLS
    i, j = iota((3 * wide, wide), 0), iota((3 * wide, wide), 1)
    k = i % wide
    q = (k // (SLOTS * cells)) * cells + k % cells
    s = (k // cells) % SLOTS
    shift = ((j // COLS == s) & (j % COLS == q + i // wide - 1)).astype(F32).astype(BF)
    edge[0] = jnp.zeros_like(edge[0])
    edge[ROWS + 1] = jnp.zeros_like(edge[0])
    for r in range(ROWS):
        tails = jnp.concatenate(
            [jnp.concatenate([x_ref[s, f, r] for s in range(SLOTS)], axis=0) for f in (6, 7)], axis=1
        )
        edge[r + 1] = dot(shift, tails).astype(BF)
    carry = None
    for h, w in TAPS:
        rows = jnp.concatenate([w_ref[tap_rows(kt, h, w), :] for kt in range(2)], axis=0)
        part = edge[h : h + ROWS, w * wide : (w + 1) * wide, :].reshape(ROWS * wide, 2 * CIN)
        term = dot(part, rows)
        carry = term if carry is None else carry + term
    out_ref[:, main:, :] = carry.astype(BF).reshape(out_ref.shape[0], SLOTS * cells, COUT)


def run_conv(frames, taps, ctx):
    cells = ROWS * COLS // ctx
    return pl.pallas_call(
        functools.partial(conv_kernel, cells),
        out_shape=jax.ShapeDtypeStruct((ctx, cells * (FRAMES + SLOTS), COUT), BF),
        in_specs=[VMEM, VMEM],
        out_specs=VMEM,
        scratch_shapes=[
            pltpu.VMEM((ROWS + 2, COLS + 2, FRAMES, 3 * CIN), BF),
            pltpu.VMEM((ROWS + 2, 3 * SLOTS * COLS, 2 * CIN), BF),
        ],
        compiler_params=params(),
        cost_estimate=cost(4_800_000_000, 4_000_000),
        name="conv_forward",
    )(frames, taps)


def tails_kernel(assign, me_ref, x_ref, out_ref, slot_of):
    fill_slots(assign, slot_of)
    me = me_ref[0]
    owners = []
    for p in range(SLOTS):
        after = assign[me * SLOTS + p] + 1
        known = after < assign.shape[0]
        owner = jnp.where(known, slot_of[jnp.where(known, after, 0)] // SLOTS, -1)
        place = jnp.int32(0)
        for earlier in owners:
            place = place + (earlier == owner).astype(jnp.int32)
        owners.append(owner)

        @pl.when(known)
        def _():
            out_ref[jnp.maximum(owner, 0), jnp.minimum(place, 1)] = x_ref[p]


def run_tails(frames, assign, me, ctx):
    shape = (SLOTS, 2, ROWS, COLS, CIN)
    return pl.pallas_call(
        tails_kernel,
        grid=(1,),
        out_shape=jax.ShapeDtypeStruct((ctx, 2) + shape[1:], BF),
        in_specs=[SMEM, SMEM, pl.BlockSpec(shape, lambda i: (0, 3, 0, 0, 0))],
        out_specs=pl.BlockSpec((ctx, 2) + shape[1:], lambda i: (0, 0, 0, 0, 0, 0)),
        scratch_shapes=[pltpu.SMEM(assign.shape, jnp.int32)],
        compiler_params=params(),
        cost_estimate=cost(0, 2_000_000),
        name="send_tails",
    )(assign, me, frames)


def grad_kernel(assign, counts, me_ref, x_ref, u_ref, tails_ref, keep_ref, send_ref, slot_of, padded, turned, whole):
    fill_slots(assign, slot_of)
    me = me_ref[0]
    found = []
    for i in range(SLOTS):
        span = assign[me * SLOTS + i]
        opening = is_opening(span, counts)
        slot = slot_of[jnp.maximum(span - 1, 0)]
        owner = slot // SLOTS
        place = jnp.int32(0)
        for p in range(SLOTS):
            after = assign[owner * SLOTS + p] + 1
            known = after < assign.shape[0]
            same = known & (slot_of[jnp.where(known, after, 0)] // SLOTS == me) & (p < slot % SLOTS)
            place = place + same.astype(jnp.int32)
        found.append((owner, jnp.minimum(place, 1), opening))

    def prev(s, f, r):
        owner, place, opening = found[s]
        got = tails_ref[owner, place, f + 2, r]
        return jnp.where(opening > 0, jnp.zeros_like(got), got)

    lay_out_taps(x_ref, prev, padded)
    swap = swap_matrix(FRAMES, COLS)
    span_rows = COLS * FRAMES
    for r in range(ROWS):
        block = jnp.concatenate(
            [u_ref[s, t, r * COLS : (r + 1) * COLS, :] for s in range(SLOTS) for t in range(STEPS)], axis=0
        )
        turned[:, r * span_rows : (r + 1) * span_rows] = dot(swap, block).T.astype(BF)
    for taps in TAP_SETS:
        product = dot(turned[...], tap_block(padded, taps)).T
        for n, (h, w) in enumerate(taps):
            for kt in range(3):
                at = (n * 3 + kt) * CIN
                whole[tap_rows(kt, h, w), :] = product[at : at + CIN, :]
    core = me % 2
    rows = keep_ref.shape[1]
    for i in range(keep_ref.shape[0]):
        keep_ref[i] = whole[pl.ds(pl.multiple_of((2 * i + core) * rows, 16), rows), :]
        send_ref[i] = whole[pl.ds(pl.multiple_of((2 * i + 1 - core) * rows, 16), rows), :].astype(BF)


def run_grad(assign, counts, me, frames, upstream, tails, ctx):
    patch = 27 * CIN
    half = (ctx // 2, patch // ctx, COUT)
    return pl.pallas_call(
        grad_kernel,
        out_shape=(jax.ShapeDtypeStruct(half, F32), jax.ShapeDtypeStruct(half, BF)),
        in_specs=[SMEM, SMEM, SMEM, VMEM, VMEM, VMEM],
        out_specs=(VMEM, VMEM),
        scratch_shapes=[
            pltpu.SMEM(assign.shape, jnp.int32),
            pltpu.VMEM((ROWS + 2, COLS + 2, FRAMES, 3 * CIN), BF),
            pltpu.VMEM((COUT, ROWS * COLS * FRAMES), BF),
            pltpu.VMEM((patch, COUT), F32),
        ],
        compiler_params=params(),
        cost_estimate=cost(4_000_000_000, 6_000_000),
        name="conv_gradient",
    )(assign, counts, me, frames, upstream, tails)


def attend_kernel(cells, assign, counts, scale, got_ref, qkv_ref, last_ref, out_ref, slot_of, rows_of, q_ref, k_ref, v_ref, bias):
    ctx = got_ref.shape[0]
    main = cells * FRAMES
    total = ctx * FRAMES
    fill_slots(assign, slot_of)

    def mark(shape, axis):
        spot = iota(shape, axis)
        span = jnp.zeros(shape, jnp.int32)
        for i in range(ctx * SLOTS):
            span = jnp.where(spot // STEPS == i, assign[i], span)
        clip, end = jnp.zeros(shape, jnp.int32), jnp.int32(0)
        for k in range(counts.shape[0]):
            end = end + counts[k]
            clip = clip + (span >= end).astype(jnp.int32)
        return span * STEPS + spot % STEPS, clip

    time_b, clip_b = mark((1, total), 1)
    time_a, clip_a = mark((total, 1), 0)
    allowed = (clip_a == clip_b) & (time_b <= time_a)
    bias[...] = jnp.where(allowed, 0.0, -1e30)

    i, j = iota((main, main), 0), iota((main, main), 1)
    held = j // (SLOTS * cells)
    fits = (i % STEPS == 0) & ((i // STEPS) % SLOTS == held) & (i // FRAMES == j % cells)
    base = jnp.where(fits, 1, 0)
    lane = iota((1, main), 1)
    from_slot = (lane // cells) % SLOTS
    lane_held = lane // (SLOTS * cells)
    same_head = (iota((COUT, COUT), 0) // 64 == iota((COUT, COUT), 1) // 64).astype(F32).astype(BF)
    head = iota((1, COUT), 1) // 64
    gain = jnp.zeros((1, COUT), F32)
    for h in range(COUT // 64):
        gain = jnp.where(head == h, scale[h], gain)

    def project(src, carry):
        pick = jnp.full((1, main), -1, jnp.int32)
        blocks = []
        for s in range(SLOTS):
            span = assign[src * SLOTS + s]
            slot = slot_of[jnp.maximum(span - 1, 0)]
            spot = jnp.where(is_opening(span, counts) > 0, -1, slot % SLOTS)
            pick = jnp.where(lane_held == s, spot, pick)
            blocks.append(got_ref[slot // SLOTS, main:, :])
        chosen = jnp.where(pick == from_slot, base, 0).astype(F32).astype(BF)
        value = got_ref[src, :main, :].astype(F32) + dot(chosen, jnp.concatenate(blocks, axis=0))
        value = value.astype(BF)
        rows_of[src] = value.reshape(cells, FRAMES, COUT)
        value = value.astype(F32)
        normed = value * lax.rsqrt(jnp.mean(value * value, axis=-1, keepdims=True) + 1e-6)
        mapped = dot(normed.astype(BF), qkv_ref[...])
        query, key = mapped[:, :COUT], mapped[:, COUT : 2 * COUT]
        query = query * (lax.rsqrt(dot((query * query).astype(BF), same_head) + 1e-6) * gain)
        key = key * lax.rsqrt(dot((key * key).astype(BF), same_head) + 1e-6)
        q_ref[src] = query.astype(BF).reshape(cells, FRAMES, COUT)
        k_ref[src] = key.astype(BF).reshape(cells, FRAMES, COUT)
        v_ref[src] = mapped[:, 2 * COUT :].astype(BF).reshape(cells, FRAMES, COUT)
        return carry

    lax.fori_loop(0, ctx, project, 0)

    low = iota((1, 128), 1) < 64
    ones = [jnp.where(low, 1.0, 0.0), jnp.where(low, 0.0, 1.0)]
    block = min(128, total)

    def mix(cell, carry):
        for pair in range(2):
            lanes = slice(pair * 128, (pair + 1) * 128)
            key = k_ref[:, cell, :, lanes].reshape(total, 128)
            value = v_ref[:, cell, :, lanes].reshape(total, 128)
            zero = jnp.zeros_like(key)
            keys = jnp.concatenate([jnp.where(low, key, zero), jnp.where(low, zero, key)], axis=0)
            sides = [jnp.where(low, value, zero), jnp.where(low, zero, value)]
            flags = [jnp.broadcast_to(ones[n].astype(BF), (total, 128)) for n in range(2)]
            values = jnp.concatenate(
                [jnp.concatenate([sides[n], flags[n]], axis=1) for n in range(2)], axis=0
            )
            for at in range(0, total, block):
                part = slice(at // FRAMES, (at + block) // FRAMES)
                query = q_ref[part, cell, :, lanes].reshape(block, 128)
                logits = dot_t(query, keys)
                mask = bias[at : at + block, :]
                weights = jnp.exp(logits + jnp.concatenate([mask, mask], axis=1)).astype(BF)
                sums = dot(weights, values)
                mixed = (sums[:, :128] / sums[:, 128:]).astype(BF)
                q_ref[part, cell, :, lanes] = mixed.reshape(block // FRAMES, FRAMES, 128)
        return carry

    lax.fori_loop(0, cells, mix, 0)

    turn = swap_matrix(cells, FRAMES)

    def finish(src, carry):
        mixed = q_ref[src].reshape(main, COUT)
        value = rows_of[src].reshape(main, COUT).astype(F32)
        latent = (value + dot(mixed, last_ref[...])).astype(BF)
        out_ref[src] = dot(turn, latent).astype(BF)
        return carry

    lax.fori_loop(0, ctx, finish, 0)


def run_attend(assign, counts, scale, got, qkv, last, ctx):
    cells = ROWS * COLS // ctx
    total = ctx * FRAMES
    held = pltpu.VMEM((ctx, cells, FRAMES, COUT), BF)
    return pl.pallas_call(
        functools.partial(attend_kernel, cells),
        out_shape=jax.ShapeDtypeStruct((ctx, cells * FRAMES, COUT), BF),
        in_specs=[SMEM, SMEM, SMEM, VMEM, VMEM, VMEM],
        out_specs=VMEM,
        scratch_shapes=[pltpu.SMEM(assign.shape, jnp.int32), held, held, held, held, pltpu.VMEM((total, total), F32)],
        compiler_params=params(),
        cost_estimate=cost(3_000_000_000, 4_000_000),
        name="attend",
    )(assign, counts, scale, got, qkv, last)


def fold_kernel(me_ref, keep_ref, got_ref, own_ref, *send_refs):
    mine = me_ref[0] // 2
    own_ref[...] = keep_ref[mine] + got_ref[mine].astype(F32)
    for k, ref in enumerate(send_refs):
        other = mine ^ (k + 1)
        ref[...] = (keep_ref[other] + got_ref[other].astype(F32)).astype(BF)


def run_fold(me, keep, got, ctx):
    piece = keep.shape[1:]
    peers = ctx // 2 - 1
    return pl.pallas_call(
        fold_kernel,
        out_shape=(jax.ShapeDtypeStruct(piece, F32),) + (jax.ShapeDtypeStruct(piece, BF),) * peers,
        in_specs=[SMEM, VMEM, VMEM],
        out_specs=(VMEM,) * (peers + 1),
        compiler_params=params(),
        cost_estimate=cost(0, 4_000_000),
        name="fold_cores",
    )(me, keep, got)


def add_kernel(own_ref, *refs):
    total = own_ref[...].astype(F32)
    for ref in refs[:-1]:
        total = total + ref[...].astype(F32)
    refs[-1][...] = total.astype(refs[-1].dtype)


def run_add(own, others, dtype):
    return pl.pallas_call(
        add_kernel,
        out_shape=jax.ShapeDtypeStruct(own.shape, dtype),
        in_specs=[VMEM] * (1 + len(others)),
        out_specs=VMEM,
        compiler_params=params(),
        cost_estimate=cost(0, 1_000_000),
        name="add_parts",
    )(own, *others)


def flip(value, axis, size, bits):
    return lax.ppermute(value, axis, [(i, i ^ bits) for i in range(size)])


def per_device(ctx, dp, frames, assign, counts, scale, taps, qkv, last, upstream):
    me = lax.axis_index("ctx").astype(jnp.int32).reshape(1)
    frames, upstream = frames[0], upstream[0]
    cells = ROWS * COLS // ctx
    tails = lax.all_to_all(run_tails(frames, assign, me, ctx), "ctx", 0, 0, tiled=True)
    sent = run_conv(frames, taps, ctx)
    got = lax.all_to_all(sent, "ctx", 0, 0, tiled=True)

    keep, send = run_grad(assign, counts, me, frames, upstream, tails, ctx)
    own, *parts = run_fold(me, keep, flip(send, "ctx", ctx, 1), ctx)
    share = run_add(own, [flip(part, "ctx", ctx, 2 * (k + 1)) for k, part in enumerate(parts)], BF)
    bits = 1
    while bits < dp:
        share = run_add(share, [flip(share, "dp", dp, bits)], BF if bits * 2 < dp else F32)
        bits *= 2

    blended = run_attend(assign, counts, scale, got, qkv, last, ctx)
    back = lax.all_to_all(blended, "ctx", 0, 0, tiled=True)
    latents = back.reshape(ctx, SLOTS, STEPS, cells, COUT).transpose(1, 2, 0, 3, 4)
    return (latents.reshape(1, SLOTS, STEPS, ctx * cells, COUT), share)


def solution(mesh):
    placed = (
        P("dp", "ctx", None, None, None, None),
        P(),
        P(),
        P(),
        P(),
        P(),
        P(),
        P("dp", "ctx", None, None, None),
    )
    return jax.shard_map(
        functools.partial(per_device, mesh.shape["ctx"], mesh.shape["dp"]),
        mesh=mesh,
        in_specs=placed,
        out_specs=(P("dp", "ctx", None, None, None), P("ctx", None)),
        check_vma=False,
    )
```

time: 220 us -> 119 us (0.54)
  matrix products: 49.7 us -> 0 us
  local copies, waits for them, and re-layouts: 53.6 us -> 5.12 us
  Pallas kernels: 0 us -> 45 us
  waiting for transfers between devices: 71.7 us -> 47.1 us
  other arithmetic: 21.6 us -> 0 us
  between operations: 14.1 us -> 0.69 us
  starting transfers between devices: 7.41 us -> 20.4 us
    dot_general x18 -> x0, matrix products: 49.7 us -> none  [the longest x4 12.3 us: timewise_softmax_mixing(): jnp.einsum('gahd,gbhd->ghab', queries, keys_all, precision=lax.Precision....]
    pallas_call x0 -> x8, Pallas kernels: none -> 45 us  [the longest x1 16.6 us: run_attend(): pl.pallas_call(functools.partial(attend_kernel, cells), out_shape=jax.Sha...]
    ppermute x0 -> x6, waiting for transfers between devices: none -> 31.5 us  [flip(): return lax.ppermute(value, axis, [(i, i ^ bits) for i in range(size)])]
    slice x21 -> x0, local copies, waits for them, and re-layouts: 30 us -> none  [the longest x8 12.6 us: timewise_softmax_mixing(): queries = projected[..., :channel_width].reshape(head_shape)]
    all_gather x1 -> x0, waiting for transfers between devices: 27 us -> none  [per_device(): shard_rows = lax.all_gather(tails, 'ctx', axis=0, tiled=True)]
    psum x1 -> x0, waiting for transfers between devices: 25.2 us -> none  [per_device(): conv_grad = lax.psum(grad_share, 'dp')]
    reduce_sum x14 -> x0, other arithmetic: 14.9 us -> none  [the longest x4 4.46 us: timewise_softmax_mixing(): jnp.mean(values32 * values32, axis=-1, keepdims=True) + 1e-06]
    ppermute x0 -> x6, starting transfers between devices: none -> 7.87 us  [flip(): return lax.ppermute(value, axis, [(i, i ^ bits) for i in range(size)])]
  transfers between devices with their start and end apart: 5 -> 9, of which waited for: 4 -> 6; matrix products, arithmetic and copies ran while one was open for 45% -> 1% of each run, Pallas kernels for 0% -> 35%
where the time goes in v1:
time: 119 us; the launch traced here: 118 us
  waiting for transfers between devices  47.1 us (40%)
  Pallas kernels  45 us (38%)
  starting transfers between devices  20.4 us (17%)
  local copies, waits for them, and re-layouts  5.12 us (4%)
    ppermute x6, waiting for transfers between devices, flip(): return lax.ppermute(value, axis, [(i, i ^ bits) for i in range(size)])  31.5 us
    pallas_call x1, Pallas kernels, run_attend(): pl.pallas_call(functools.partial(attend_kernel, cells), out_shape=jax.Sha...  16.6 us
    pallas_call x1, Pallas kernels, run_grad(): pl.pallas_call(grad_kernel, out_shape=(jax.ShapeDtypeStruct(half, F32), j...  9.33 us
    all_to_all x1, waiting for transfers between devices, per_device(): got = lax.all_to_all(sent, 'ctx', 0, 0, tiled=True)  8.41 us
    pallas_call x1, Pallas kernels, run_conv(): pl.pallas_call(functools.partial(conv_kernel, cells), out_shape=jax.Shape...  8.22 us
    ppermute x6, starting transfers between devices, flip(): return lax.ppermute(value, axis, [(i, i ^ bits) for i in range(size)])  7.87 us
    all_to_all x1, waiting for transfers between devices, per_device(): lax.all_to_all(run_tails(frames, assign, me, ctx), 'ctx', 0, 0, tiled=True)  7.19 us
    pallas_call x3, Pallas kernels, run_add(): pl.pallas_call(add_kernel, out_shape=jax.ShapeDtypeStruct(own.shape, dtyp...  5.67 us
  transfers between devices with their start and end apart: 9, of which 6 were waited for; matrix products, arithmetic and copies ran while one was open for 1% of the time, Pallas kernels for 35%

profile of v1, /device:TPU:0, one launch (start us, length us, event | category | flops | bytes accessed | tf_op | source)
XLA Modules:
  0.0 118.2 jit_solution(18155331628964680391)
XLA Ops:
  0.6 2.3 %send_tails.1 = bf16[8,2,2,8,16,128]{5,4,3,2,1,0:T(8,128)(2,1)} custom-call(s32[32]{0:T(128)} %assign.5, s32[1]{0:T(128)} %bitcast.4.me_ref, bf16[4,8,8,16,128]{4,3,2,1,0:T(8,128)(2,1)} %bitcast.9), custom_call_target="tpu_custom_call" | custom-call | bytes 2000000 | tf_op jit(solution)/shard_map/send_tails/pallas_call | solution.py:163
  3.0 5.2 %all-to-all-start.2 = ((bf16[8,2,2,8,16,128]{5,4,3,2,1,0:T(8,128)(2,1)}), bf16[8,2,2,8,16,128]{5,4,3,2,1,0:T(8,128)(2,1)S(1)}, u32[]{:S(2)}, u32[]{:S(2)}) async-start(bf16[8,2,2,8,16,128]{5,4,3,2,1,0:T(8,128)(2,1)} %send_tails.1), calls=%async_computation.2 | async-start | bytes 2097152 | tf_op jit(solution)/shard_map/all_to_all | solution.py:406
  8.1 8.2 %conv_forward.1 = bf16[8,320,256]{2,1,0:T(8,128)(2,1)} custom-call(bf16[4,8,8,16,128]{4,3,2,1,0:T(8,128)(2,1)} %bitcast.10, bf16[3456,256]{1,0:T(8,128)(2,1)} %w_ref.1), custom_call_target="tpu_custom_call" | custom-call | flops 4800000000 | bytes 4000000 | tf_op jit(solution)/shard_map/conv_forward/pallas_call | solution.py:128
  16.4 7.2 %all-to-all-done.2.tails_ref = bf16[8,2,2,8,16,128]{5,4,3,2,1,0:T(8,128)(2,1)S(1)} async-done(((bf16[8,2,2,8,16,128]{5,4,3,2,1,0:T(8,128)(2,1)}), bf16[8,2,2,8,16,128]{5,4,3,2,1,0:T(8,128)(2,1)S(1)}, u32[]{:S(2)}, u32[]{:S(2)}) %all-to-all-start.2) | async-done | bytes 1048608 | tf_op jit(solution)/shard_map/all_to_all | solution.py:406
  23.6 3.8 %all-to-all-start = ((bf16[8,320,256]{2,1,0:T(8,128)(2,1)}), bf16[8,320,256]{2,1,0:T(8,128)(2,1)S(1)}, u32[]{:S(2)}, u32[]{:S(2)}) async-start(bf16[8,320,256]{2,1,0:T(8,128)(2,1)} %conv_forward.1), calls=%async_computation | async-start | bytes 2621440 | tf_op jit(solution)/shard_map/all_to_all | solution.py:408
  27.3 9.3 %conv_gradient.1 = (f32[4,432,256]{2,1,0:T(8,128)}, bf16[4,432,256]{2,1,0:T(8,128)(2,1)}) custom-call(s32[32]{0:T(128)} %assign.5, s32[4]{0:T(128)} %counts.3, s32[1]{0:T(128)} %bitcast.4.me_ref, bf16[4,8,8,16,128]{4,3,2,1,0:T(8,128)(2,1)} %bitcast.11, bf16[4,4,128,256]{3,2,1,0:T(8,128)(2,1)} %bitcast.12, bf16[8,2,2,8,16,128]{5,4,3,2,1,0:T(8,128)(2,1)} %copy-done.1), custom_call_target="tpu_custom_call" | custom-call | flops 4000000000 | bytes 6000000 | tf_op jit(solution)/shard_map/conv_gradient/pallas_call | solution.py:222
  36.7 0.2 collective-permute-start
  36.9 8.4 %all-to-all-done.got_ref = bf16[8,320,256]{2,1,0:T(8,128)(2,1)S(1)} async-done(((bf16[8,320,256]{2,1,0:T(8,128)(2,1)}), bf16[8,320,256]{2,1,0:T(8,128)(2,1)S(1)}, u32[]{:S(2)}, u32[]{:S(2)}) %all-to-all-start) | async-done | bytes 1310752 | tf_op jit(solution)/shard_map/all_to_all | solution.py:408
  45.3 1.1 copy-done
  46.3 16.6 %attend.1 = bf16[8,256,256]{2,1,0:T(8,128)(2,1)} custom-call(s32[32]{0:T(128)} %assign.5, s32[4]{0:T(128)} %counts.3, f32[4]{0:T(128)} %scale.1, bf16[8,320,256]{2,1,0:T(8,128)(2,1)} %copy-done, bf16[256,768]{1,0:T(8,128)(2,1)} %qkv_ref.1, bf16[256,256]{1,0:T(8,128)(2,1)} %last_ref.1), custom_call_target="tpu_custom_call" | custom-call | flops 3000000000 | bytes 4000000 | tf_op jit(solution)/shard_map/attend/pallas_call | solution.py:345
  62.9 3.6 %all-to-all-start.1 = ((bf16[8,256,256]{2,1,0:T(8,128)(2,1)}), bf16[8,256,256]{2,1,0:T(8,128)(2,1)S(1)}, u32[]{:S(2)}, u32[]{:S(2)}) async-start(bf16[8,256,256]{2,1,0:T(8,128)(2,1)} %attend.1), calls=%async_computation.1 | async-start | bytes 2097152 | tf_op jit(solution)/shard_map/all_to_all | solution.py:419
  66.5 0.0 collective-permute-done.got_ref
  66.5 0.9 copy-done.2
  67.4 2.8 %fold_cores.1 = (f32[432,256]{1,0:T(8,128)}, bf16[432,256]{1,0:T(8,128)(2,1)}, bf16[432,256]{1,0:T(8,128)(2,1)}, bf16[432,256]{1,0:T(8,128)(2,1)}) custom-call(s32[1]{0:T(128)} %bitcast.4.me_ref, f32[4,432,256]{2,1,0:T(8,128)} %get-tuple-element.8.keep_ref, bf16[4,432,256]{2,1,0:T(8,128)(2,1)} %copy-done.2), custom_call_target="tpu_custom_call" | custom-call | bytes 4000000 | tf_op jit(solution)/shard_map/fold_cores/pallas_call | solution.py:368
  70.2 1.9 %collective-permute-start.1 = (bf16[432,256]{1,0:T(8,128)(2,1)}, bf16[432,256]{1,0:T(8,128)(2,1)S(1)}, u32[]{:S(2)}, u32[]{:S(2)}) collective-permute-start(bf16[432,256]{1,0:T(8,128)(2,1)} %get-tuple-element.11), channel_id=1, source_target_pairs={{0,2},{1,3},{2,0},{3,1},{4,6},{5,7},{6,4},{7,5},{8,10},{9,11},{10,... | collective-permute-start | bytes 663560 | tf_op jit(solution)/shard_map/ppermute | solution.py:399
  72.2 1.5 %collective-permute-start.2 = (bf16[432,256]{1,0:T(8,128)(2,1)}, bf16[432,256]{1,0:T(8,128)(2,1)S(1)}, u32[]{:S(2)}, u32[]{:S(2)}) collective-permute-start(bf16[432,256]{1,0:T(8,128)(2,1)} %get-tuple-element.12), channel_id=1, source_target_pairs={{0,4},{1,5},{2,6},{3,7},{4,0},{5,1},{6,2},{7,3},{8,12},{9,13},{10,... | collective-permute-start | bytes 663560 | tf_op jit(solution)/shard_map/ppermute | solution.py:399
  73.7 0.1 collective-permute-start.3
  73.7 12.4 %collective-permute-done.1.refs_0_ = bf16[432,256]{1,0:T(8,128)(2,1)S(1)} collective-permute-done((bf16[432,256]{1,0:T(8,128)(2,1)}, bf16[432,256]{1,0:T(8,128)(2,1)S(1)}, u32[]{:S(2)}, u32[]{:S(2)}) %collective-permute-start.1) | collective-permute-done | bytes 221216 | tf_op jit(solution)/shard_map/ppermute | solution.py:399
  86.2 0.0 collective-permute-done.2.refs_1_
  86.2 5.2 %collective-permute-done.3.refs_2_ = bf16[432,256]{1,0:T(8,128)(2,1)S(1)} collective-permute-done((bf16[432,256]{1,0:T(8,128)(2,1)}, bf16[432,256]{1,0:T(8,128)(2,1)S(1)}, u32[]{:S(2)}, u32[]{:S(2)}) %collective-permute-start.3) | collective-permute-done | bytes 221216 | tf_op jit(solution)/shard_map/ppermute | solution.py:399
  91.4 0.7 copy-done.7
  92.1 2.0 %add_parts.3.own_ref = bf16[432,256]{1,0:T(8,128)(2,1)} custom-call(f32[432,256]{1,0:T(8,128)} %get-tuple-element.10.own_ref, bf16[432,256]{1,0:T(8,128)(2,1)} %copy-done.5, bf16[432,256]{1,0:T(8,128)(2,1)} %copy-done.6, bf16[432,256]{1,0:T(8,128)(2,1)} %copy-done.7), custom_call_target="tpu_custom_call" | custom-call | bytes 1000000 | tf_op jit(solution)/shard_map/add_parts/pallas_call | solution.py:387
  94.1 1.6 %collective-permute-start.4 = (bf16[432,256]{1,0:T(8,128)(2,1)}, bf16[432,256]{1,0:T(8,128)(2,1)S(1)}, u32[]{:S(2)}, u32[]{:S(2)}) collective-permute-start(bf16[432,256]{1,0:T(8,128)(2,1)} %add_parts.3.own_ref), channel_id=1, source_target_pairs={{0,8},{8,0},{16,24},{24,16},{1,9},{9,1},{17,25},{25,17},{2,10},{10... | collective-permute-start | bytes 663560 | tf_op jit(solution)/shard_map/ppermute | solution.py:399
  95.7 5.6 %collective-permute-done.4.refs_0_ = bf16[432,256]{1,0:T(8,128)(2,1)S(1)} collective-permute-done((bf16[432,256]{1,0:T(8,128)(2,1)}, bf16[432,256]{1,0:T(8,128)(2,1)S(1)}, u32[]{:S(2)}, u32[]{:S(2)}) %collective-permute-start.4) | collective-permute-done | bytes 221216 | tf_op jit(solution)/shard_map/ppermute | solution.py:399
  101.3 0.7 copy-done.4
  102.0 1.8 %add_parts.4.own_ref = bf16[432,256]{1,0:T(8,128)(2,1)} custom-call(bf16[432,256]{1,0:T(8,128)(2,1)} %add_parts.3.own_ref, bf16[432,256]{1,0:T(8,128)(2,1)} %copy-done.4), custom_call_target="tpu_custom_call" | custom-call | bytes 1000000 | tf_op jit(solution)/shard_map/add_parts/pallas_call | solution.py:387
  103.8 2.6 %collective-permute-start.5 = (bf16[432,256]{1,0:T(8,128)(2,1)}, bf16[432,256]{1,0:T(8,128)(2,1)S(1)}, u32[]{:S(2)}, u32[]{:S(2)}) collective-permute-start(bf16[432,256]{1,0:T(8,128)(2,1)} %add_parts.4.own_ref), channel_id=1, source_target_pairs={{0,16},{8,24},{16,0},{24,8},{1,17},{9,25},{17,1},{25,9},{2,18},{10... | collective-permute-start | bytes 663560 | tf_op jit(solution)/shard_map/ppermute | solution.py:399
  106.3 0.0 all-to-all-done.1
  106.4 1.1 copy.10
  107.4 8.2 %collective-permute-done.5.refs_0_ = bf16[432,256]{1,0:T(8,128)(2,1)S(1)} collective-permute-done((bf16[432,256]{1,0:T(8,128)(2,1)}, bf16[432,256]{1,0:T(8,128)(2,1)S(1)}, u32[]{:S(2)}, u32[]{:S(2)}) %collective-permute-start.5) | collective-permute-done | bytes 221216 | tf_op jit(solution)/shard_map/ppermute | solution.py:399
  115.7 0.7 copy-done.3
  116.4 1.8 %add_parts.5 = f32[432,256]{1,0:T(8,128)} custom-call(bf16[432,256]{1,0:T(8,128)(2,1)} %add_parts.4.own_ref, bf16[432,256]{1,0:T(8,128)(2,1)} %copy-done.3), custom_call_target="tpu_custom_call" | custom-call | bytes 1000000 | tf_op jit(solution)/shard_map/add_parts/pallas_call | solution.py:387
  (11 shorter events, 0.0 us)
Async XLA Ops:
  3.0 20.6 %all-to-all-start.2 = ((bf16[8,2,2,8,16,128]{5,4,3,2,1,0:T(8,128)(2,1)}), bf16[8,2,2,8,16,128]{5,4,3,2,1,0:T(8,128)(2,1)S(1)}, u32[]{:S(2)}, u32[]{:S(2)}) async-start(bf16[8,2,2,8,16,128]{5,4,3,2,1,0:T(8,128)(2,1)} %send_tails.1), calls=%async_computation.2 | async-start | bytes 2097152 | tf_op jit(solution)/shard_map/all_to_all | solution.py:406
  23.6 3.8 %copy-start.1 = (bf16[8,2,2,8,16,128]{5,4,3,2,1,0:T(8,128)(2,1)}, bf16[8,2,2,8,16,128]{5,4,3,2,1,0:T(8,128)(2,1)S(1)}, u32[]{:S(2)}) copy-start(bf16[8,2,2,8,16,128]{5,4,3,2,1,0:T(8,128)(2,1)S(1)} %all-to-all-done.2.tails_ref) | copy-start | bytes 3145732
  23.6 21.7 %all-to-all-start = ((bf16[8,320,256]{2,1,0:T(8,128)(2,1)}), bf16[8,320,256]{2,1,0:T(8,128)(2,1)S(1)}, u32[]{:S(2)}, u32[]{:S(2)}) async-start(bf16[8,320,256]{2,1,0:T(8,128)(2,1)} %conv_forward.1), calls=%async_computation | async-start | bytes 2621440 | tf_op jit(solution)/shard_map/all_to_all | solution.py:408
  36.7 29.8 %collective-permute-start = (bf16[4,432,256]{2,1,0:T(8,128)(2,1)}, bf16[4,432,256]{2,1,0:T(8,128)(2,1)S(1)}, u32[]{:S(2)}, u32[]{:S(2)}) collective-permute-start(bf16[4,432,256]{2,1,0:T(8,128)(2,1)} %get-tuple-element.9), channel_id=1, source_target_pairs={{0,1},{1,0},{2,3},{3,2},{4,5},{5,4},{6,7},{7,6},{8,9},{9,8},{10,11... | collective-permute-start | bytes 2654216 | tf_op jit(solution)/shard_map/ppermute | solution.py:399
  45.3 1.1 copy-start
  62.9 43.4 %all-to-all-start.1 = ((bf16[8,256,256]{2,1,0:T(8,128)(2,1)}), bf16[8,256,256]{2,1,0:T(8,128)(2,1)S(1)}, u32[]{:S(2)}, u32[]{:S(2)}) async-start(bf16[8,256,256]{2,1,0:T(8,128)(2,1)} %attend.1), calls=%async_computation.1 | async-start | bytes 2097152 | tf_op jit(solution)/shard_map/all_to_all | solution.py:419
  66.5 0.9 copy-start.2
  70.2 15.9 %collective-permute-start.1 = (bf16[432,256]{1,0:T(8,128)(2,1)}, bf16[432,256]{1,0:T(8,128)(2,1)S(1)}, u32[]{:S(2)}, u32[]{:S(2)}) collective-permute-start(bf16[432,256]{1,0:T(8,128)(2,1)} %get-tuple-element.11), channel_id=1, source_target_pairs={{0,2},{1,3},{2,0},{3,1},{4,6},{5,7},{6,4},{7,5},{8,10},{9,11},{10,... | collective-permute-start | bytes 663560 | tf_op jit(solution)/shard_map/ppermute | solution.py:399
  72.2 14.0 %collective-permute-start.2 = (bf16[432,256]{1,0:T(8,128)(2,1)}, bf16[432,256]{1,0:T(8,128)(2,1)S(1)}, u32[]{:S(2)}, u32[]{:S(2)}) collective-permute-start(bf16[432,256]{1,0:T(8,128)(2,1)} %get-tuple-element.12), channel_id=1, source_target_pairs={{0,4},{1,5},{2,6},{3,7},{4,0},{5,1},{6,2},{7,3},{8,12},{9,13},{10,... | collective-permute-start | bytes 663560 | tf_op jit(solution)/shard_map/ppermute | solution.py:399
  73.7 17.7 %collective-permute-start.3 = (bf16[432,256]{1,0:T(8,128)(2,1)}, bf16[432,256]{1,0:T(8,128)(2,1)S(1)}, u32[]{:S(2)}, u32[]{:S(2)}) collective-permute-start(bf16[432,256]{1,0:T(8,128)(2,1)} %get-tuple-element.13), channel_id=1, source_target_pairs={{0,6},{1,7},{2,4},{3,5},{4,2},{5,3},{6,0},{7,1},{8,14},{9,15},{10,... | collective-permute-start | bytes 663560 | tf_op jit(solution)/shard_map/ppermute | solution.py:399
  86.2 5.2 %copy-start.5 = (bf16[432,256]{1,0:T(8,128)(2,1)}, bf16[432,256]{1,0:T(8,128)(2,1)S(1)}, u32[]{:S(2)}) copy-start(bf16[432,256]{1,0:T(8,128)(2,1)S(1)} %collective-permute-done.1.refs_0_) | copy-start | bytes 663556
  86.2 5.2 %copy-start.6 = (bf16[432,256]{1,0:T(8,128)(2,1)}, bf16[432,256]{1,0:T(8,128)(2,1)S(1)}, u32[]{:S(2)}) copy-start(bf16[432,256]{1,0:T(8,128)(2,1)S(1)} %collective-permute-done.2.refs_1_) | copy-start | bytes 663556
  91.4 0.7 copy-start.7
  94.1 7.2 %collective-permute-start.4 = (bf16[432,256]{1,0:T(8,128)(2,1)}, bf16[432,256]{1,0:T(8,128)(2,1)S(1)}, u32[]{:S(2)}, u32[]{:S(2)}) collective-permute-start(bf16[432,256]{1,0:T(8,128)(2,1)} %add_parts.3.own_ref), channel_id=1, source_target_pairs={{0,8},{8,0},{16,24},{24,16},{1,9},{9,1},{17,25},{25,17},{2,10},{10... | collective-permute-start | bytes 663560 | tf_op jit(solution)/shard_map/ppermute | solution.py:399
  101.3 0.7 copy-start.4
  103.8 11.9 %collective-permute-start.5 = (bf16[432,256]{1,0:T(8,128)(2,1)}, bf16[432,256]{1,0:T(8,128)(2,1)S(1)}, u32[]{:S(2)}, u32[]{:S(2)}) collective-permute-start(bf16[432,256]{1,0:T(8,128)(2,1)} %add_parts.4.own_ref), channel_id=1, source_target_pairs={{0,16},{8,24},{16,0},{24,8},{1,17},{9,25},{17,1},{25,9},{2,18},{10... | collective-permute-start | bytes 663560 | tf_op jit(solution)/shard_map/ppermute | solution.py:399
  115.7 0.7 copy-start.3

commit v2 on v1

--- a/solution.py
+++ b/solution.py
@@ -45,6 +45,7 @@
 
 VMEM = pl.BlockSpec(memory_space=pltpu.VMEM)
 SMEM = pl.BlockSpec(memory_space=pltpu.SMEM)
+ANY = pl.BlockSpec(memory_space=pl.ANY)
 
 
 def fill_slots(assign, slot_of):
@@ -92,7 +93,12 @@
     return slice(at, at + CIN)
 
 
-def conv_kernel(cells, x_ref, w_ref, out_ref, padded, edge):
+def device_at(me, chip_bits, core_bit):
+    return me ^ (2 * chip_bits + core_bit)
+
+
+def conv_kernel(cells, me_ref, x_ref, w_ref, *refs):
+    out_refs, (main_part, edge_part, padded, edge) = refs[:-4], refs[-4:]
     lay_out_taps(x_ref, lambda s, f, r: jnp.zeros((COLS, CIN), BF), padded)
     total = None
     for taps in TAP_SETS:
@@ -100,7 +106,7 @@
         term = dot(tap_block(padded, taps), rows)
         total = term if total is None else total + term
     main = cells * FRAMES
-    out_ref[:, :main, :] = total.astype(BF).reshape(out_ref.shape[0], main, COUT)
+    main_part[...] = total.astype(BF).reshape(main_part.shape)
     wide = SLOTS * COLS
     i, j = iota((3 * wide, wide), 0), iota((3 * wide, wide), 1)
     k = i % wide
@@ -120,80 +126,76 @@
         part = edge[h : h + ROWS, w * wide : (w + 1) * wide, :].reshape(ROWS * wide, 2 * CIN)
         term = dot(part, rows)
         carry = term if carry is None else carry + term
-    out_ref[:, main:, :] = carry.astype(BF).reshape(out_ref.shape[0], SLOTS * cells, COUT)
-
-
-def run_conv(frames, taps, ctx):
+    edge_part[...] = carry.astype(BF).reshape(edge_part.shape)
+    me = me_ref[0]
+    for k, ref in enumerate(out_refs):
+        for c in range(2):
+            to = device_at(me, k, c)
+            ref[c, :main, :] = main_part[to]
+            ref[c, main:, :] = edge_part[to]
+
+
+def run_conv(me, frames, taps, ctx):
     cells = ROWS * COLS // ctx
     return pl.pallas_call(
         functools.partial(conv_kernel, cells),
-        out_shape=jax.ShapeDtypeStruct((ctx, cells * (FRAMES + SLOTS), COUT), BF),
-        in_specs=[VMEM, VMEM],
-        out_specs=VMEM,
+        out_shape=[jax.ShapeDtypeStruct((2, cells * (FRAMES + SLOTS), COUT), BF)] * (ctx // 2),
+        in_specs=[SMEM, VMEM, VMEM],
+        out_specs=[VMEM] * (ctx // 2),
         scratch_shapes=[
+            pltpu.VMEM((ctx, cells * FRAMES, COUT), BF),
+            pltpu.VMEM((ctx, cells * SLOTS, COUT), BF),
             pltpu.VMEM((ROWS + 2, COLS + 2, FRAMES, 3 * CIN), BF),
             pltpu.VMEM((ROWS + 2, 3 * SLOTS * COLS, 2 * CIN), BF),
         ],
         compiler_params=params(),
         cost_estimate=cost(4_800_000_000, 4_000_000),
         name="conv_forward",
-    )(frames, taps)
-
-
-def tails_kernel(assign, me_ref, x_ref, out_ref, slot_of):
+    )(me, frames, taps)
+
+
+def copy_kernel(x_ref, out_ref):
+    out_ref[...] = x_ref[...]
+
+
+def run_tails(frames):
+    shape = (SLOTS, 2, ROWS, COLS, CIN)
+    return pl.pallas_call(
+        copy_kernel,
+        grid=(1,),
+        out_shape=jax.ShapeDtypeStruct(shape, BF),
+        in_specs=[pl.BlockSpec(shape, lambda i: (0, 3, 0, 0, 0))],
+        out_specs=pl.BlockSpec(shape, lambda i: (0, 0, 0, 0, 0)),
+        compiler_params=params(),
+        cost_estimate=cost(0, 500_000),
+        name="cut_tails",
+    )(frames)
+
+
+def grad_kernel(chips, assign, counts, me_ref, x_ref, u_ref, unused_ref, *refs):
+    tails, refs = refs[: 2 * chips], refs[2 * chips :]
+    sends, keeps = refs[:chips], refs[chips : 2 * chips]
+    slot_of, padded, turned, whole, before, sem = refs[2 * chips :]
     fill_slots(assign, slot_of)
     me = me_ref[0]
-    owners = []
-    for p in range(SLOTS):
-        after = assign[me * SLOTS + p] + 1
-        known = after < assign.shape[0]
-        owner = jnp.where(known, slot_of[jnp.where(known, after, 0)] // SLOTS, -1)
-        place = jnp.int32(0)
-        for earlier in owners:
-            place = place + (earlier == owner).astype(jnp.int32)
-        owners.append(owner)
-
-        @pl.when(known)
-        def _():
-            out_ref[jnp.maximum(owner, 0), jnp.minimum(place, 1)] = x_ref[p]
-
-
-def run_tails(frames, assign, me, ctx):
-    shape = (SLOTS, 2, ROWS, COLS, CIN)
-    return pl.pallas_call(
-        tails_kernel,
-        grid=(1,),
-        out_shape=jax.ShapeDtypeStruct((ctx, 2) + shape[1:], BF),
-        in_specs=[SMEM, SMEM, pl.BlockSpec(shape, lambda i: (0, 3, 0, 0, 0))],
-        out_specs=pl.BlockSpec((ctx, 2) + shape[1:], lambda i: (0, 0, 0, 0, 0, 0)),
-        scratch_shapes=[pltpu.SMEM(assign.shape, jnp.int32)],
-        compiler_params=params(),
-        cost_estimate=cost(0, 2_000_000),
-        name="send_tails",
-    )(assign, me, frames)
-
-
-def grad_kernel(assign, counts, me_ref, x_ref, u_ref, tails_ref, keep_ref, send_ref, slot_of, padded, turned, whole):
-    fill_slots(assign, slot_of)
-    me = me_ref[0]
-    found = []
+    openings = []
     for i in range(SLOTS):
         span = assign[me * SLOTS + i]
-        opening = is_opening(span, counts)
+        openings.append(is_opening(span, counts))
         slot = slot_of[jnp.maximum(span - 1, 0)]
-        owner = slot // SLOTS
-        place = jnp.int32(0)
-        for p in range(SLOTS):
-            after = assign[owner * SLOTS + p] + 1
-            known = after < assign.shape[0]
-            same = known & (slot_of[jnp.where(known, after, 0)] // SLOTS == me) & (p < slot % SLOTS)
-            place = place + same.astype(jnp.int32)
-        found.append((owner, jnp.minimum(place, 1), opening))
+        apart = (slot // SLOTS) ^ me
+        for n, ref in enumerate(tails):
+
+            @pl.when(apart == n)
+            def _():
+                pltpu.make_async_copy(ref.at[slot % SLOTS], before.at[i], sem.at[i]).start()
+
+    for i in range(SLOTS):
+        pltpu.make_async_copy(tails[0].at[0], before.at[i], sem.at[i]).wait()
 
     def prev(s, f, r):
-        owner, place, opening = found[s]
-        got = tails_ref[owner, place, f + 2, r]
-        return jnp.where(opening > 0, jnp.zeros_like(got), got)
+        got = before[s, f + 2, r]
+        return jnp.where(openings[s] > 0, jnp.zeros_like(got), got)
 
     lay_out_taps(x_ref, prev, padded)
     swap = swap_matrix(FRAMES, COLS)
@@ -209,35 +211,40 @@
             for kt in range(3):
                 at = (n * 3 + kt) * CIN
                 whole[tap_rows(kt, h, w), :] = product[at : at + CIN, :]
-    core = me % 2
-    rows = keep_ref.shape[1]
-    for i in range(keep_ref.shape[0]):
-        keep_ref[i] = whole[pl.ds(pl.multiple_of((2 * i + core) * rows, 16), rows), :]
-        send_ref[i] = whole[pl.ds(pl.multiple_of((2 * i + 1 - core) * rows, 16), rows), :].astype(BF)
-
-
-def run_grad(assign, counts, me, frames, upstream, tails, ctx):
+    rows = keeps[0].shape[0]
+    for k in range(chips):
+        kept, sent = device_at(me, k, 0), device_at(me, k, 1)
+        keeps[k][...] = whole[pl.ds(pl.multiple_of(kept * rows, 16), rows), :]
+        sends[k][...] = whole[pl.ds(pl.multiple_of(sent * rows, 16), rows), :].astype(BF)
+
+
+def run_grad(assign, counts, me, frames, upstream, after, tails, ctx):
     patch = 27 * CIN
-    half = (ctx // 2, patch // ctx, COUT)
+    chips, rows = ctx // 2, patch // ctx
     return pl.pallas_call(
-        grad_kernel,
-        out_shape=(jax.ShapeDtypeStruct(half, F32), jax.ShapeDtypeStruct(half, BF)),
-        in_specs=[SMEM, SMEM, SMEM, VMEM, VMEM, VMEM],
-        out_specs=(VMEM, VMEM),
+        functools.partial(grad_kernel, chips),
+        out_shape=[jax.ShapeDtypeStruct((rows, COUT), dtype) for dtype in (BF, F32) for k in range(chips)],
+        in_specs=[SMEM, SMEM, SMEM, VMEM, VMEM, ANY] + [ANY] * ctx,
+        out_specs=[VMEM] * (2 * chips),
         scratch_shapes=[
             pltpu.SMEM(assign.shape, jnp.int32),
             pltpu.VMEM((ROWS + 2, COLS + 2, FRAMES, 3 * CIN), BF),
             pltpu.VMEM((COUT, ROWS * COLS * FRAMES), BF),
             pltpu.VMEM((patch, COUT), F32),
+            pltpu.VMEM((SLOTS, 2, ROWS, COLS, CIN), BF),
+            pltpu.SemaphoreType.DMA((SLOTS,)),
         ],
         compiler_params=params(),
         cost_estimate=cost(4_000_000_000, 6_000_000),
         name="conv_gradient",
-    )(assign, counts, me, frames, upstream, tails)
-
-
-def attend_kernel(cells, assign, counts, scale, got_ref, qkv_ref, last_ref, out_ref, slot_of, rows_of, q_ref, k_ref, v_ref, bias):
-    ctx = got_ref.shape[0]
+    )(assign, counts, me, frames, upstream, after, *tails)
+
+
+def attend_kernel(cells, ctx, assign, counts, scale, me_ref, qkv_ref, last_ref, *refs):
+    chips = ctx // 2
+    got_refs, out_refs = refs[:ctx], refs[ctx : ctx + chips]
+    slot_of, rows_of, q_ref, k_ref, v_ref, edges, bias = refs[ctx + chips :]
+    me = me_ref[0]
     main = cells * FRAMES
     total = ctx * FRAMES
     fill_slots(assign, slot_of)
@@ -246,7 +253,7 @@
         spot = iota(shape, axis)
         span = jnp.zeros(shape, jnp.int32)
         for i in range(ctx * SLOTS):
-            span = jnp.where(spot // STEPS == i, assign[i], span)
+            span = jnp.where(spot // STEPS == i, assign[(me ^ (i // SLOTS)) * SLOTS + i % SLOTS], span)
         clip, end = jnp.zeros(shape, jnp.int32), jnp.int32(0)
         for k in range(counts.shape[0]):
             end = end + counts[k]
@@ -271,17 +278,21 @@
     for h in range(COUT // 64):
         gain = jnp.where(head == h, scale[h], gain)
 
+    for src in range(ctx):
+        edges[src] = got_refs[src][0, main:, :]
+        rows_of[src] = got_refs[src][0, :main, :].reshape(cells, FRAMES, COUT)
+
     def project(src, carry):
         pick = jnp.full((1, main), -1, jnp.int32)
         blocks = []
         for s in range(SLOTS):
-            span = assign[src * SLOTS + s]
+            span = assign[(me ^ src) * SLOTS + s]
             slot = slot_of[jnp.maximum(span - 1, 0)]
             spot = jnp.where(is_opening(span, counts) > 0, -1, slot % SLOTS)
             pick = jnp.where(lane_held == s, spot, pick)
-            blocks.append(got_ref[slot // SLOTS, main:, :])
+            blocks.append(edges[(slot // SLOTS) ^ me])
         chosen = jnp.where(pick == from_slot, base, 0).astype(F32).astype(BF)
-        value = got_ref[src, :main, :].astype(F32) + dot(chosen, jnp.concatenate(blocks, axis=0))
+        value = rows_of[src].reshape(main, COUT).astype(F32) + dot(chosen, jnp.concatenate(blocks, axis=0))
         value = value.astype(BF)
         rows_of[src] = value.reshape(cells, FRAMES, COUT)
         value = value.astype(F32)
@@ -328,96 +339,109 @@
 
     turn = swap_matrix(cells, FRAMES)
 
-    def finish(src, carry):
+    for src in range(ctx):
         mixed = q_ref[src].reshape(main, COUT)
         value = rows_of[src].reshape(main, COUT).astype(F32)
         latent = (value + dot(mixed, last_ref[...])).astype(BF)
-        out_ref[src] = dot(turn, latent).astype(BF)
-        return carry
-
-    lax.fori_loop(0, ctx, finish, 0)
-
-
-def run_attend(assign, counts, scale, got, qkv, last, ctx):
+        out_refs[src // 2][src % 2] = dot(turn, latent).astype(BF)
+
+
+def run_attend(assign, counts, scale, me, got, qkv, last, ctx):
     cells = ROWS * COLS // ctx
     total = ctx * FRAMES
     held = pltpu.VMEM((ctx, cells, FRAMES, COUT), BF)
+    piece = (1, cells * (FRAMES + SLOTS), COUT)
+
+    def whole(array):
+        return pl.BlockSpec(array.shape, lambda i: (0,) * array.ndim)
+
+    def half(n):
+        return pl.BlockSpec(piece, lambda i: (n, 0, 0))
+
+    out = (2, cells * FRAMES, COUT)
     return pl.pallas_call(
-        functools.partial(attend_kernel, cells),
-        out_shape=jax.ShapeDtypeStruct((ctx, cells * FRAMES, COUT), BF),
-        in_specs=[SMEM, SMEM, SMEM, VMEM, VMEM, VMEM],
-        out_specs=VMEM,
-        scratch_shapes=[pltpu.SMEM(assign.shape, jnp.int32), held, held, held, held, pltpu.VMEM((total, total), F32)],
+        functools.partial(attend_kernel, cells, ctx),
+        grid=(1,),
+        out_shape=[jax.ShapeDtypeStruct(out, BF)] * (ctx // 2),
+        in_specs=[SMEM, SMEM, SMEM, SMEM, whole(qkv), whole(last)] + [half(n % 2) for n in range(ctx)],
+        out_specs=[pl.BlockSpec(out, lambda i: (0, 0, 0))] * (ctx // 2),
+        scratch_shapes=[
+            pltpu.SMEM(assign.shape, jnp.int32),
+            held,
+            held,
+            held,
+            held,
+            pltpu.VMEM((ctx, cells * SLOTS, COUT), BF),
+            pltpu.VMEM((total, total), F32),
+        ],
         compiler_params=params(),
         cost_estimate=cost(3_000_000_000, 4_000_000),
         name="attend",
-    )(assign, counts, scale, got, qkv, last)
-
-
-def fold_kernel(me_ref, keep_ref, got_ref, own_ref, *send_refs):
-    mine = me_ref[0] // 2
-    own_ref[...] = keep_ref[mine] + got_ref[mine].astype(F32)
-    for k, ref in enumerate(send_refs):
-        other = mine ^ (k + 1)
-        ref[...] = (keep_ref[other] + got_ref[other].astype(F32)).astype(BF)
-
-
-def run_fold(me, keep, got, ctx):
-    piece = keep.shape[1:]
-    peers = ctx // 2 - 1
+    )(assign, counts, scale, me, qkv, last, *got)
+
+
+def place_kernel(me_ref, *refs):
+    out_ref = refs[-1]
+    for n, ref in enumerate(refs[:-1]):
+        out_ref[:, me_ref[0] ^ n] = ref[0]
+
+
+def run_place(me, pieces, ctx):
+    cells = ROWS * COLS // ctx
+    pieces = [piece.reshape(2, FRAMES, cells, COUT) for piece in pieces]
+    shape = (FRAMES, ctx, cells, COUT)
+
+    def half(n):
+        return pl.BlockSpec((1,) + pieces[0].shape[1:], lambda i: (n, 0, 0, 0))
+
     return pl.pallas_call(
-        fold_kernel,
-        out_shape=(jax.ShapeDtypeStruct(piece, F32),) + (jax.ShapeDtypeStruct(piece, BF),) * peers,
-        in_specs=[SMEM, VMEM, VMEM],
-        out_specs=(VMEM,) * (peers + 1),
+        place_kernel,
+        grid=(1,),
+        out_shape=jax.ShapeDtypeStruct(shape, BF),
+        in_specs=[SMEM] + [half(n % 2) for n in range(ctx)],
+        out_specs=pl.BlockSpec(shape, lambda i: (0, 0, 0, 0)),
         compiler_params=params(),
-        cost_estimate=cost(0, 4_000_000),
-        name="fold_cores",
-    )(me, keep, got)
-
-
-def add_kernel(own_ref, *refs):
-    total = own_ref[...].astype(F32)
-    for ref in refs[:-1]:
-        total = total + ref[...].astype(F32)
-    refs[-1][...] = total.astype(refs[-1].dtype)
-
-
-def run_add(own, others, dtype):
-    return pl.pallas_call(
-        add_kernel,
-        out_shape=jax.ShapeDtypeStruct(own.shape, dtype),
-        in_specs=[VMEM] * (1 + len(others)),
-        out_specs=VMEM,
-        compiler_params=params(),
-        cost_estimate=cost(0, 1_000_000),
-        name="add_parts",
-    )(own, *others)
+        cost_estimate=cost(0, 2_000_000),
+        name="place_latents",
+    )(me, *pieces)
 
 
 def flip(value, axis, size, bits):
     return lax.ppermute(value, axis, [(i, i ^ bits) for i in range(size)])
+
+
+def exchange(parts, ctx, after=None):
+    far = [parts[0]] + [None] * (len(parts) - 1)
+    for k in reversed(range(1, len(parts))):
+        far[k] = flip(parts[k], "ctx", ctx, 2 * k)
+    if after is not None:
+        far = lax.optimization_barrier((far, after))[0]
+    near = [flip(part, "ctx", ctx, 1) for part in far]
+    return [piece for pair in zip(far, near) for piece in pair]
 
 
 def per_device(ctx, dp, frames, assign, counts, scale, taps, qkv, last, upstream):
     me = lax.axis_index("ctx").astype(jnp.int32).reshape(1)
     frames, upstream = frames[0], upstream[0]
     cells = ROWS * COLS // ctx
-    tails = lax.all_to_all(run_tails(frames, assign, me, ctx), "ctx", 0, 0, tiled=True)
-    sent = run_conv(frames, taps, ctx)
-    got = lax.all_to_all(sent, "ctx", 0, 0, tiled=True)
-
-    keep, send = run_grad(assign, counts, me, frames, upstream, tails, ctx)
-    own, *parts = run_fold(me, keep, flip(send, "ctx", ctx, 1), ctx)
-    share = run_add(own, [flip(part, "ctx", ctx, 2 * (k + 1)) for k, part in enumerate(parts)], BF)
+    chips = ctx // 2
+    sent = run_conv(me, frames, taps, ctx)
+    tails = exchange([run_tails(frames)] * chips, ctx, sent[0])
+    got = exchange(sent, ctx)
+
+    parts = run_grad(assign, counts, me, frames, upstream, sent[0], tails, ctx)
+    sums = [kept + flip(part, "ctx", ctx, 1).astype(F32) for part, kept in zip(parts[:chips], parts[chips:])]
+    share = sums[0]
+    for k in reversed(range(1, chips)):
+        share = share + flip(sums[k].astype(BF), "ctx", ctx, 2 * k).astype(F32)
     bits = 1
     while bits < dp:
-        share = run_add(share, [flip(share, "dp", dp, bits)], BF if bits * 2 < dp else F32)
+        share = share.astype(BF)
+        share = share.astype(F32) + flip(share, "dp", dp, bits).astype(F32)
         bits *= 2
 
-    blended = run_attend(assign, counts, scale, got, qkv, last, ctx)
-    back = lax.all_to_all(blended, "ctx", 0, 0, tiled=True)
-    latents = back.reshape(ctx, SLOTS, STEPS, cells, COUT).transpose(1, 2, 0, 3, 4)
+    blended = run_attend(assign, counts, scale, me, got, qkv, last, ctx)
+    latents = run_place(me, exchange(blended, ctx), ctx)
     return (latents.reshape(1, SLOTS, STEPS, ctx * cells, COUT), share)
 
 

time: 119 us -> 89.9 us (0.76)
  waiting for transfers between devices: 47.1 us -> 25.2 us
  Pallas kernels: 45 us -> 35.9 us
  other arithmetic: 0 us -> 3.21 us
  local copies, waits for them, and re-layouts: 5.12 us -> 2.41 us
  starting transfers between devices: 20.4 us -> 21.8 us
    all_to_all x3 -> x0, waiting for transfers between devices: 15.6 us -> none  [the longest x1 8.41 us: per_device(): got = lax.all_to_all(sent, 'ctx', 0, 0, tiled=True)]
    ppermute x6 -> x30, starting transfers between devices: 7.87 us -> 21.8 us  [flip(): return lax.ppermute(value, axis, [(i, i ^ bits) for i in range(size)])]
    all_to_all x3 -> x0, starting transfers between devices: 12.5 us -> none  [the longest x1 5.18 us: per_device(): lax.all_to_all(run_tails(frames, assign, me, ctx), 'ctx', 0, 0, tiled=True)]
    pallas_call x8 -> x5, Pallas kernels: 45 us -> 35.9 us  [the longest x1 14.1 us: run_attend(): pl.pallas_call(functools.partial(attend_kernel, cells, ctx), grid=(1,), o...]
    ppermute x6 -> x30, waiting for transfers between devices: 31.5 us -> 25.2 us  [flip(): return lax.ppermute(value, axis, [(i, i ^ bits) for i in range(size)])]
    convert_element_type x0 -> x5, other arithmetic: none -> 2.39 us  [the longest x3 2.18 us: per_device(): share = share + flip(sums[k].astype(BF), 'ctx', ctx, 2 * k).astype(F32)]
    unnamed x16 -> x52, local copies, waits for them, and re-layouts: 4.03 us -> 2.41 us
  transfers between devices with their start and end apart: 9 -> 30, of which waited for: 6 -> 9; matrix products, arithmetic and copies ran while one was open for 1% -> 3% of each run, Pallas kernels for 35% -> 38%
where the time goes in v2:
time: 89.9 us; the launch traced here: 89.5 us
  Pallas kernels  35.9 us (40%)
  waiting for transfers between devices  25.2 us (28%)
  starting transfers between devices  21.8 us (24%)
  other arithmetic  3.21 us (4%)
  local copies, waits for them, and re-layouts  2.41 us (3%)
  between operations  0.93 us (1%)
    ppermute x30, waiting for transfers between devices, flip(): return lax.ppermute(value, axis, [(i, i ^ bits) for i in range(size)])  25.2 us
    ppermute x30, starting transfers between devices, flip(): return lax.ppermute(value, axis, [(i, i ^ bits) for i in range(size)])  21.8 us
    pallas_call x1, Pallas kernels, run_attend(): pl.pallas_call(functools.partial(attend_kernel, cells, ctx), grid=(1,), o...  14.1 us
    pallas_call x1, Pallas kernels, run_grad(): pl.pallas_call(functools.partial(grad_kernel, chips), out_shape=[jax.Shap...  9.55 us
    pallas_call x1, Pallas kernels, run_conv(): pl.pallas_call(functools.partial(conv_kernel, cells), out_shape=[jax.Shap...  8.29 us
    unnamed x52, local copies, waits for them, and re-layouts  2.41 us
    pallas_call x1, Pallas kernels, run_place(): pl.pallas_call(place_kernel, grid=(1,), out_shape=jax.ShapeDtypeStruct(sh...  2.32 us
    convert_element_type x3, other arithmetic, per_device(): share = share + flip(sums[k].astype(BF), 'ctx', ctx, 2 * k).astype(F32)  2.18 us
  transfers between devices with their start and end apart: 30, of which 9 were waited for; matrix products, arithmetic and copies ran while one was open for 3% of the time, Pallas kernels for 38%

profile of v2, /device:TPU:0, one launch (start us, length us, event | category | flops | bytes accessed | tf_op | source)
XLA Modules:
  0.0 89.5 jit_solution(14856673933633435688)
XLA Ops:
  0.6 1.7 %cut_tails.1.refs_0_ = bf16[4,2,8,16,128]{4,3,2,1,0:T(8,128)(2,1)} custom-call(bf16[4,8,8,16,128]{4,3,2,1,0:T(8,128)(2,1)} %bitcast.12), custom_call_target="tpu_custom_call" | custom-call | bytes 500000 | tf_op jit(solution)/shard_map/cut_tails/pallas_call | solution.py:163
  2.3 2.9 %collective-permute-start.14 = (bf16[4,2,8,16,128]{4,3,2,1,0:T(8,128)(2,1)}, bf16[4,2,8,16,128]{4,3,2,1,0:T(8,128)(2,1)S(1)}, u32[]{:S(2)}, u32[]{:S(2)}) collective-permute-start(bf16[4,2,8,16,128]{4,3,2,1,0:T(8,128)(2,1)} %cut_tails.1.refs_0_), channel_id=1, source_target_pairs={{0,2},{1,3},{2,0},{3,1},{4,6},{5,7},{6,4},{7,5},{8,10},{9,11},{10,... | collective-permute-start | bytes 786440 | tf_op jit(solution)/shard_map/ppermute | solution.py:410
  5.3 1.5 %collective-permute-start.15 = (bf16[4,2,8,16,128]{4,3,2,1,0:T(8,128)(2,1)}, bf16[4,2,8,16,128]{4,3,2,1,0:T(8,128)(2,1)S(1)}, u32[]{:S(2)}, u32[]{:S(2)}) collective-permute-start(bf16[4,2,8,16,128]{4,3,2,1,0:T(8,128)(2,1)} %cut_tails.1.refs_0_), channel_id=1, source_target_pairs={{0,4},{1,5},{2,6},{3,7},{4,0},{5,1},{6,2},{7,3},{8,12},{9,13},{10,... | collective-permute-start | bytes 786440 | tf_op jit(solution)/shard_map/ppermute | solution.py:410
  6.8 8.3 %conv_forward.1 = (bf16[2,320,256]{2,1,0:T(8,128)(2,1)}, bf16[2,320,256]{2,1,0:T(8,128)(2,1)}, bf16[2,320,256]{2,1,0:T(8,128)(2,1)}, bf16[2,320,256]{2,1,0:T(8,128)(2,1)}) custom-call(s32[1]{0:T(128)} %bitcast.me_ref, bf16[4,8,8,16,128]{4,3,2,1,0:T(8,128)(2,1)} %bitcast.13, bf16[3456,256]{1,0:T(8,128)(2,1)} %w_ref.1), custom_call_target="tpu_custom_call" | custom-call | flops 4800000000 | bytes 4000000 | tf_op jit(solution)/shard_map/conv_forward/pallas_call | solution.py:140
  15.1 3.8 %collective-permute-done.15.refs_4_ = bf16[4,2,8,16,128]{4,3,2,1,0:T(8,128)(2,1)S(1)} collective-permute-done((bf16[4,2,8,16,128]{4,3,2,1,0:T(8,128)(2,1)}, bf16[4,2,8,16,128]{4,3,2,1,0:T(8,128)(2,1)S(1)}, u32[]{:S(2)}, u32[]{:S(2)}) %collective-permute-start.15) | collective-permute-done | bytes 262176 | tf_op jit(solution)/shard_map/ppermute | solution.py:410
  20.0 1.2 %collective-permute-start.1 = (bf16[2,320,256]{2,1,0:T(8,128)(2,1)}, bf16[2,320,256]{2,1,0:T(8,128)(2,1)S(1)}, u32[]{:S(2)}, u32[]{:S(2)}) collective-permute-start(bf16[2,320,256]{2,1,0:T(8,128)(2,1)} %get-tuple-element.23), channel_id=1, source_target_pairs={{0,2},{1,3},{2,0},{3,1},{4,6},{5,7},{6,4},{7,5},{8,10},{9,11},{10,... | collective-permute-start | bytes 983048 | tf_op jit(solution)/shard_map/ppermute | solution.py:410
  21.1 0.9 collective-permute-start.3
  22.0 1.4 %collective-permute-start.5 = (bf16[2,320,256]{2,1,0:T(8,128)(2,1)}, bf16[2,320,256]{2,1,0:T(8,128)(2,1)S(1)}, u32[]{:S(2)}, u32[]{:S(2)}) collective-permute-start(bf16[2,320,256]{2,1,0:T(8,128)(2,1)} %get-tuple-element.25), channel_id=1, source_target_pairs={{0,6},{1,7},{2,4},{3,5},{4,2},{5,3},{6,0},{7,1},{8,14},{9,15},{10,... | collective-permute-start | bytes 983048 | tf_op jit(solution)/shard_map/ppermute | solution.py:410
  23.5 0.6 copy-done.23
  24.3 9.5 %conv_gradient.1 = (bf16[432,256]{1,0:T(8,128)(2,1)}, bf16[432,256]{1,0:T(8,128)(2,1)}, bf16[432,256]{1,0:T(8,128)(2,1)}, bf16[432,256]{1,0:T(8,128)(2,1)}, f32[...) custom-call(s32[32]{0:T(128)} %assign.3, s32[4]{0:T(128)} %counts.3, ...), custom_call_target="tpu_custom_call" | custom-call | flops 4000000000 | bytes 6000000 | tf_op jit(solution)/shard_map/conv_gradient/pallas_call | solution.py:224
  34.5 2.1 %collective-permute-done.3.refs_4_ = bf16[2,320,256]{2,1,0:T(8,128)(2,1)S(1)} collective-permute-done((bf16[2,320,256]{2,1,0:T(8,128)(2,1)}, bf16[2,320,256]{2,1,0:T(8,128)(2,1)S(1)}, u32[]{:S(2)}, u32[]{:S(2)}) %collective-permute-start.3) | collective-permute-done | bytes 327712 | tf_op jit(solution)/shard_map/ppermute | solution.py:410
  36.6 1.2 %collective-permute-done.5.refs_6_ = bf16[2,320,256]{2,1,0:T(8,128)(2,1)S(1)} collective-permute-done((bf16[2,320,256]{2,1,0:T(8,128)(2,1)}, bf16[2,320,256]{2,1,0:T(8,128)(2,1)S(1)}, u32[]{:S(2)}, u32[]{:S(2)}) %collective-permute-start.5) | collective-permute-done | bytes 327712 | tf_op jit(solution)/shard_map/ppermute | solution.py:410
  38.4 1.1 %add_convert_fusion.4 = bf16[432,256]{1,0:T(8,128)(2,1)S(1)} fusion(f32[432,256]{1,0:T(8,128)} %get-tuple-element.36, bf16[432,256]{1,0:T(8,128)(2,1)S(1)} %collective-permute-done.22), kind=kLoop, calls=%fused_computation.5 | loop fusion | flops 331776 | bytes 884736 | tf_op jit(solution)/shard_map/convert_element_type | solution.py:436
  39.4 0.6 collective-permute-done.24
  40.1 1.1 %add_convert_fusion.3 = bf16[432,256]{1,0:T(8,128)(2,1)S(1)} fusion(f32[432,256]{1,0:T(8,128)} %get-tuple-element.38, bf16[432,256]{1,0:T(8,128)(2,1)S(1)} %collective-permute-done.24), kind=kLoop, calls=%fused_computation.4 | loop fusion | flops 331776 | bytes 884736 | tf_op jit(solution)/shard_map/convert_element_type | solution.py:436
  41.9 2.3 %collective-permute-start.23 = (bf16[432,256]{1,0:T(8,128)(2,1)S(1)}, bf16[432,256]{1,0:T(8,128)(2,1)S(1)}, u32[]{:S(2)}, u32[]{:S(2)}) collective-permute-start(bf16[432,256]{1,0:T(8,128)(2,1)S(1)} %add_convert_fusion.4), channel_id=1, source_target_pairs={{0,6},{1,7},{2,4},{3,5},{4,2},{5,3},{6,0},{7,1},{8,14},{9,15},{10,... | collective-permute-start | bytes 663560 | tf_op jit(solution)/shard_map/ppermute | solution.py:410
  44.2 0.5 collective-permute-start.25
  44.7 0.8 collective-permute-start.27
  45.6 0.7 copy-done.17
  46.3 14.1 %attend.1 = (bf16[2,256,256]{2,1,0:T(8,128)(2,1)}, bf16[2,256,256]{2,1,0:T(8,128)(2,1)}, bf16[2,256,256]{2,1,0:T(8,128)(2,1)}, bf16[2,256,256]{2,1,0:T(8,128)(2,1)}) custom-call(s32[32]{0:T(128)} %assign.3, s32[4]{0:T(128)} %counts.3, f32[4]{0:T(128)} %scale.1, s32[1]{0:T(128)} %bitcast.me_ref, bf16[256,768]{1,0:T(8,128)(2,1)} %qkv_ref.1, ...), custom_call_target="tpu_custom_call" | custom-call | flops 3000000000 | bytes 4000000 | tf_op jit(solution)/shard_map/attend/pallas_call | solution.py:362
  60.4 1.3 %collective-permute-start.8 = (bf16[2,256,256]{2,1,0:T(8,128)(2,1)}, bf16[2,256,256]{2,1,0:T(8,128)(2,1)S(1)}, u32[]{:S(2)}, u32[]{:S(2)}) collective-permute-start(bf16[2,256,256]{2,1,0:T(8,128)(2,1)} %get-tuple-element.27), channel_id=1, source_target_pairs={{0,2},{1,3},{2,0},{3,1},{4,6},{5,7},{6,4},{7,5},{8,10},{9,11},{10,... | collective-permute-start | bytes 786440 | tf_op jit(solution)/shard_map/ppermute | solution.py:410
  61.6 1.5 %collective-permute-start.10 = (bf16[2,256,256]{2,1,0:T(8,128)(2,1)}, bf16[2,256,256]{2,1,0:T(8,128)(2,1)S(1)}, u32[]{:S(2)}, u32[]{:S(2)}) collective-permute-start(bf16[2,256,256]{2,1,0:T(8,128)(2,1)} %get-tuple-element.28), channel_id=1, source_target_pairs={{0,4},{1,5},{2,6},{3,7},{4,0},{5,1},{6,2},{7,3},{8,12},{9,13},{10,... | collective-permute-start | bytes 786440 | tf_op jit(solution)/shard_map/ppermute | solution.py:410
  63.2 0.7 collective-permute-start.12
  64.0 1.6 %collective-permute-start.28 = (bf16[432,256]{1,0:T(8,128)(2,1)S(1)}, bf16[432,256]{1,0:T(8,128)(2,1)S(1)}, u32[]{:S(2)}, u32[]{:S(2)}) collective-permute-start(bf16[432,256]{1,0:T(8,128)(2,1)S(1)} %add_convert_fusion.1), channel_id=1, source_target_pairs={{0,8},{8,0},{16,24},{24,16},{1,9},{9,1},{17,25},{25,17},{2,10},{10... | collective-permute-start | bytes 663560 | tf_op jit(solution)/shard_map/ppermute | solution.py:410
  65.7 4.1 %collective-permute-done.8 = bf16[2,256,256]{2,1,0:T(8,128)(2,1)S(1)} collective-permute-done((bf16[2,256,256]{2,1,0:T(8,128)(2,1)}, bf16[2,256,256]{2,1,0:T(8,128)(2,1)S(1)}, u32[]{:S(2)}, u32[]{:S(2)}) %collective-permute-start.8) | collective-permute-done | bytes 262176 | tf_op jit(solution)/shard_map/ppermute | solution.py:410
  69.8 4.3 %collective-permute-done.10 = bf16[2,256,256]{2,1,0:T(8,128)(2,1)S(1)} collective-permute-done((bf16[2,256,256]{2,1,0:T(8,128)(2,1)}, bf16[2,256,256]{2,1,0:T(8,128)(2,1)S(1)}, u32[]{:S(2)}, u32[]{:S(2)}) %collective-permute-start.10) | collective-permute-done | bytes 262176 | tf_op jit(solution)/shard_map/ppermute | solution.py:410
  74.1 1.0 %collective-permute-done.12 = bf16[2,256,256]{2,1,0:T(8,128)(2,1)S(1)} collective-permute-done((bf16[2,256,256]{2,1,0:T(8,128)(2,1)}, bf16[2,256,256]{2,1,0:T(8,128)(2,1)S(1)}, u32[]{:S(2)}, u32[]{:S(2)}) %collective-permute-start.12) | collective-permute-done | bytes 262176 | tf_op jit(solution)/shard_map/ppermute | solution.py:410
  75.2 2.7 %collective-permute-start.29 = (bf16[432,256]{1,0:T(8,128)(2,1)S(1)}, bf16[432,256]{1,0:T(8,128)(2,1)S(1)}, u32[]{:S(2)}, u32[]{:S(2)}) collective-permute-start(bf16[432,256]{1,0:T(8,128)(2,1)S(1)} %add_convert_fusion), channel_id=1, source_target_pairs={{0,16},{8,24},{16,0},{24,8},{1,17},{9,25},{17,1},{25,9},{2,18},{10... | collective-permute-start | bytes 663560 | tf_op jit(solution)/shard_map/ppermute | solution.py:410
  77.9 0.6 copy-done.6
  78.8 2.3 %place_latents.1 = bf16[16,8,16,256]{3,2,1,0:T(8,128)(2,1)} custom-call(s32[1]{0:T(128)} %bitcast.me_ref, bf16[2,16,16,256]{3,2,1,0:T(8,128)(2,1)} %bitcast.16, bf16[2,16,16,256]{3,2,1,0:T(8,128)(2,1)} %bitcast.20, bf16[2,16,16,256]{3,2,1,0:T(8,128)(2,1)} %bitcast.17, bf16[2,16,16,256]{3,2,1,0:T(8,128)(2,1)} %bitcast.21, bf16[2,16,16,256]{3,2,1,0:T(8,128)(2,1)} %bitcast.18, ...), custom_call_target="tpu_custom_call" | custom-call | bytes 2000000 | tf_op jit(solution)/shard_map/place_latents/pallas_call | solution.py:397
  81.1 7.6 %collective-permute-done.29 = bf16[432,256]{1,0:T(8,128)(2,1)S(1)} collective-permute-done((bf16[432,256]{1,0:T(8,128)(2,1)S(1)}, bf16[432,256]{1,0:T(8,128)(2,1)S(1)}, u32[]{:S(2)}, u32[]{:S(2)}) %collective-permute-start.29) | collective-permute-done | bytes 221216 | tf_op jit(solution)/shard_map/ppermute | solution.py:410
  88.7 0.8 convert_add_fusion
  (91 shorter events, 3.8 us)
Async XLA Ops:
  2.3 12.8 %collective-permute-start.14 = (bf16[4,2,8,16,128]{4,3,2,1,0:T(8,128)(2,1)}, bf16[4,2,8,16,128]{4,3,2,1,0:T(8,128)(2,1)S(1)}, u32[]{:S(2)}, u32[]{:S(2)}) collective-permute-start(bf16[4,2,8,16,128]{4,3,2,1,0:T(8,128)(2,1)} %cut_tails.1.refs_0_), channel_id=1, source_target_pairs={{0,2},{1,3},{2,0},{3,1},{4,6},{5,7},{6,4},{7,5},{8,10},{9,11},{10,... | collective-permute-start | bytes 786440 | tf_op jit(solution)/shard_map/ppermute | solution.py:410
  5.3 13.6 %collective-permute-start.15 = (bf16[4,2,8,16,128]{4,3,2,1,0:T(8,128)(2,1)}, bf16[4,2,8,16,128]{4,3,2,1,0:T(8,128)(2,1)S(1)}, u32[]{:S(2)}, u32[]{:S(2)}) collective-permute-start(bf16[4,2,8,16,128]{4,3,2,1,0:T(8,128)(2,1)} %cut_tails.1.refs_0_), channel_id=1, source_target_pairs={{0,4},{1,5},{2,6},{3,7},{4,0},{5,1},{6,2},{7,3},{8,12},{9,13},{10,... | collective-permute-start | bytes 786440 | tf_op jit(solution)/shard_map/ppermute | solution.py:410
  6.8 12.1 %collective-permute-start.16 = (bf16[4,2,8,16,128]{4,3,2,1,0:T(8,128)(2,1)}, bf16[4,2,8,16,128]{4,3,2,1,0:T(8,128)(2,1)S(1)}, u32[]{:S(2)}, u32[]{:S(2)}) collective-permute-start(bf16[4,2,8,16,128]{4,3,2,1,0:T(8,128)(2,1)} %cut_tails.1.refs_0_), channel_id=1, source_target_pairs={{0,6},{1,7},{2,4},{3,5},{4,2},{5,3},{6,0},{7,1},{8,14},{9,15},{10,... | collective-permute-start | bytes 786440 | tf_op jit(solution)/shard_map/ppermute | solution.py:410
  6.8 12.1 %copy-start.2 = (bf16[4,2,8,16,128]{4,3,2,1,0:T(8,128)(2,1)S(1)}, bf16[4,2,8,16,128]{4,3,2,1,0:T(8,128)(2,1)}, u32[]{:S(2)}) copy-start(bf16[4,2,8,16,128]{4,3,2,1,0:T(8,128)(2,1)} %cut_tails.1.refs_0_) | copy-start | bytes 786436
  18.9 2.3 %collective-permute-start.17 = (bf16[4,2,8,16,128]{4,3,2,1,0:T(8,128)(2,1)S(1)}, bf16[4,2,8,16,128]{4,3,2,1,0:T(8,128)(2,1)S(1)}, u32[]{:S(2)}, u32[]{:S(2)}) collective-permute-start(bf16[4,2,8,16,128]{4,3,2,1,0:T(8,128)(2,1)S(1)} %copy-done.2), channel_id=1, source_target_pairs={{0,1},{1,0},{2,3},{3,2},{4,5},{5,4},{6,7},{7,6},{8,9},{9,8},{10,11... | collective-permute-start | bytes 786440 | tf_op jit(solution)/shard_map/ppermute | solution.py:410
  18.9 3.1 %collective-permute-start.18 = (bf16[4,2,8,16,128]{4,3,2,1,0:T(8,128)(2,1)S(1)}, bf16[4,2,8,16,128]{4,3,2,1,0:T(8,128)(2,1)S(1)}, u32[]{:S(2)}, u32[]{:S(2)}) collective-permute-start(bf16[4,2,8,16,128]{4,3,2,1,0:T(8,128)(2,1)S(1)} %collective-permute-done.14.refs_2_), channel_id=1, source_target_pairs={{0,1},{1,0},{2,3},{3,2},{4,5},{5,4},{6,7},{7,6},{8,9},{9,8},{10,11... | collective-permute-start | bytes 786440 | tf_op jit(solution)/shard_map/ppermute | solution.py:410
  19.4 4.0 %collective-permute-start.19 = (bf16[4,2,8,16,128]{4,3,2,1,0:T(8,128)(2,1)S(1)}, bf16[4,2,8,16,128]{4,3,2,1,0:T(8,128)(2,1)S(1)}, u32[]{:S(2)}, u32[]{:S(2)}) collective-permute-start(bf16[4,2,8,16,128]{4,3,2,1,0:T(8,128)(2,1)S(1)} %collective-permute-done.15.refs_4_), channel_id=1, source_target_pairs={{0,1},{1,0},{2,3},{3,2},{4,5},{5,4},{6,7},{7,6},{8,9},{9,8},{10,11... | collective-permute-start | bytes 786440 | tf_op jit(solution)/shard_map/ppermute | solution.py:410
  19.5 3.9 %collective-permute-start.20 = (bf16[4,2,8,16,128]{4,3,2,1,0:T(8,128)(2,1)S(1)}, bf16[4,2,8,16,128]{4,3,2,1,0:T(8,128)(2,1)S(1)}, u32[]{:S(2)}, u32[]{:S(2)}) collective-permute-start(bf16[4,2,8,16,128]{4,3,2,1,0:T(8,128)(2,1)S(1)} %collective-permute-done.16.refs_6_), channel_id=1, source_target_pairs={{0,1},{1,0},{2,3},{3,2},{4,5},{5,4},{6,7},{7,6},{8,9},{9,8},{10,11... | collective-permute-start | bytes 786440 | tf_op jit(solution)/shard_map/ppermute | solution.py:410
  20.0 14.5 %collective-permute-start.1 = (bf16[2,320,256]{2,1,0:T(8,128)(2,1)}, bf16[2,320,256]{2,1,0:T(8,128)(2,1)S(1)}, u32[]{:S(2)}, u32[]{:S(2)}) collective-permute-start(bf16[2,320,256]{2,1,0:T(8,128)(2,1)} %get-tuple-element.23), channel_id=1, source_target_pairs={{0,2},{1,3},{2,0},{3,1},{4,6},{5,7},{6,4},{7,5},{8,10},{9,11},{10,... | collective-permute-start | bytes 983048 | tf_op jit(solution)/shard_map/ppermute | solution.py:410
  21.1 15.5 %collective-permute-start.3 = (bf16[2,320,256]{2,1,0:T(8,128)(2,1)}, bf16[2,320,256]{2,1,0:T(8,128)(2,1)S(1)}, u32[]{:S(2)}, u32[]{:S(2)}) collective-permute-start(bf16[2,320,256]{2,1,0:T(8,128)(2,1)} %get-tuple-element.24), channel_id=1, source_target_pairs={{0,4},{1,5},{2,6},{3,7},{4,0},{5,1},{6,2},{7,3},{8,12},{9,13},{10,... | collective-permute-start | bytes 983048 | tf_op jit(solution)/shard_map/ppermute | solution.py:410
  22.0 15.8 %collective-permute-start.5 = (bf16[2,320,256]{2,1,0:T(8,128)(2,1)}, bf16[2,320,256]{2,1,0:T(8,128)(2,1)S(1)}, u32[]{:S(2)}, u32[]{:S(2)}) collective-permute-start(bf16[2,320,256]{2,1,0:T(8,128)(2,1)} %get-tuple-element.25), channel_id=1, source_target_pairs={{0,6},{1,7},{2,4},{3,5},{4,2},{5,3},{6,0},{7,1},{8,14},{9,15},{10,... | collective-permute-start | bytes 983048 | tf_op jit(solution)/shard_map/ppermute | solution.py:410
  33.8 4.0 %collective-permute-start.22 = (bf16[432,256]{1,0:T(8,128)(2,1)}, bf16[432,256]{1,0:T(8,128)(2,1)S(1)}, u32[]{:S(2)}, u32[]{:S(2)}) collective-permute-start(bf16[432,256]{1,0:T(8,128)(2,1)} %get-tuple-element.37), channel_id=1, source_target_pairs={{0,1},{1,0},{2,3},{3,2},{4,5},{5,4},{6,7},{7,6},{8,9},{9,8},{10,11... | collective-permute-start | bytes 663560 | tf_op jit(solution)/shard_map/ppermute | solution.py:410
  33.9 8.0 %collective-permute-start = (bf16[2,320,256]{2,1,0:T(8,128)(2,1)S(1)}, bf16[2,320,256]{2,1,0:T(8,128)(2,1)S(1)}, u32[]{:S(2)}, u32[]{:S(2)}) collective-permute-start(bf16[2,320,256]{2,1,0:T(8,128)(2,1)S(1)} %copy-done.10), channel_id=1, source_target_pairs={{0,1},{1,0},{2,3},{3,2},{4,5},{5,4},{6,7},{7,6},{8,9},{9,8},{10,11... | collective-permute-start | bytes 983048 | tf_op jit(solution)/shard_map/ppermute | solution.py:410
  34.4 9.8 %collective-permute-start.2 = (bf16[2,320,256]{2,1,0:T(8,128)(2,1)S(1)}, bf16[2,320,256]{2,1,0:T(8,128)(2,1)S(1)}, u32[]{:S(2)}, u32[]{:S(2)}) collective-permute-start(bf16[2,320,256]{2,1,0:T(8,128)(2,1)S(1)} %collective-permute-done.1.refs_2_), channel_id=1, source_target_pairs={{0,1},{1,0},{2,3},{3,2},{4,5},{5,4},{6,7},{7,6},{8,9},{9,8},{10,11... | collective-permute-start | bytes 983048 | tf_op jit(solution)/shard_map/ppermute | solution.py:410
  36.6 8.1 %collective-permute-start.4 = (bf16[2,320,256]{2,1,0:T(8,128)(2,1)S(1)}, bf16[2,320,256]{2,1,0:T(8,128)(2,1)S(1)}, u32[]{:S(2)}, u32[]{:S(2)}) collective-permute-start(bf16[2,320,256]{2,1,0:T(8,128)(2,1)S(1)} %collective-permute-done.3.refs_4_), channel_id=1, source_target_pairs={{0,1},{1,0},{2,3},{3,2},{4,5},{5,4},{6,7},{7,6},{8,9},{9,8},{10,11... | collective-permute-start | bytes 983048 | tf_op jit(solution)/shard_map/ppermute | solution.py:410
  37.8 7.7 %collective-permute-start.6 = (bf16[2,320,256]{2,1,0:T(8,128)(2,1)S(1)}, bf16[2,320,256]{2,1,0:T(8,128)(2,1)S(1)}, u32[]{:S(2)}, u32[]{:S(2)}) collective-permute-start(bf16[2,320,256]{2,1,0:T(8,128)(2,1)S(1)} %collective-permute-done.5.refs_6_), channel_id=1, source_target_pairs={{0,1},{1,0},{2,3},{3,2},{4,5},{5,4},{6,7},{7,6},{8,9},{9,8},{10,11... | collective-permute-start | bytes 983048 | tf_op jit(solution)/shard_map/ppermute | solution.py:410
  37.8 2.1 %collective-permute-start.24 = (bf16[432,256]{1,0:T(8,128)(2,1)}, bf16[432,256]{1,0:T(8,128)(2,1)S(1)}, u32[]{:S(2)}, u32[]{:S(2)}) collective-permute-start(bf16[432,256]{1,0:T(8,128)(2,1)} %get-tuple-element.39), channel_id=1, source_target_pairs={{0,1},{1,0},{2,3},{3,2},{4,5},{5,4},{6,7},{7,6},{8,9},{9,8},{10,11... | collective-permute-start | bytes 663560 | tf_op jit(solution)/shard_map/ppermute | solution.py:410
  40.0 1.7 %collective-permute-start.26 = (bf16[432,256]{1,0:T(8,128)(2,1)}, bf16[432,256]{1,0:T(8,128)(2,1)S(1)}, u32[]{:S(2)}, u32[]{:S(2)}) collective-permute-start(bf16[432,256]{1,0:T(8,128)(2,1)} %get-tuple-element.41), channel_id=1, source_target_pairs={{0,1},{1,0},{2,3},{3,2},{4,5},{5,4},{6,7},{7,6},{8,9},{9,8},{10,11... | collective-permute-start | bytes 663560 | tf_op jit(solution)/shard_map/ppermute | solution.py:410
  41.7 19.9 %collective-permute-start.21 = (bf16[432,256]{1,0:T(8,128)(2,1)S(1)}, bf16[432,256]{1,0:T(8,128)(2,1)S(1)}, u32[]{:S(2)}, u32[]{:S(2)}) collective-permute-start(bf16[432,256]{1,0:T(8,128)(2,1)S(1)} %copy-done.25), channel_id=1, source_target_pairs={{0,1},{1,0},{2,3},{3,2},{4,5},{5,4},{6,7},{7,6},{8,9},{9,8},{10,11... | collective-permute-start | bytes 663560 | tf_op jit(solution)/shard_map/ppermute | solution.py:410
  41.9 22.0 %copy-start = (f32[432,256]{1,0:T(8,128)S(1)}, f32[432,256]{1,0:T(8,128)}, u32[]{:S(2)}) copy-start(f32[432,256]{1,0:T(8,128)} %get-tuple-element.34) | copy-start | bytes 1327108
  41.9 21.2 %collective-permute-start.23 = (bf16[432,256]{1,0:T(8,128)(2,1)S(1)}, bf16[432,256]{1,0:T(8,128)(2,1)S(1)}, u32[]{:S(2)}, u32[]{:S(2)}) collective-permute-start(bf16[432,256]{1,0:T(8,128)(2,1)S(1)} %add_convert_fusion.4), channel_id=1, source_target_pairs={{0,6},{1,7},{2,4},{3,5},{4,2},{5,3},{6,0},{7,1},{8,14},{9,15},{10,... | collective-permute-start | bytes 663560 | tf_op jit(solution)/shard_map/ppermute | solution.py:410
  44.2 19.6 %collective-permute-start.25 = (bf16[432,256]{1,0:T(8,128)(2,1)S(1)}, bf16[432,256]{1,0:T(8,128)(2,1)S(1)}, u32[]{:S(2)}, u32[]{:S(2)}) collective-permute-start(bf16[432,256]{1,0:T(8,128)(2,1)S(1)} %add_convert_fusion.3), channel_id=1, source_target_pairs={{0,4},{1,5},{2,6},{3,7},{4,0},{5,1},{6,2},{7,3},{8,12},{9,13},{10,... | collective-permute-start | bytes 663560 | tf_op jit(solution)/shard_map/ppermute | solution.py:410
  44.7 19.1 %collective-permute-start.27 = (bf16[432,256]{1,0:T(8,128)(2,1)S(1)}, bf16[432,256]{1,0:T(8,128)(2,1)S(1)}, u32[]{:S(2)}, u32[]{:S(2)}) collective-permute-start(bf16[432,256]{1,0:T(8,128)(2,1)S(1)} %add_convert_fusion.2), channel_id=1, source_target_pairs={{0,2},{1,3},{2,0},{3,1},{4,6},{5,7},{6,4},{7,5},{8,10},{9,11},{10,... | collective-permute-start | bytes 663560 | tf_op jit(solution)/shard_map/ppermute | solution.py:410
  60.4 9.4 %collective-permute-start.8 = (bf16[2,256,256]{2,1,0:T(8,128)(2,1)}, bf16[2,256,256]{2,1,0:T(8,128)(2,1)S(1)}, u32[]{:S(2)}, u32[]{:S(2)}) collective-permute-start(bf16[2,256,256]{2,1,0:T(8,128)(2,1)} %get-tuple-element.27), channel_id=1, source_target_pairs={{0,2},{1,3},{2,0},{3,1},{4,6},{5,7},{6,4},{7,5},{8,10},{9,11},{10,... | collective-permute-start | bytes 786440 | tf_op jit(solution)/shard_map/ppermute | solution.py:410
  61.6 12.4 %collective-permute-start.10 = (bf16[2,256,256]{2,1,0:T(8,128)(2,1)}, bf16[2,256,256]{2,1,0:T(8,128)(2,1)S(1)}, u32[]{:S(2)}, u32[]{:S(2)}) collective-permute-start(bf16[2,256,256]{2,1,0:T(8,128)(2,1)} %get-tuple-element.28), channel_id=1, source_target_pairs={{0,4},{1,5},{2,6},{3,7},{4,0},{5,1},{6,2},{7,3},{8,12},{9,13},{10,... | collective-permute-start | bytes 786440 | tf_op jit(solution)/shard_map/ppermute | solution.py:410
  63.2 11.9 %collective-permute-start.12 = (bf16[2,256,256]{2,1,0:T(8,128)(2,1)}, bf16[2,256,256]{2,1,0:T(8,128)(2,1)S(1)}, u32[]{:S(2)}, u32[]{:S(2)}) collective-permute-start(bf16[2,256,256]{2,1,0:T(8,128)(2,1)} %get-tuple-element.29), channel_id=1, source_target_pairs={{0,6},{1,7},{2,4},{3,5},{4,2},{5,3},{6,0},{7,1},{8,14},{9,15},{10,... | collective-permute-start | bytes 786440 | tf_op jit(solution)/shard_map/ppermute | solution.py:410
  64.0 11.1 %collective-permute-start.28 = (bf16[432,256]{1,0:T(8,128)(2,1)S(1)}, bf16[432,256]{1,0:T(8,128)(2,1)S(1)}, u32[]{:S(2)}, u32[]{:S(2)}) collective-permute-start(bf16[432,256]{1,0:T(8,128)(2,1)S(1)} %add_convert_fusion.1), channel_id=1, source_target_pairs={{0,8},{8,0},{16,24},{24,16},{1,9},{9,1},{17,25},{25,17},{2,10},{10... | collective-permute-start | bytes 663560 | tf_op jit(solution)/shard_map/ppermute | solution.py:410
  65.7 12.1 %collective-permute-start.7 = (bf16[2,256,256]{2,1,0:T(8,128)(2,1)}, bf16[2,256,256]{2,1,0:T(8,128)(2,1)S(1)}, u32[]{:S(2)}, u32[]{:S(2)}) collective-permute-start(bf16[2,256,256]{2,1,0:T(8,128)(2,1)} %get-tuple-element.26), channel_id=1, source_target_pairs={{0,1},{1,0},{2,3},{3,2},{4,5},{5,4},{6,7},{7,6},{8,9},{9,8},{10,11... | collective-permute-start | bytes 786440 | tf_op jit(solution)/shard_map/ppermute | solution.py:410
  69.8 8.0 %collective-permute-start.9 = (bf16[2,256,256]{2,1,0:T(8,128)(2,1)S(1)}, bf16[2,256,256]{2,1,0:T(8,128)(2,1)S(1)}, u32[]{:S(2)}, u32[]{:S(2)}) collective-permute-start(bf16[2,256,256]{2,1,0:T(8,128)(2,1)S(1)} %collective-permute-done.8), channel_id=1, source_target_pairs={{0,1},{1,0},{2,3},{3,2},{4,5},{5,4},{6,7},{7,6},{8,9},{9,8},{10,11... | collective-permute-start | bytes 786440 | tf_op jit(solution)/shard_map/ppermute | solution.py:410
  74.1 3.8 %collective-permute-start.11 = (bf16[2,256,256]{2,1,0:T(8,128)(2,1)S(1)}, bf16[2,256,256]{2,1,0:T(8,128)(2,1)S(1)}, u32[]{:S(2)}, u32[]{:S(2)}) collective-permute-start(bf16[2,256,256]{2,1,0:T(8,128)(2,1)S(1)} %collective-permute-done.10), channel_id=1, source_target_pairs={{0,1},{1,0},{2,3},{3,2},{4,5},{5,4},{6,7},{7,6},{8,9},{9,8},{10,11... | collective-permute-start | bytes 786440 | tf_op jit(solution)/shard_map/ppermute | solution.py:410
  75.1 2.8 %collective-permute-start.13 = (bf16[2,256,256]{2,1,0:T(8,128)(2,1)S(1)}, bf16[2,256,256]{2,1,0:T(8,128)(2,1)S(1)}, u32[]{:S(2)}, u32[]{:S(2)}) collective-permute-start(bf16[2,256,256]{2,1,0:T(8,128)(2,1)S(1)} %collective-permute-done.12), channel_id=1, source_target_pairs={{0,1},{1,0},{2,3},{3,2},{4,5},{5,4},{6,7},{7,6},{8,9},{9,8},{10,11... | collective-permute-start | bytes 786440 | tf_op jit(solution)/shard_map/ppermute | solution.py:410
  75.2 13.5 %collective-permute-start.29 = (bf16[432,256]{1,0:T(8,128)(2,1)S(1)}, bf16[432,256]{1,0:T(8,128)(2,1)S(1)}, u32[]{:S(2)}, u32[]{:S(2)}) collective-permute-start(bf16[432,256]{1,0:T(8,128)(2,1)S(1)} %add_convert_fusion), channel_id=1, source_target_pairs={{0,16},{8,24},{16,0},{24,8},{1,17},{9,25},{17,1},{25,9},{2,18},{10... | collective-permute-start | bytes 663560 | tf_op jit(solution)/shard_map/ppermute | solution.py:410
  (24 other events, 100.6 us)

commit v3 on v2

--- a/solution.py
+++ b/solution.py
@@ -9,10 +9,11 @@
 
 BF = jnp.bfloat16
 F32 = jnp.float32
-VMEM_LIMIT = 56 * 1024 * 1024
+MIB = 1024 * 1024
 ROWS, COLS, CIN, COUT = 8, 16, 128, 256
 SLOTS, STEPS = 4, 4
 FRAMES = SLOTS * STEPS
+PADDED = (3, ROWS + 2, COLS + 2, FRAMES, CIN)
 TAPS = [(h, w) for h in range(3) for w in range(3)]
 TAP_SETS = [TAPS[0:2], TAPS[2:4], TAPS[4:6], TAPS[6:8], TAPS[8:9]]
 
@@ -35,8 +36,8 @@
     return ((i % outer == j // inner) & (i // outer == j % inner)).astype(F32).astype(BF)
 
 
-def params(**kw):
-    return pltpu.CompilerParams(vmem_limit_bytes=VMEM_LIMIT, **kw)
+def params(mib):
+    return pltpu.CompilerParams(vmem_limit_bytes=mib * MIB)
 
 
 def cost(flops, nbytes):
@@ -45,6 +46,7 @@
 
 VMEM = pl.BlockSpec(memory_space=pltpu.VMEM)
 SMEM = pl.BlockSpec(memory_space=pltpu.SMEM)
+HBM = pl.BlockSpec(memory_space=pltpu.HBM)
 ANY = pl.BlockSpec(memory_space=pl.ANY)
 
 
@@ -80,12 +82,14 @@
             turned = dot(swap, jnp.concatenate(cols, axis=1)).astype(BF)
             for n in range(2):
                 part = turned[:, n * CIN : (n + 1) * CIN].reshape(COLS, FRAMES, CIN)
-                padded[r + n + 1, 1 : COLS + 1, :, kt * CIN : (kt + 1) * CIN] = part
+                padded[kt, r + n + 1, 1 : COLS + 1] = part
 
 
 def tap_block(padded, taps):
-    blocks = [padded[h : h + ROWS, w : w + COLS].reshape(ROWS * COLS * FRAMES, 3 * CIN) for h, w in taps]
-    return blocks[0] if len(blocks) == 1 else jnp.concatenate(blocks, axis=1)
+    blocks = [
+        padded[kt, h : h + ROWS, w : w + COLS].reshape(ROWS * COLS * FRAMES, CIN) for h, w in taps for kt in range(3)
+    ]
+    return jnp.concatenate(blocks, axis=1)
 
 
 def tap_rows(kt, h, w):
@@ -98,15 +102,13 @@
 
 
 def conv_kernel(cells, me_ref, x_ref, w_ref, *refs):
-    out_refs, (main_part, edge_part, padded, edge) = refs[:-4], refs[-4:]
+    out_refs, (main_part, edge_part, padded, edge, x_in, w_in, sem) = refs[:-7], refs[-7:]
+    copies = [pltpu.make_async_copy(x_ref, x_in, sem.at[0]), pltpu.make_async_copy(w_ref, w_in, sem.at[1])]
+    for copy in copies:
+        copy.start()
+    x_ref, w_ref = x_in, w_in
+    copies[0].wait()
     lay_out_taps(x_ref, lambda s, f, r: jnp.zeros((COLS, CIN), BF), padded)
-    total = None
-    for taps in TAP_SETS:
-        rows = jnp.concatenate([w_ref[tap_rows(kt, h, w), :] for h, w in taps for kt in range(3)], axis=0)
-        term = dot(tap_block(padded, taps), rows)
-        total = term if total is None else total + term
-    main = cells * FRAMES
-    main_part[...] = total.astype(BF).reshape(main_part.shape)
     wide = SLOTS * COLS
     i, j = iota((3 * wide, wide), 0), iota((3 * wide, wide), 1)
     k = i % wide
@@ -120,6 +122,14 @@
             [jnp.concatenate([x_ref[s, f, r] for s in range(SLOTS)], axis=0) for f in (6, 7)], axis=1
         )
         edge[r + 1] = dot(shift, tails).astype(BF)
+    copies[1].wait()
+    total = None
+    for taps in TAP_SETS:
+        rows = jnp.concatenate([w_ref[tap_rows(kt, h, w), :] for h, w in taps for kt in range(3)], axis=0)
+        term = dot(tap_block(padded, taps), rows)
+        total = term if total is None else total + term
+    main = cells * FRAMES
+    main_part[...] = total.astype(BF).reshape(main_part.shape)
     carry = None
     for h, w in TAPS:
         rows = jnp.concatenate([w_ref[tap_rows(kt, h, w), :] for kt in range(2)], axis=0)
@@ -140,104 +150,127 @@
     return pl.pallas_call(
         functools.partial(conv_kernel, cells),
         out_shape=[jax.ShapeDtypeStruct((2, cells * (FRAMES + SLOTS), COUT), BF)] * (ctx // 2),
-        in_specs=[SMEM, VMEM, VMEM],
+        in_specs=[SMEM, HBM, HBM],
         out_specs=[VMEM] * (ctx // 2),
         scratch_shapes=[
             pltpu.VMEM((ctx, cells * FRAMES, COUT), BF),
             pltpu.VMEM((ctx, cells * SLOTS, COUT), BF),
-            pltpu.VMEM((ROWS + 2, COLS + 2, FRAMES, 3 * CIN), BF),
+            pltpu.VMEM(PADDED, BF),
             pltpu.VMEM((ROWS + 2, 3 * SLOTS * COLS, 2 * CIN), BF),
+            pltpu.VMEM(frames.shape, BF),
+            pltpu.VMEM(taps.shape, BF),
+            pltpu.SemaphoreType.DMA((2,)),
         ],
-        compiler_params=params(),
+        compiler_params=params(24),
         cost_estimate=cost(4_800_000_000, 4_000_000),
         name="conv_forward",
     )(me, frames, taps)
 
 
-def copy_kernel(x_ref, out_ref):
-    out_ref[...] = x_ref[...]
+def tails_kernel(x_ref, out_ref, sem):
+    copy = pltpu.make_async_copy(x_ref.at[:, 6:8], out_ref, sem)
+    copy.start()
+    copy.wait()
 
 
 def run_tails(frames):
-    shape = (SLOTS, 2, ROWS, COLS, CIN)
     return pl.pallas_call(
-        copy_kernel,
-        grid=(1,),
-        out_shape=jax.ShapeDtypeStruct(shape, BF),
-        in_specs=[pl.BlockSpec(shape, lambda i: (0, 3, 0, 0, 0))],
-        out_specs=pl.BlockSpec(shape, lambda i: (0, 0, 0, 0, 0)),
-        compiler_params=params(),
+        tails_kernel,
+        out_shape=jax.ShapeDtypeStruct((SLOTS, 2, ROWS, COLS, CIN), BF),
+        in_specs=[HBM],
+        out_specs=VMEM,
+        scratch_shapes=[pltpu.SemaphoreType.DMA],
+        compiler_params=params(4),
         cost_estimate=cost(0, 500_000),
         name="cut_tails",
     )(frames)
 
 
-def grad_kernel(chips, assign, counts, me_ref, x_ref, u_ref, unused_ref, *refs):
+def grad_kernel(chips, assign, counts, me_ref, xs_ref, xo_ref, us_ref, uo_ref, *refs):
     tails, refs = refs[: 2 * chips], refs[2 * chips :]
-    sends, keeps = refs[:chips], refs[chips : 2 * chips]
-    slot_of, padded, turned, whole, before, sem = refs[2 * chips :]
+    out_refs = refs[:chips]
+    slot_of, padded, turned, product, before, sem = refs[chips:]
     fill_slots(assign, slot_of)
     me = me_ref[0]
     openings = []
-    for i in range(SLOTS):
-        span = assign[me * SLOTS + i]
-        openings.append(is_opening(span, counts))
-        slot = slot_of[jnp.maximum(span - 1, 0)]
-        apart = (slot // SLOTS) ^ me
-        for n, ref in enumerate(tails):
-
-            @pl.when(apart == n)
-            def _():
-                pltpu.make_async_copy(ref.at[slot % SLOTS], before.at[i], sem.at[i]).start()
-
-    for i in range(SLOTS):
-        pltpu.make_async_copy(tails[0].at[0], before.at[i], sem.at[i]).wait()
-
-    def prev(s, f, r):
-        got = before[s, f + 2, r]
-        return jnp.where(openings[s] > 0, jnp.zeros_like(got), got)
-
-    lay_out_taps(x_ref, prev, padded)
+    for core in range(2):
+        for i in range(SLOTS):
+            span = assign[(me ^ core) * SLOTS + i]
+            openings.append(is_opening(span, counts))
+            slot = slot_of[jnp.maximum(span - 1, 0)]
+            apart = (slot // SLOTS) ^ me
+            for n, ref in enumerate(tails):
+
+                @pl.when(apart == n)
+                def _():
+                    at = core * SLOTS + i
+                    pltpu.make_async_copy(ref.at[slot % SLOTS], before.at[at], sem.at[at]).start()
+
+    for at in range(2 * SLOTS):
+        pltpu.make_async_copy(tails[0].at[0], before.at[at], sem.at[at]).wait()
+
     swap = swap_matrix(FRAMES, COLS)
     span_rows = COLS * FRAMES
-    for r in range(ROWS):
-        block = jnp.concatenate(
-            [u_ref[s, t, r * COLS : (r + 1) * COLS, :] for s in range(SLOTS) for t in range(STEPS)], axis=0
-        )
-        turned[:, r * span_rows : (r + 1) * span_rows] = dot(swap, block).T.astype(BF)
-    for taps in TAP_SETS:
-        product = dot(turned[...], tap_block(padded, taps)).T
-        for n, (h, w) in enumerate(taps):
-            for kt in range(3):
-                at = (n * 3 + kt) * CIN
-                whole[tap_rows(kt, h, w), :] = product[at : at + CIN, :]
-    rows = keeps[0].shape[0]
-    for k in range(chips):
-        kept, sent = device_at(me, k, 0), device_at(me, k, 1)
-        keeps[k][...] = whole[pl.ds(pl.multiple_of(kept * rows, 16), rows), :]
-        sends[k][...] = whole[pl.ds(pl.multiple_of(sent * rows, 16), rows), :].astype(BF)
-
-
-def run_grad(assign, counts, me, frames, upstream, after, tails, ctx):
-    patch = 27 * CIN
-    chips, rows = ctx // 2, patch // ctx
+    total = ROWS * span_rows
+    for core, (x_ref, u_ref) in enumerate(((xs_ref, us_ref), (xo_ref, uo_ref))):
+
+        def prev(s, f, r):
+            got = before[core * SLOTS + s, f + 2, r]
+            return jnp.where(openings[core * SLOTS + s] > 0, jnp.zeros_like(got), got)
+
+        lay_out_taps(x_ref, prev, padded.at[core])
+        for r in range(ROWS):
+            block = jnp.concatenate(
+                [u_ref[s, t, r * COLS : (r + 1) * COLS, :] for s in range(SLOTS) for t in range(STEPS)], axis=0
+            )
+            at = core * total + r * span_rows
+            turned[:, at : at + span_rows] = dot(swap, block).T.astype(BF)
+
+    def entries(tap):
+        kt, h, w = tap // 9, (tap // 3) % 3, tap % 3
+        cores = [
+            padded[core, kt, pl.ds(h, ROWS), pl.ds(w, COLS)].reshape(total, CIN) for core in range(2)
+        ]
+        return jnp.concatenate(cores, axis=0)
+
+    rows = out_refs[0].shape[0]
+    count = -(-rows // CIN)
+    for k, ref in enumerate(out_refs):
+        first = device_at(me, k, 0) * rows
+        tap, offset = first // CIN, first % CIN
+        near = jnp.concatenate([entries(jnp.minimum(tap + n, 26)) for n in range(count)], axis=1)
+        product[: count * CIN, :] = dot(turned[...], near).T
+
+        @pl.when(offset + rows > count * CIN)
+        def _():
+            product[count * CIN :, :] = dot(turned[...], entries(jnp.minimum(tap + count, 26))).T
+
+        if rows % 16 == 0:
+            ref[...] = product[pl.ds(pl.multiple_of(offset, 16), rows), :].astype(ref.dtype)
+        else:
+            size = product.shape[0]
+            ref[...] = pltpu.roll(product[...], (size - offset) % size, 0)[:rows].astype(ref.dtype)
+
+
+def run_grad(assign, counts, me, frames, upstream, tails, ctx):
+    chips, rows = ctx // 2, 27 * CIN // ctx
     return pl.pallas_call(
         functools.partial(grad_kernel, chips),
-        out_shape=[jax.ShapeDtypeStruct((rows, COUT), dtype) for dtype in (BF, F32) for k in range(chips)],
-        in_specs=[SMEM, SMEM, SMEM, VMEM, VMEM, ANY] + [ANY] * ctx,
-        out_specs=[VMEM] * (2 * chips),
+        out_shape=[jax.ShapeDtypeStruct((rows, COUT), F32 if k == 0 else BF) for k in range(chips)],
+        in_specs=[SMEM, SMEM, SMEM, VMEM, VMEM, VMEM, VMEM] + [ANY] * ctx,
+        out_specs=[VMEM] * chips,
         scratch_shapes=[
             pltpu.SMEM(assign.shape, jnp.int32),
-            pltpu.VMEM((ROWS + 2, COLS + 2, FRAMES, 3 * CIN), BF),
-            pltpu.VMEM((COUT, ROWS * COLS * FRAMES), BF),
-            pltpu.VMEM((patch, COUT), F32),
-            pltpu.VMEM((SLOTS, 2, ROWS, COLS, CIN), BF),
-            pltpu.SemaphoreType.DMA((SLOTS,)),
+            pltpu.VMEM((2,) + PADDED, BF),
+            pltpu.VMEM((COUT, 2 * ROWS * COLS * FRAMES), BF),
+            pltpu.VMEM(((-(-rows // CIN) + 1) * CIN, COUT), F32),
+            pltpu.VMEM((2 * SLOTS, 2, ROWS, COLS, CIN), BF),
+            pltpu.SemaphoreType.DMA((2 * SLOTS,)),
         ],
-        compiler_params=params(),
-        cost_estimate=cost(4_000_000_000, 6_000_000),
+        compiler_params=params(32),
+        cost_estimate=cost(1000, 1000),
         name="conv_gradient",
-    )(assign, counts, me, frames, upstream, after, *tails)
+    )(assign, counts, me, *frames, *upstream, *tails)
 
 
 def attend_kernel(cells, ctx, assign, counts, scale, me_ref, qkv_ref, last_ref, *refs):
@@ -374,7 +407,7 @@
             pltpu.VMEM((ctx, cells * SLOTS, COUT), BF),
             pltpu.VMEM((total, total), F32),
         ],
-        compiler_params=params(),
+        compiler_params=params(24),
         cost_estimate=cost(3_000_000_000, 4_000_000),
         name="attend",
     )(assign, counts, scale, me, qkv, last, *got)
@@ -400,7 +433,7 @@
         out_shape=jax.ShapeDtypeStruct(shape, BF),
         in_specs=[SMEM] + [half(n % 2) for n in range(ctx)],
         out_specs=pl.BlockSpec(shape, lambda i: (0, 0, 0, 0)),
-        compiler_params=params(),
+        compiler_params=params(8),
         cost_estimate=cost(0, 2_000_000),
         name="place_latents",
     )(me, *pieces)
@@ -410,13 +443,22 @@
     return lax.ppermute(value, axis, [(i, i ^ bits) for i in range(size)])
 
 
-def exchange(parts, ctx, after=None):
+def send_far(parts, ctx):
     far = [parts[0]] + [None] * (len(parts) - 1)
     for k in reversed(range(1, len(parts))):
         far[k] = flip(parts[k], "ctx", ctx, 2 * k)
-    if after is not None:
-        far = lax.optimization_barrier((far, after))[0]
-    near = [flip(part, "ctx", ctx, 1) for part in far]
+    return far
+
+
+def send_near(value, ctx):
+    return flip(value, "ctx", ctx, 1)
+
+
+def hold(values, after):
+    return lax.optimization_barrier((values, after))[0]
+
+
+def weave(far, near):
     return [piece for pair in zip(far, near) for piece in pair]
 
 
@@ -425,23 +467,29 @@
     frames, upstream = frames[0], upstream[0]
     cells = ROWS * COLS // ctx
     chips = ctx // 2
+    both_frames = (frames, send_near(frames, ctx))
+    both_upstream = (upstream, send_near(upstream, ctx))
+    tails = send_far([run_tails(frames)] * chips, ctx)
     sent = run_conv(me, frames, taps, ctx)
-    tails = exchange([run_tails(frames)] * chips, ctx, sent[0])
-    got = exchange(sent, ctx)
-
-    parts = run_grad(assign, counts, me, frames, upstream, sent[0], tails, ctx)
-    sums = [kept + flip(part, "ctx", ctx, 1).astype(F32) for part, kept in zip(parts[:chips], parts[chips:])]
-    share = sums[0]
-    for k in reversed(range(1, chips)):
-        share = share + flip(sums[k].astype(BF), "ctx", ctx, 2 * k).astype(F32)
+    got = send_far(sent, ctx)
+
+    tails = hold(tails, sent[0])
+    tails = weave(tails, [send_near(part, ctx) for part in tails])
+    halves = run_grad(assign, counts, me, both_frames, both_upstream, tails, ctx)
+    got = [got[0]] + hold(got[1:], halves[1:])
+    got_near = [send_near(part, ctx) for part in got]
+    moved = [flip(halves[k], "ctx", ctx, 2 * k) for k in range(1, chips)]
+    blended = run_attend(assign, counts, scale, me, weave(got, got_near), qkv, last, ctx)
+    share = halves[0]
+    for part in hold(moved, blended[0]):
+        share = share + part.astype(F32)
+    back = send_far(blended, ctx)
     bits = 1
     while bits < dp:
         share = share.astype(BF)
         share = share.astype(F32) + flip(share, "dp", dp, bits).astype(F32)
         bits *= 2
-
-    blended = run_attend(assign, counts, scale, me, got, qkv, last, ctx)
-    latents = run_place(me, exchange(blended, ctx), ctx)
+    latents = run_place(me, weave(back, [send_near(part, ctx) for part in back]), ctx)
     return (latents.reshape(1, SLOTS, STEPS, ctx * cells, COUT), share)
 
 

time: 89.9 us -> 75.4 us (0.84)
  waiting for transfers between devices: 25.2 us -> 17.2 us
  Pallas kernels: 35.9 us -> 33 us
  other arithmetic: 3.21 us -> 0.99 us
  local copies, waits for them, and re-layouts: 2.41 us -> 1.5 us
    ppermute x30 -> x28, waiting for transfers between devices: 25.2 us -> 17.2 us  [flip(): return lax.ppermute(value, axis, [(i, i ^ bits) for i in range(size)])]
    convert_element_type x3 -> x0, other arithmetic: 2.18 us -> none  [per_device(): share = share + flip(sums[k].astype(BF), 'ctx', ctx, 2 * k).astype(F32)]
    pallas_call x1, Pallas kernels: 9.55 us -> 11.5 us  [run_grad(): pl.pallas_call(functools.partial(grad_kernel, chips), out_shape=[jax.Shap...]
    pallas_call x1, Pallas kernels: 14.1 us -> 12.4 us  [run_attend(): pl.pallas_call(functools.partial(attend_kernel, cells, ctx), grid=(1,), o...]
    pallas_call x1, Pallas kernels: 2.32 us -> 1.04 us  [run_place(): pl.pallas_call(place_kernel, grid=(1,), out_shape=jax.ShapeDtypeStruct(sh...]
    pallas_call x1, Pallas kernels: 8.29 us -> 7.09 us  [run_conv(): pl.pallas_call(functools.partial(conv_kernel, cells), out_shape=[jax.Shap...]
    unnamed x52 -> x14, local copies, waits for them, and re-layouts: 2.41 us -> 1.5 us
    ppermute x30 -> x28, starting transfers between devices: 21.8 us -> 21.6 us  [flip(): return lax.ppermute(value, axis, [(i, i ^ bits) for i in range(size)])]
  transfers between devices with their start and end apart: 30 -> 28, of which waited for: 9 -> 9; matrix products, arithmetic and copies ran while one was open for 3% -> 1% of each run, Pallas kernels for 38% -> 41%
where the time goes in v3:
time: 75.4 us; the launch traced here: 75.1 us
  Pallas kernels  33 us (44%)
  starting transfers between devices  21.6 us (29%)
  waiting for transfers between devices  17.2 us (23%)
  local copies, waits for them, and re-layouts  1.5 us (2%)
  other arithmetic  0.99 us (1%)
  between operations  0.8 us (1%)
    ppermute x28, starting transfers between devices, flip(): return lax.ppermute(value, axis, [(i, i ^ bits) for i in range(size)])  21.6 us
    ppermute x28, waiting for transfers between devices, flip(): return lax.ppermute(value, axis, [(i, i ^ bits) for i in range(size)])  17.2 us
    pallas_call x1, Pallas kernels, run_attend(): pl.pallas_call(functools.partial(attend_kernel, cells, ctx), grid=(1,), o...  12.4 us
    pallas_call x1, Pallas kernels, run_grad(): pl.pallas_call(functools.partial(grad_kernel, chips), out_shape=[jax.Shap...  11.5 us
    pallas_call x1, Pallas kernels, run_conv(): pl.pallas_call(functools.partial(conv_kernel, cells), out_shape=[jax.Shap...  7.09 us
  transfers between devices with their start and end apart: 28, of which 9 were waited for; matrix products, arithmetic and copies ran while one was open for 1% of the time, Pallas kernels for 41%

profile of v3, /device:TPU:0, one launch (start us, length us, event | category | flops | bytes accessed | tf_op | source)
XLA Modules:
  0.0 75.1 jit_solution(16098875331166167513)
XLA Ops:
  0.6 1.0 %cut_tails.1.refs_0_ = bf16[4,2,8,16,128]{4,3,2,1,0:T(8,128)(2,1)S(1)} custom-call(bf16[4,8,8,16,128]{4,3,2,1,0:T(8,128)(2,1)} %bitcast.1.x_ref.xs_ref), custom_call_target="tpu_custom_call" | custom-call | bytes 500000 | tf_op jit(solution)/shard_map/cut_tails/pallas_call | solution.py:177
  1.6 4.0 %collective-permute-start.8 = (bf16[4,2,8,16,128]{4,3,2,1,0:T(8,128)(2,1)S(1)}, bf16[4,2,8,16,128]{4,3,2,1,0:T(8,128)(2,1)S(1)}, u32[]{:S(2)}, u32[]{:S(2)}) collective-permute-start(bf16[4,2,8,16,128]{4,3,2,1,0:T(8,128)(2,1)S(1)} %cut_tails.1.refs_0_), channel_id=1, source_target_pairs={{0,6},{1,7},{2,4},{3,5},{4,2},{5,3},{6,0},{7,1},{8,14},{9,15},{10,... | collective-permute-start | bytes 786440 | tf_op jit(solution)/shard_map/ppermute | solution.py:443
  5.6 0.5 collective-permute-start.7
  6.2 0.5 collective-permute-start.5
  6.7 1.5 %copy-done.3 = bf16[3456,256]{1,0:T(8,128)(2,1)S(1)} copy-done((bf16[3456,256]{1,0:T(8,128)(2,1)S(1)}, bf16[3456,256]{1,0:T(8,128)(2,1)}, u32[]{:S(2)}) %copy-start.3) | copy-done | bytes 1769496
  8.2 7.1 %conv_forward.1 = (bf16[2,320,256]{2,1,0:T(8,128)(2,1)S(1)}, bf16[2,320,256]{2,1,0:T(8,128)(2,1)S(1)}, bf16[2,320,256]{2,1,0:T(8,128)(2,1)S(1)}, bf16[2,320,256]{2,1,0:T(8,128)(2,1)S(1)}) custom-call(s32[1]{0:T(128)} %bitcast.me_ref, bf16[4,8,8,16,128]{4,3,2,1,0:T(8,128)(2,1)} %bitcast.1.x_ref.xs_ref, bf16[3456,256]{1,0:T(8,128)(2,1)S(1)} %copy-done.3), custom_call_target="tpu_custom_call" | custom-call | flops 4800000000 | bytes 4000000 | tf_op jit(solution)/shard_map/conv_forward/pallas_call | solution.py:150
  15.3 2.2 %collective-permute-done.7.refs_4_ = bf16[4,2,8,16,128]{4,3,2,1,0:T(8,128)(2,1)S(1)} collective-permute-done((bf16[4,2,8,16,128]{4,3,2,1,0:T(8,128)(2,1)S(1)}, bf16[4,2,8,16,128]{4,3,2,1,0:T(8,128)(2,1)S(1)}, u32[]{:S(2)}, u32[]{:S(2)}) %collective-permute-start.7) | collective-permute-done | bytes 262176 | tf_op jit(solution)/shard_map/ppermute | solution.py:443
  17.5 0.3 collective-permute-done.6.refs_2_
  17.8 0.5 collective-permute-start.10
  18.3 1.0 %collective-permute-done.9.refs_1_ = bf16[4,2,8,16,128]{4,3,2,1,0:T(8,128)(2,1)S(1)} collective-permute-done((bf16[4,2,8,16,128]{4,3,2,1,0:T(8,128)(2,1)S(1)}, bf16[4,2,8,16,128]{4,3,2,1,0:T(8,128)(2,1)S(1)}, u32[]{:S(2)}, u32[]{:S(2)}) %collective-permute-start.9) | collective-permute-done | bytes 262176 | tf_op jit(solution)/shard_map/ppermute | solution.py:443
  19.7 1.5 %collective-permute-start.1 = (bf16[2,320,256]{2,1,0:T(8,128)(2,1)S(1)}, bf16[2,320,256]{2,1,0:T(8,128)(2,1)S(1)}, u32[]{:S(2)}, u32[]{:S(2)}) collective-permute-start(bf16[2,320,256]{2,1,0:T(8,128)(2,1)S(1)} %get-tuple-element.25), channel_id=1, source_target_pairs={{0,2},{1,3},{2,0},{3,1},{4,6},{5,7},{6,4},{7,5},{8,10},{9,11},{10,... | collective-permute-start | bytes 983048 | tf_op jit(solution)/shard_map/ppermute | solution.py:443
  21.2 0.6 collective-permute-start.2
  21.8 1.5 %collective-permute-start.3 = (bf16[2,320,256]{2,1,0:T(8,128)(2,1)S(1)}, bf16[2,320,256]{2,1,0:T(8,128)(2,1)S(1)}, u32[]{:S(2)}, u32[]{:S(2)}) collective-permute-start(bf16[2,320,256]{2,1,0:T(8,128)(2,1)S(1)} %get-tuple-element.27), channel_id=1, source_target_pairs={{0,6},{1,7},{2,4},{3,5},{4,2},{5,3},{6,0},{7,1},{8,14},{9,15},{10,... | collective-permute-start | bytes 983048 | tf_op jit(solution)/shard_map/ppermute | solution.py:443
  23.3 11.5 %conv_gradient.1 = (f32[432,256]{1,0:T(8,128)S(1)}, bf16[432,256]{1,0:T(8,128)(2,1)S(1)}, bf16[432,256]{1,0:T(8,128)(2,1)S(1)}, bf16[432,256]{1,0:T(8,128)(2,1)S(1)}) custom-call(s32[32]{0:T(128)S(1)} %copy-done.1, s32[4]{0:T(128)S(1)} %copy-done.2, s32[1]{0:T(128)} %bitcast.me_ref, bf16[4,8,8,16,128]{4,3,2,1,0:T(8,128)(2,1)} %bitcast.1.x_ref.xs_ref, ...), custom_call_target="tpu_custom_call" | custom-call | flops 1000 | bytes 1000 | tf_op jit(solution)/shard_map/conv_gradient/pallas_call | solution.py:257
  34.8 2.9 %collective-permute-done.2.refs_4_ = bf16[2,320,256]{2,1,0:T(8,128)(2,1)S(1)} collective-permute-done((bf16[2,320,256]{2,1,0:T(8,128)(2,1)S(1)}, bf16[2,320,256]{2,1,0:T(8,128)(2,1)S(1)}, u32[]{:S(2)}, u32[]{:S(2)}) %collective-permute-start.2) | collective-permute-done | bytes 327712 | tf_op jit(solution)/shard_map/ppermute | solution.py:443
  37.7 0.5 collective-permute-start.14
  38.2 0.6 collective-permute-start.23
  38.9 1.3 %collective-permute-start.24 = (bf16[432,256]{1,0:T(8,128)(2,1)S(1)}, bf16[432,256]{1,0:T(8,128)(2,1)S(1)}, u32[]{:S(2)}, u32[]{:S(2)}) collective-permute-start(bf16[432,256]{1,0:T(8,128)(2,1)S(1)} %get-tuple-element.33), channel_id=1, source_target_pairs={{0,4},{1,5},{2,6},{3,7},{4,0},{5,1},{6,2},{7,3},{8,12},{9,13},{10,... | collective-permute-start | bytes 663560 | tf_op jit(solution)/shard_map/ppermute | solution.py:443
  40.2 1.5 %collective-permute-start.25 = (bf16[432,256]{1,0:T(8,128)(2,1)S(1)}, bf16[432,256]{1,0:T(8,128)(2,1)S(1)}, u32[]{:S(2)}, u32[]{:S(2)}) collective-permute-start(bf16[432,256]{1,0:T(8,128)(2,1)S(1)} %get-tuple-element.34), channel_id=1, source_target_pairs={{0,6},{1,7},{2,4},{3,5},{4,2},{5,3},{6,0},{7,1},{8,14},{9,15},{10,... | collective-permute-start | bytes 663560 | tf_op jit(solution)/shard_map/ppermute | solution.py:443
  41.7 12.4 %attend.1 = (bf16[2,256,256]{2,1,0:T(8,128)(2,1)S(1)}, bf16[2,256,256]{2,1,0:T(8,128)(2,1)S(1)}, bf16[2,256,256]{2,1,0:T(8,128)(2,1)S(1)}, bf16[2,256,256]{2,1,0:T(8,128)(2,1)S(1)}) custom-call(s32[32]{0:T(128)S(1)} %copy-done.1, s32[4]{0:T(128)S(1)} %copy-done.2, f32[4]{0:T(128)S(1)} %copy-done.6, s32[1]{0:T(128)} %bitcast.me_ref, ...), custom_call_target="tpu_custom_call" | custom-call | flops 3000000000 | bytes 4000000 | tf_op jit(solution)/shard_map/attend/pallas_call | solution.py:395
  54.3 1.6 %collective-permute-start.26 = (bf16[432,256]{1,0:T(8,128)(2,1)S(1)}, bf16[432,256]{1,0:T(8,128)(2,1)S(1)}, u32[]{:S(2)}, u32[]{:S(2)}) collective-permute-start(bf16[432,256]{1,0:T(8,128)(2,1)S(1)} %add_convert_fusion.1), channel_id=1, source_target_pairs={{0,8},{8,0},{16,24},{24,16},{1,9},{9,1},{17,25},{25,17},{2,10},{10... | collective-permute-start | bytes 663560 | tf_op jit(solution)/shard_map/ppermute | solution.py:443
  56.0 0.6 collective-permute-start.17
  56.6 1.3 %collective-permute-start.19 = (bf16[2,256,256]{2,1,0:T(8,128)(2,1)S(1)}, bf16[2,256,256]{2,1,0:T(8,128)(2,1)S(1)}, u32[]{:S(2)}, u32[]{:S(2)}) collective-permute-start(bf16[2,256,256]{2,1,0:T(8,128)(2,1)S(1)} %get-tuple-element.40), channel_id=1, source_target_pairs={{0,4},{1,5},{2,6},{3,7},{4,0},{5,1},{6,2},{7,3},{8,12},{9,13},{10,... | collective-permute-start | bytes 786440 | tf_op jit(solution)/shard_map/ppermute | solution.py:443
  57.9 1.5 %collective-permute-start.21 = (bf16[2,256,256]{2,1,0:T(8,128)(2,1)S(1)}, bf16[2,256,256]{2,1,0:T(8,128)(2,1)S(1)}, u32[]{:S(2)}, u32[]{:S(2)}) collective-permute-start(bf16[2,256,256]{2,1,0:T(8,128)(2,1)S(1)} %get-tuple-element.41), channel_id=1, source_target_pairs={{0,6},{1,7},{2,4},{3,5},{4,2},{5,3},{6,0},{7,1},{8,14},{9,15},{10,... | collective-permute-start | bytes 786440 | tf_op jit(solution)/shard_map/ppermute | solution.py:443
  59.4 1.9 %collective-permute-done.26 = bf16[432,256]{1,0:T(8,128)(2,1)S(1)} collective-permute-done((bf16[432,256]{1,0:T(8,128)(2,1)S(1)}, bf16[432,256]{1,0:T(8,128)(2,1)S(1)}, u32[]{:S(2)}, u32[]{:S(2)}) %collective-permute-start.26) | collective-permute-done | bytes 221216 | tf_op jit(solution)/shard_map/ppermute | solution.py:443
  61.4 2.7 %collective-permute-start.27 = (bf16[432,256]{1,0:T(8,128)(2,1)S(1)}, bf16[432,256]{1,0:T(8,128)(2,1)S(1)}, u32[]{:S(2)}, u32[]{:S(2)}) collective-permute-start(bf16[432,256]{1,0:T(8,128)(2,1)S(1)} %add_convert_fusion), channel_id=1, source_target_pairs={{0,16},{8,24},{16,0},{24,8},{1,17},{9,25},{17,1},{25,9},{2,18},{10... | collective-permute-start | bytes 663560 | tf_op jit(solution)/shard_map/ppermute | solution.py:443
  64.1 1.1 %collective-permute-done.17 = bf16[2,256,256]{2,1,0:T(8,128)(2,1)S(1)} collective-permute-done((bf16[2,256,256]{2,1,0:T(8,128)(2,1)S(1)}, bf16[2,256,256]{2,1,0:T(8,128)(2,1)S(1)}, u32[]{:S(2)}, u32[]{:S(2)}) %collective-permute-start.17) | collective-permute-done | bytes 262176 | tf_op jit(solution)/shard_map/ppermute | solution.py:443
  65.2 4.3 %collective-permute-done.19 = bf16[2,256,256]{2,1,0:T(8,128)(2,1)S(1)} collective-permute-done((bf16[2,256,256]{2,1,0:T(8,128)(2,1)S(1)}, bf16[2,256,256]{2,1,0:T(8,128)(2,1)S(1)}, u32[]{:S(2)}, u32[]{:S(2)}) %collective-permute-start.19) | collective-permute-done | bytes 262176 | tf_op jit(solution)/shard_map/ppermute | solution.py:443
  69.5 0.5 collective-permute-start.22
  70.1 3.2 %collective-permute-done.27 = bf16[432,256]{1,0:T(8,128)(2,1)S(1)} collective-permute-done((bf16[432,256]{1,0:T(8,128)(2,1)S(1)}, bf16[432,256]{1,0:T(8,128)(2,1)S(1)}, u32[]{:S(2)}, u32[]{:S(2)}) %collective-permute-start.27) | collective-permute-done | bytes 221216 | tf_op jit(solution)/shard_map/ppermute | solution.py:443
  73.3 0.8 %convert_add_fusion = f32[432,256]{1,0:T(8,128)} fusion(bf16[432,256]{1,0:T(8,128)(2,1)S(1)} %collective-permute-done.27, bf16[432,256]{1,0:T(8,128)(2,1)S(1)} %add_convert_fusion), kind=kLoop, calls=%fused_computation | loop fusion | flops 331776 | bytes 884736 | tf_op jit(solution)/shard_map/add | solution.py:490
  74.1 1.0 %place_latents.1 = bf16[16,8,16,256]{3,2,1,0:T(8,128)(2,1)} custom-call(s32[1]{0:T(128)} %bitcast.me_ref, bf16[2,16,16,256]{3,2,1,0:T(8,128)(2,1)S(1)} %bitcast.14, bf16[2,16,16,256]{3,2,1,0:T(8,128)(2,1)S(1)} %bitcast.18, bf16[2,16,16,256]{3,2,1,0:T(8,128)(2,1)S(1)} %bitcast.15, bf16[2,16,16,256]{3,2,1,0:T(8,128)(2,1)S(1)} %bitcast.19, ...), custom_call_target="tpu_custom_call" | custom-call | bytes 2000000 | tf_op jit(solution)/shard_map/place_latents/pallas_call | solution.py:430
  (46 shorter events, 0.8 us)
Async XLA Ops:
  1.6 13.7 %collective-permute-start.8 = (bf16[4,2,8,16,128]{4,3,2,1,0:T(8,128)(2,1)S(1)}, bf16[4,2,8,16,128]{4,3,2,1,0:T(8,128)(2,1)S(1)}, u32[]{:S(2)}, u32[]{:S(2)}) collective-permute-start(bf16[4,2,8,16,128]{4,3,2,1,0:T(8,128)(2,1)S(1)} %cut_tails.1.refs_0_), channel_id=1, source_target_pairs={{0,6},{1,7},{2,4},{3,5},{4,2},{5,3},{6,0},{7,1},{8,14},{9,15},{10,... | collective-permute-start | bytes 786440 | tf_op jit(solution)/shard_map/ppermute | solution.py:443
  5.6 11.9 %collective-permute-start.7 = (bf16[4,2,8,16,128]{4,3,2,1,0:T(8,128)(2,1)S(1)}, bf16[4,2,8,16,128]{4,3,2,1,0:T(8,128)(2,1)S(1)}, u32[]{:S(2)}, u32[]{:S(2)}) collective-permute-start(bf16[4,2,8,16,128]{4,3,2,1,0:T(8,128)(2,1)S(1)} %cut_tails.1.refs_0_), channel_id=1, source_target_pairs={{0,4},{1,5},{2,6},{3,7},{4,0},{5,1},{6,2},{7,3},{8,12},{9,13},{10,... | collective-permute-start | bytes 786440 | tf_op jit(solution)/shard_map/ppermute | solution.py:443
  6.1 11.7 %collective-permute-start.6 = (bf16[4,2,8,16,128]{4,3,2,1,0:T(8,128)(2,1)S(1)}, bf16[4,2,8,16,128]{4,3,2,1,0:T(8,128)(2,1)S(1)}, u32[]{:S(2)}, u32[]{:S(2)}) collective-permute-start(bf16[4,2,8,16,128]{4,3,2,1,0:T(8,128)(2,1)S(1)} %cut_tails.1.refs_0_), channel_id=1, source_target_pairs={{0,2},{1,3},{2,0},{3,1},{4,6},{5,7},{6,4},{7,5},{8,10},{9,11},{10,... | collective-permute-start | bytes 786440 | tf_op jit(solution)/shard_map/ppermute | solution.py:443
  6.2 17.1 %collective-permute-start.4 = (bf16[4,8,8,16,128]{4,3,2,1,0:T(8,128)(2,1)}, bf16[4,8,8,16,128]{4,3,2,1,0:T(8,128)(2,1)S(1)}, u32[]{:S(2)}, u32[]{:S(2)}) collective-permute-start(bf16[4,8,8,16,128]{4,3,2,1,0:T(8,128)(2,1)} %bitcast.1.x_ref.xs_ref), channel_id=1, source_target_pairs={{0,1},{1,0},{2,3},{3,2},{4,5},{5,4},{6,7},{7,6},{8,9},{9,8},{10,11... | collective-permute-start | bytes 3145736 | tf_op jit(solution)/shard_map/ppermute | solution.py:443
  6.2 17.1 %collective-permute-start.5 = (bf16[4,4,128,256]{3,2,1,0:T(8,128)(2,1)}, bf16[4,4,128,256]{3,2,1,0:T(8,128)(2,1)S(1)}, u32[]{:S(2)}, u32[]{:S(2)}) collective-permute-start(bf16[4,4,128,256]{3,2,1,0:T(8,128)(2,1)} %bitcast.12), channel_id=1, source_target_pairs={{0,1},{1,0},{2,3},{3,2},{4,5},{5,4},{6,7},{7,6},{8,9},{9,8},{10,11... | collective-permute-start | bytes 3145736 | tf_op jit(solution)/shard_map/ppermute | solution.py:443
  8.2 15.1 %copy-start.2 = (s32[4]{0:T(128)S(1)}, s32[4]{0:T(128)}, u32[]{:S(2)}) copy-start(s32[4]{0:T(128)} %counts.3) | copy-start | bytes 52
  17.8 1.5 %collective-permute-start.9 = (bf16[4,2,8,16,128]{4,3,2,1,0:T(8,128)(2,1)S(1)}, bf16[4,2,8,16,128]{4,3,2,1,0:T(8,128)(2,1)S(1)}, u32[]{:S(2)}, u32[]{:S(2)}) collective-permute-start(bf16[4,2,8,16,128]{4,3,2,1,0:T(8,128)(2,1)S(1)} %cut_tails.1.refs_0_), channel_id=1, source_target_pairs={{0,1},{1,0},{2,3},{3,2},{4,5},{5,4},{6,7},{7,6},{8,9},{9,8},{10,11... | collective-permute-start | bytes 786440 | tf_op jit(solution)/shard_map/ppermute | solution.py:443
  17.8 1.9 %collective-permute-start.10 = (bf16[4,2,8,16,128]{4,3,2,1,0:T(8,128)(2,1)S(1)}, bf16[4,2,8,16,128]{4,3,2,1,0:T(8,128)(2,1)S(1)}, u32[]{:S(2)}, u32[]{:S(2)}) collective-permute-start(bf16[4,2,8,16,128]{4,3,2,1,0:T(8,128)(2,1)S(1)} %collective-permute-done.6.refs_2_), channel_id=1, source_target_pairs={{0,1},{1,0},{2,3},{3,2},{4,5},{5,4},{6,7},{7,6},{8,9},{9,8},{10,11... | collective-permute-start | bytes 786440 | tf_op jit(solution)/shard_map/ppermute | solution.py:443
  18.3 2.9 %collective-permute-start.11 = (bf16[4,2,8,16,128]{4,3,2,1,0:T(8,128)(2,1)S(1)}, bf16[4,2,8,16,128]{4,3,2,1,0:T(8,128)(2,1)S(1)}, u32[]{:S(2)}, u32[]{:S(2)}) collective-permute-start(bf16[4,2,8,16,128]{4,3,2,1,0:T(8,128)(2,1)S(1)} %collective-permute-done.7.refs_4_), channel_id=1, source_target_pairs={{0,1},{1,0},{2,3},{3,2},{4,5},{5,4},{6,7},{7,6},{8,9},{9,8},{10,11... | collective-permute-start | bytes 786440 | tf_op jit(solution)/shard_map/ppermute | solution.py:443
  19.3 2.5 %collective-permute-start.12 = (bf16[4,2,8,16,128]{4,3,2,1,0:T(8,128)(2,1)S(1)}, bf16[4,2,8,16,128]{4,3,2,1,0:T(8,128)(2,1)S(1)}, u32[]{:S(2)}, u32[]{:S(2)}) collective-permute-start(bf16[4,2,8,16,128]{4,3,2,1,0:T(8,128)(2,1)S(1)} %collective-permute-done.8.refs_6_), channel_id=1, source_target_pairs={{0,1},{1,0},{2,3},{3,2},{4,5},{5,4},{6,7},{7,6},{8,9},{9,8},{10,11... | collective-permute-start | bytes 786440 | tf_op jit(solution)/shard_map/ppermute | solution.py:443
  19.7 15.1 %collective-permute-start.1 = (bf16[2,320,256]{2,1,0:T(8,128)(2,1)S(1)}, bf16[2,320,256]{2,1,0:T(8,128)(2,1)S(1)}, u32[]{:S(2)}, u32[]{:S(2)}) collective-permute-start(bf16[2,320,256]{2,1,0:T(8,128)(2,1)S(1)} %get-tuple-element.25), channel_id=1, source_target_pairs={{0,2},{1,3},{2,0},{3,1},{4,6},{5,7},{6,4},{7,5},{8,10},{9,11},{10,... | collective-permute-start | bytes 983048 | tf_op jit(solution)/shard_map/ppermute | solution.py:443
  21.2 16.5 %collective-permute-start.2 = (bf16[2,320,256]{2,1,0:T(8,128)(2,1)S(1)}, bf16[2,320,256]{2,1,0:T(8,128)(2,1)S(1)}, u32[]{:S(2)}, u32[]{:S(2)}) collective-permute-start(bf16[2,320,256]{2,1,0:T(8,128)(2,1)S(1)} %get-tuple-element.26), channel_id=1, source_target_pairs={{0,4},{1,5},{2,6},{3,7},{4,0},{5,1},{6,2},{7,3},{8,12},{9,13},{10,... | collective-permute-start | bytes 983048 | tf_op jit(solution)/shard_map/ppermute | solution.py:443
  21.8 19.9 %copy-start.4 = (bf16[256,768]{1,0:T(8,128)(2,1)S(1)}, bf16[256,768]{1,0:T(8,128)(2,1)}, u32[]{:S(2)}) copy-start(bf16[256,768]{1,0:T(8,128)(2,1)} %qkv_ref.1) | copy-start | bytes 1179652
  21.8 19.9 %copy-start.5 = (bf16[256,256]{1,0:T(8,128)(2,1)S(1)}, bf16[256,256]{1,0:T(8,128)(2,1)}, u32[]{:S(2)}) copy-start(bf16[256,256]{1,0:T(8,128)(2,1)} %last_ref.1) | copy-start | bytes 393220
  21.8 19.9 %copy-start.6 = (f32[4]{0:T(128)S(1)}, f32[4]{0:T(128)}, u32[]{:S(2)}) copy-start(f32[4]{0:T(128)} %scale.1) | copy-start | bytes 52
  21.8 15.9 %collective-permute-start.3 = (bf16[2,320,256]{2,1,0:T(8,128)(2,1)S(1)}, bf16[2,320,256]{2,1,0:T(8,128)(2,1)S(1)}, u32[]{:S(2)}, u32[]{:S(2)}) collective-permute-start(bf16[2,320,256]{2,1,0:T(8,128)(2,1)S(1)} %get-tuple-element.27), channel_id=1, source_target_pairs={{0,6},{1,7},{2,4},{3,5},{4,2},{5,3},{6,0},{7,1},{8,14},{9,15},{10,... | collective-permute-start | bytes 983048 | tf_op jit(solution)/shard_map/ppermute | solution.py:443
  23.3 15.6 %collective-permute-start = (bf16[2,320,256]{2,1,0:T(8,128)(2,1)S(1)}, bf16[2,320,256]{2,1,0:T(8,128)(2,1)S(1)}, u32[]{:S(2)}, u32[]{:S(2)}) collective-permute-start(bf16[2,320,256]{2,1,0:T(8,128)(2,1)S(1)} %get-tuple-element.24.refs_0_), channel_id=1, source_target_pairs={{0,1},{1,0},{2,3},{3,2},{4,5},{5,4},{6,7},{7,6},{8,9},{9,8},{10,11... | collective-permute-start | bytes 983048 | tf_op jit(solution)/shard_map/ppermute | solution.py:443
  37.7 2.5 %collective-permute-start.13 = (bf16[2,320,256]{2,1,0:T(8,128)(2,1)S(1)}, bf16[2,320,256]{2,1,0:T(8,128)(2,1)S(1)}, u32[]{:S(2)}, u32[]{:S(2)}) collective-permute-start(bf16[2,320,256]{2,1,0:T(8,128)(2,1)S(1)} %collective-permute-done.1.refs_2_), channel_id=1, source_target_pairs={{0,1},{1,0},{2,3},{3,2},{4,5},{5,4},{6,7},{7,6},{8,9},{9,8},{10,11... | collective-permute-start | bytes 983048 | tf_op jit(solution)/shard_map/ppermute | solution.py:443
  37.7 4.0 %collective-permute-start.14 = (bf16[2,320,256]{2,1,0:T(8,128)(2,1)S(1)}, bf16[2,320,256]{2,1,0:T(8,128)(2,1)S(1)}, u32[]{:S(2)}, u32[]{:S(2)}) collective-permute-start(bf16[2,320,256]{2,1,0:T(8,128)(2,1)S(1)} %collective-permute-done.2.refs_4_), channel_id=1, source_target_pairs={{0,1},{1,0},{2,3},{3,2},{4,5},{5,4},{6,7},{7,6},{8,9},{9,8},{10,11... | collective-permute-start | bytes 983048 | tf_op jit(solution)/shard_map/ppermute | solution.py:443
  38.2 3.5 %collective-permute-start.15 = (bf16[2,320,256]{2,1,0:T(8,128)(2,1)S(1)}, bf16[2,320,256]{2,1,0:T(8,128)(2,1)S(1)}, u32[]{:S(2)}, u32[]{:S(2)}) collective-permute-start(bf16[2,320,256]{2,1,0:T(8,128)(2,1)S(1)} %collective-permute-done.3.refs_6_), channel_id=1, source_target_pairs={{0,1},{1,0},{2,3},{3,2},{4,5},{5,4},{6,7},{7,6},{8,9},{9,8},{10,11... | collective-permute-start | bytes 983048 | tf_op jit(solution)/shard_map/ppermute | solution.py:443
  38.2 16.0 %collective-permute-start.23 = (bf16[432,256]{1,0:T(8,128)(2,1)S(1)}, bf16[432,256]{1,0:T(8,128)(2,1)S(1)}, u32[]{:S(2)}, u32[]{:S(2)}) collective-permute-start(bf16[432,256]{1,0:T(8,128)(2,1)S(1)} %get-tuple-element.32), channel_id=1, source_target_pairs={{0,2},{1,3},{2,0},{3,1},{4,6},{5,7},{6,4},{7,5},{8,10},{9,11},{10,... | collective-permute-start | bytes 663560 | tf_op jit(solution)/shard_map/ppermute | solution.py:443
  38.9 15.3 %collective-permute-start.24 = (bf16[432,256]{1,0:T(8,128)(2,1)S(1)}, bf16[432,256]{1,0:T(8,128)(2,1)S(1)}, u32[]{:S(2)}, u32[]{:S(2)}) collective-permute-start(bf16[432,256]{1,0:T(8,128)(2,1)S(1)} %get-tuple-element.33), channel_id=1, source_target_pairs={{0,4},{1,5},{2,6},{3,7},{4,0},{5,1},{6,2},{7,3},{8,12},{9,13},{10,... | collective-permute-start | bytes 663560 | tf_op jit(solution)/shard_map/ppermute | solution.py:443
  40.2 14.0 %collective-permute-start.25 = (bf16[432,256]{1,0:T(8,128)(2,1)S(1)}, bf16[432,256]{1,0:T(8,128)(2,1)S(1)}, u32[]{:S(2)}, u32[]{:S(2)}) collective-permute-start(bf16[432,256]{1,0:T(8,128)(2,1)S(1)} %get-tuple-element.34), channel_id=1, source_target_pairs={{0,6},{1,7},{2,4},{3,5},{4,2},{5,3},{6,0},{7,1},{8,14},{9,15},{10,... | collective-permute-start | bytes 663560 | tf_op jit(solution)/shard_map/ppermute | solution.py:443
  54.3 7.1 %collective-permute-start.26 = (bf16[432,256]{1,0:T(8,128)(2,1)S(1)}, bf16[432,256]{1,0:T(8,128)(2,1)S(1)}, u32[]{:S(2)}, u32[]{:S(2)}) collective-permute-start(bf16[432,256]{1,0:T(8,128)(2,1)S(1)} %add_convert_fusion.1), channel_id=1, source_target_pairs={{0,8},{8,0},{16,24},{24,16},{1,9},{9,1},{17,25},{25,17},{2,10},{10... | collective-permute-start | bytes 663560 | tf_op jit(solution)/shard_map/ppermute | solution.py:443
  56.0 9.2 %collective-permute-start.17 = (bf16[2,256,256]{2,1,0:T(8,128)(2,1)S(1)}, bf16[2,256,256]{2,1,0:T(8,128)(2,1)S(1)}, u32[]{:S(2)}, u32[]{:S(2)}) collective-permute-start(bf16[2,256,256]{2,1,0:T(8,128)(2,1)S(1)} %get-tuple-element.39), channel_id=1, source_target_pairs={{0,2},{1,3},{2,0},{3,1},{4,6},{5,7},{6,4},{7,5},{8,10},{9,11},{10,... | collective-permute-start | bytes 786440 | tf_op jit(solution)/shard_map/ppermute | solution.py:443
  56.6 12.9 %collective-permute-start.19 = (bf16[2,256,256]{2,1,0:T(8,128)(2,1)S(1)}, bf16[2,256,256]{2,1,0:T(8,128)(2,1)S(1)}, u32[]{:S(2)}, u32[]{:S(2)}) collective-permute-start(bf16[2,256,256]{2,1,0:T(8,128)(2,1)S(1)} %get-tuple-element.40), channel_id=1, source_target_pairs={{0,4},{1,5},{2,6},{3,7},{4,0},{5,1},{6,2},{7,3},{8,12},{9,13},{10,... | collective-permute-start | bytes 786440 | tf_op jit(solution)/shard_map/ppermute | solution.py:443
  57.9 11.6 %collective-permute-start.21 = (bf16[2,256,256]{2,1,0:T(8,128)(2,1)S(1)}, bf16[2,256,256]{2,1,0:T(8,128)(2,1)S(1)}, u32[]{:S(2)}, u32[]{:S(2)}) collective-permute-start(bf16[2,256,256]{2,1,0:T(8,128)(2,1)S(1)} %get-tuple-element.41), channel_id=1, source_target_pairs={{0,6},{1,7},{2,4},{3,5},{4,2},{5,3},{6,0},{7,1},{8,14},{9,15},{10,... | collective-permute-start | bytes 786440 | tf_op jit(solution)/shard_map/ppermute | solution.py:443
  61.4 11.8 %collective-permute-start.27 = (bf16[432,256]{1,0:T(8,128)(2,1)S(1)}, bf16[432,256]{1,0:T(8,128)(2,1)S(1)}, u32[]{:S(2)}, u32[]{:S(2)}) collective-permute-start(bf16[432,256]{1,0:T(8,128)(2,1)S(1)} %add_convert_fusion), channel_id=1, source_target_pairs={{0,16},{8,24},{16,0},{24,8},{1,17},{9,25},{17,1},{25,9},{2,18},{10... | collective-permute-start | bytes 663560 | tf_op jit(solution)/shard_map/ppermute | solution.py:443
  64.1 10.0 %collective-permute-start.16 = (bf16[2,256,256]{2,1,0:T(8,128)(2,1)S(1)}, bf16[2,256,256]{2,1,0:T(8,128)(2,1)S(1)}, u32[]{:S(2)}, u32[]{:S(2)}) collective-permute-start(bf16[2,256,256]{2,1,0:T(8,128)(2,1)S(1)} %get-tuple-element.38), channel_id=1, source_target_pairs={{0,1},{1,0},{2,3},{3,2},{4,5},{5,4},{6,7},{7,6},{8,9},{9,8},{10,11... | collective-permute-start | bytes 786440 | tf_op jit(solution)/shard_map/ppermute | solution.py:443
  65.2 8.9 %collective-permute-start.18 = (bf16[2,256,256]{2,1,0:T(8,128)(2,1)S(1)}, bf16[2,256,256]{2,1,0:T(8,128)(2,1)S(1)}, u32[]{:S(2)}, u32[]{:S(2)}) collective-permute-start(bf16[2,256,256]{2,1,0:T(8,128)(2,1)S(1)} %collective-permute-done.17), channel_id=1, source_target_pairs={{0,1},{1,0},{2,3},{3,2},{4,5},{5,4},{6,7},{7,6},{8,9},{9,8},{10,11... | collective-permute-start | bytes 786440 | tf_op jit(solution)/shard_map/ppermute | solution.py:443
  69.5 4.5 %collective-permute-start.20 = (bf16[2,256,256]{2,1,0:T(8,128)(2,1)S(1)}, bf16[2,256,256]{2,1,0:T(8,128)(2,1)S(1)}, u32[]{:S(2)}, u32[]{:S(2)}) collective-permute-start(bf16[2,256,256]{2,1,0:T(8,128)(2,1)S(1)} %collective-permute-done.19), channel_id=1, source_target_pairs={{0,1},{1,0},{2,3},{3,2},{4,5},{5,4},{6,7},{7,6},{8,9},{9,8},{10,11... | collective-permute-start | bytes 786440 | tf_op jit(solution)/shard_map/ppermute | solution.py:443
  69.5 4.5 %collective-permute-start.22 = (bf16[2,256,256]{2,1,0:T(8,128)(2,1)S(1)}, bf16[2,256,256]{2,1,0:T(8,128)(2,1)S(1)}, u32[]{:S(2)}, u32[]{:S(2)}) collective-permute-start(bf16[2,256,256]{2,1,0:T(8,128)(2,1)S(1)} %collective-permute-done.21), channel_id=1, source_target_pairs={{0,1},{1,0},{2,3},{3,2},{4,5},{5,4},{6,7},{7,6},{8,9},{9,8},{10,11... | collective-permute-start | bytes 786440 | tf_op jit(solution)/shard_map/ppermute | solution.py:443
  (3 other events, 31.7 us)

commit v4 on v3

--- a/solution.py
+++ b/solution.py
@@ -161,7 +161,7 @@
             pltpu.VMEM(taps.shape, BF),
             pltpu.SemaphoreType.DMA((2,)),
         ],
-        compiler_params=params(24),
+        compiler_params=params(50),
         cost_estimate=cost(4_800_000_000, 4_000_000),
         name="conv_forward",
     )(me, frames, taps)
@@ -280,6 +280,7 @@
     me = me_ref[0]
     main = cells * FRAMES
     total = ctx * FRAMES
+    block = min(128, total)
     fill_slots(assign, slot_of)
 
     def mark(shape, axis):
@@ -339,11 +340,10 @@
         v_ref[src] = mapped[:, 2 * COUT :].astype(BF).reshape(cells, FRAMES, COUT)
         return carry
 
-    lax.fori_loop(0, ctx, project, 0)
+    lax.fori_loop(0, ctx, project, 0, unroll=8 if total == block else 1)
 
     low = iota((1, 128), 1) < 64
     ones = [jnp.where(low, 1.0, 0.0), jnp.where(low, 0.0, 1.0)]
-    block = min(128, total)
 
     def mix(cell, carry):
         for pair in range(2):
@@ -368,7 +368,7 @@
                 q_ref[part, cell, :, lanes] = mixed.reshape(block // FRAMES, FRAMES, 128)
         return carry
 
-    lax.fori_loop(0, cells, mix, 0)
+    lax.fori_loop(0, cells, mix, 0, unroll=8 if total == block else 1)
 
     turn = swap_matrix(cells, FRAMES)
 
@@ -408,7 +408,7 @@
             pltpu.VMEM((total, total), F32),
         ],
         compiler_params=params(24),
-        cost_estimate=cost(3_000_000_000, 4_000_000),
+        cost_estimate=cost(1000, 1000),
         name="attend",
     )(assign, counts, scale, me, qkv, last, *got)
 

time: 75.4 us -> 72 us (0.955)
  Pallas kernels: 33 us -> 27.7 us
  waiting for transfers between devices: 17.2 us -> 20.6 us
  local copies, waits for them, and re-layouts: 1.5 us -> 0.02 us
    pallas_call x1, Pallas kernels: 12.4 us -> 7.09 us  [run_attend(): pl.pallas_call(functools.partial(attend_kernel, cells, ctx), grid=(1,), o...]
    ppermute x28, waiting for transfers between devices: 17.2 us -> 20.6 us  [flip(): return lax.ppermute(value, axis, [(i, i ^ bits) for i in range(size)])]
    unnamed x14 -> x12, local copies, waits for them, and re-layouts: 1.5 us -> 0.02 us
  transfers between devices with their start and end apart: 28 -> 28, of which waited for: 9 -> 10; matrix products, arithmetic and copies ran while one was open for 1% -> 1% of each run, Pallas kernels for 41% -> 36%
where the time goes in v4:
time: 72 us; the launch traced here: 71.8 us
  Pallas kernels  27.7 us (38%)
  starting transfers between devices  21.7 us (30%)
  waiting for transfers between devices  20.6 us (29%)
  other arithmetic  1 us (1%)
  between operations  0.78 us (1%)
    ppermute x28, starting transfers between devices, flip(): return lax.ppermute(value, axis, [(i, i ^ bits) for i in range(size)])  21.7 us
    ppermute x28, waiting for transfers between devices, flip(): return lax.ppermute(value, axis, [(i, i ^ bits) for i in range(size)])  20.6 us
    pallas_call x1, Pallas kernels, run_grad(): pl.pallas_call(functools.partial(grad_kernel, chips), out_shape=[jax.Shap...  11.5 us
    pallas_call x1, Pallas kernels, run_attend(): pl.pallas_call(functools.partial(attend_kernel, cells, ctx), grid=(1,), o...  7.09 us
    pallas_call x1, Pallas kernels, run_conv(): pl.pallas_call(functools.partial(conv_kernel, cells), out_shape=[jax.Shap...  7.07 us
  transfers between devices with their start and end apart: 28, of which 10 were waited for; matrix products, arithmetic and copies ran while one was open for 1% of the time, Pallas kernels for 36%

profile of v4, /device:TPU:0, one launch (start us, length us, event | category | flops | bytes accessed | tf_op | source)
XLA Modules:
  0.0 71.8 jit_solution(2654489101857572552)
XLA Ops:
  0.6 1.0 %cut_tails.1.refs_0_ = bf16[4,2,8,16,128]{4,3,2,1,0:T(8,128)(2,1)S(1)} custom-call(bf16[4,8,8,16,128]{4,3,2,1,0:T(8,128)(2,1)} %bitcast.1.x_ref.xs_ref), custom_call_target="tpu_custom_call" | custom-call | bytes 500000 | tf_op jit(solution)/shard_map/cut_tails/pallas_call | solution.py:177
  1.6 4.0 %collective-permute-start.8 = (bf16[4,2,8,16,128]{4,3,2,1,0:T(8,128)(2,1)S(1)}, bf16[4,2,8,16,128]{4,3,2,1,0:T(8,128)(2,1)S(1)}, u32[]{:S(2)}, u32[]{:S(2)}) collective-permute-start(bf16[4,2,8,16,128]{4,3,2,1,0:T(8,128)(2,1)S(1)} %cut_tails.1.refs_0_), channel_id=1, source_target_pairs={{0,6},{1,7},{2,4},{3,5},{4,2},{5,3},{6,0},{7,1},{8,14},{9,15},{10,... | collective-permute-start | bytes 786440 | tf_op jit(solution)/shard_map/ppermute | solution.py:443
  5.6 0.5 collective-permute-start.7
  6.2 0.5 collective-permute-start.5
  6.7 7.1 %conv_forward.1 = (bf16[2,320,256]{2,1,0:T(8,128)(2,1)S(1)}, bf16[2,320,256]{2,1,0:T(8,128)(2,1)S(1)}, bf16[2,320,256]{2,1,0:T(8,128)(2,1)S(1)}, bf16[2,320,256]{2,1,0:T(8,128)(2,1)S(1)}) custom-call(s32[1]{0:T(128)} %bitcast.me_ref, bf16[4,8,8,16,128]{4,3,2,1,0:T(8,128)(2,1)} %bitcast.1.x_ref.xs_ref, bf16[3456,256]{1,0:T(8,128)(2,1)} %w_ref.1), custom_call_target="tpu_custom_call" | custom-call | flops 4800000000 | bytes 4000000 | tf_op jit(solution)/shard_map/conv_forward/pallas_call | solution.py:150
  13.8 3.7 %collective-permute-done.7.refs_4_ = bf16[4,2,8,16,128]{4,3,2,1,0:T(8,128)(2,1)S(1)} collective-permute-done((bf16[4,2,8,16,128]{4,3,2,1,0:T(8,128)(2,1)S(1)}, bf16[4,2,8,16,128]{4,3,2,1,0:T(8,128)(2,1)S(1)}, u32[]{:S(2)}, u32[]{:S(2)}) %collective-permute-start.7) | collective-permute-done | bytes 262176 | tf_op jit(solution)/shard_map/ppermute | solution.py:443
  17.5 0.3 collective-permute-done.6.refs_2_
  17.8 0.5 collective-permute-start.10
  18.3 1.0 %collective-permute-done.9.refs_1_ = bf16[4,2,8,16,128]{4,3,2,1,0:T(8,128)(2,1)S(1)} collective-permute-done((bf16[4,2,8,16,128]{4,3,2,1,0:T(8,128)(2,1)S(1)}, bf16[4,2,8,16,128]{4,3,2,1,0:T(8,128)(2,1)S(1)}, u32[]{:S(2)}, u32[]{:S(2)}) %collective-permute-start.9) | collective-permute-done | bytes 262176 | tf_op jit(solution)/shard_map/ppermute | solution.py:443
  19.7 1.5 %collective-permute-start.1 = (bf16[2,320,256]{2,1,0:T(8,128)(2,1)S(1)}, bf16[2,320,256]{2,1,0:T(8,128)(2,1)S(1)}, u32[]{:S(2)}, u32[]{:S(2)}) collective-permute-start(bf16[2,320,256]{2,1,0:T(8,128)(2,1)S(1)} %get-tuple-element.25), channel_id=1, source_target_pairs={{0,2},{1,3},{2,0},{3,1},{4,6},{5,7},{6,4},{7,5},{8,10},{9,11},{10,... | collective-permute-start | bytes 983048 | tf_op jit(solution)/shard_map/ppermute | solution.py:443
  21.2 0.6 collective-permute-start.2
  21.8 1.5 %collective-permute-start.3 = (bf16[2,320,256]{2,1,0:T(8,128)(2,1)S(1)}, bf16[2,320,256]{2,1,0:T(8,128)(2,1)S(1)}, u32[]{:S(2)}, u32[]{:S(2)}) collective-permute-start(bf16[2,320,256]{2,1,0:T(8,128)(2,1)S(1)} %get-tuple-element.27), channel_id=1, source_target_pairs={{0,6},{1,7},{2,4},{3,5},{4,2},{5,3},{6,0},{7,1},{8,14},{9,15},{10,... | collective-permute-start | bytes 983048 | tf_op jit(solution)/shard_map/ppermute | solution.py:443
  23.3 11.5 %conv_gradient.1 = (f32[432,256]{1,0:T(8,128)S(1)}, bf16[432,256]{1,0:T(8,128)(2,1)S(1)}, bf16[432,256]{1,0:T(8,128)(2,1)S(1)}, bf16[432,256]{1,0:T(8,128)(2,1)S(1)}) custom-call(s32[32]{0:T(128)S(1)} %copy-done.3, s32[4]{0:T(128)S(1)} %copy-done.4, s32[1]{0:T(128)} %bitcast.me_ref, bf16[4,8,8,16,128]{4,3,2,1,0:T(8,128)(2,1)} %bitcast.1.x_ref.xs_ref, ...), custom_call_target="tpu_custom_call" | custom-call | flops 1000 | bytes 1000 | tf_op jit(solution)/shard_map/conv_gradient/pallas_call | solution.py:257
  34.8 2.9 %collective-permute-done.2.refs_4_ = bf16[2,320,256]{2,1,0:T(8,128)(2,1)S(1)} collective-permute-done((bf16[2,320,256]{2,1,0:T(8,128)(2,1)S(1)}, bf16[2,320,256]{2,1,0:T(8,128)(2,1)S(1)}, u32[]{:S(2)}, u32[]{:S(2)}) %collective-permute-start.2) | collective-permute-done | bytes 327712 | tf_op jit(solution)/shard_map/ppermute | solution.py:443
  37.7 0.5 collective-permute-start.14
  38.2 0.6 collective-permute-start.23
  38.9 1.3 %collective-permute-start.24 = (bf16[432,256]{1,0:T(8,128)(2,1)S(1)}, bf16[432,256]{1,0:T(8,128)(2,1)S(1)}, u32[]{:S(2)}, u32[]{:S(2)}) collective-permute-start(bf16[432,256]{1,0:T(8,128)(2,1)S(1)} %get-tuple-element.33), channel_id=1, source_target_pairs={{0,4},{1,5},{2,6},{3,7},{4,0},{5,1},{6,2},{7,3},{8,12},{9,13},{10,... | collective-permute-start | bytes 663560 | tf_op jit(solution)/shard_map/ppermute | solution.py:443
  40.2 1.5 %collective-permute-start.25 = (bf16[432,256]{1,0:T(8,128)(2,1)S(1)}, bf16[432,256]{1,0:T(8,128)(2,1)S(1)}, u32[]{:S(2)}, u32[]{:S(2)}) collective-permute-start(bf16[432,256]{1,0:T(8,128)(2,1)S(1)} %get-tuple-element.34), channel_id=1, source_target_pairs={{0,6},{1,7},{2,4},{3,5},{4,2},{5,3},{6,0},{7,1},{8,14},{9,15},{10,... | collective-permute-start | bytes 663560 | tf_op jit(solution)/shard_map/ppermute | solution.py:443
  41.7 7.1 %attend.1 = (bf16[2,256,256]{2,1,0:T(8,128)(2,1)S(1)}, bf16[2,256,256]{2,1,0:T(8,128)(2,1)S(1)}, bf16[2,256,256]{2,1,0:T(8,128)(2,1)S(1)}, bf16[2,256,256]{2,1,0:T(8,128)(2,1)S(1)}) custom-call(s32[32]{0:T(128)S(1)} %copy-done.3, s32[4]{0:T(128)S(1)} %copy-done.4, f32[4]{0:T(128)S(1)} %copy-done.5, s32[1]{0:T(128)} %bitcast.me_ref, ...), custom_call_target="tpu_custom_call" | custom-call | flops 1000 | bytes 1000 | tf_op jit(solution)/shard_map/attend/pallas_call | solution.py:395
  48.8 2.3 %collective-permute-done.24 = bf16[432,256]{1,0:T(8,128)(2,1)S(1)} collective-permute-done((bf16[432,256]{1,0:T(8,128)(2,1)S(1)}, bf16[432,256]{1,0:T(8,128)(2,1)S(1)}, u32[]{:S(2)}, u32[]{:S(2)}) %collective-permute-start.24) | collective-permute-done | bytes 221216 | tf_op jit(solution)/shard_map/ppermute | solution.py:443
  51.3 1.6 %collective-permute-start.26 = (bf16[432,256]{1,0:T(8,128)(2,1)S(1)}, bf16[432,256]{1,0:T(8,128)(2,1)S(1)}, u32[]{:S(2)}, u32[]{:S(2)}) collective-permute-start(bf16[432,256]{1,0:T(8,128)(2,1)S(1)} %add_convert_fusion.1), channel_id=1, source_target_pairs={{0,8},{8,0},{16,24},{24,16},{1,9},{9,1},{17,25},{25,17},{2,10},{10... | collective-permute-start | bytes 663560 | tf_op jit(solution)/shard_map/ppermute | solution.py:443
  52.9 1.4 %collective-permute-start.17 = (bf16[2,256,256]{2,1,0:T(8,128)(2,1)S(1)}, bf16[2,256,256]{2,1,0:T(8,128)(2,1)S(1)}, u32[]{:S(2)}, u32[]{:S(2)}) collective-permute-start(bf16[2,256,256]{2,1,0:T(8,128)(2,1)S(1)} %get-tuple-element.39), channel_id=1, source_target_pairs={{0,2},{1,3},{2,0},{3,1},{4,6},{5,7},{6,4},{7,5},{8,10},{9,11},{10,... | collective-permute-start | bytes 786440 | tf_op jit(solution)/shard_map/ppermute | solution.py:443
  54.3 0.7 %collective-permute-start.19 = (bf16[2,256,256]{2,1,0:T(8,128)(2,1)S(1)}, bf16[2,256,256]{2,1,0:T(8,128)(2,1)S(1)}, u32[]{:S(2)}, u32[]{:S(2)}) collective-permute-start(bf16[2,256,256]{2,1,0:T(8,128)(2,1)S(1)} %get-tuple-element.40), channel_id=1, source_target_pairs={{0,4},{1,5},{2,6},{3,7},{4,0},{5,1},{6,2},{7,3},{8,12},{9,13},{10,... | collective-permute-start | bytes 786440 | tf_op jit(solution)/shard_map/ppermute | solution.py:443
  55.0 1.4 %collective-permute-start.21 = (bf16[2,256,256]{2,1,0:T(8,128)(2,1)S(1)}, bf16[2,256,256]{2,1,0:T(8,128)(2,1)S(1)}, u32[]{:S(2)}, u32[]{:S(2)}) collective-permute-start(bf16[2,256,256]{2,1,0:T(8,128)(2,1)S(1)} %get-tuple-element.41), channel_id=1, source_target_pairs={{0,6},{1,7},{2,4},{3,5},{4,2},{5,3},{6,0},{7,1},{8,14},{9,15},{10,... | collective-permute-start | bytes 786440 | tf_op jit(solution)/shard_map/ppermute | solution.py:443
  56.4 1.7 %collective-permute-done.26 = bf16[432,256]{1,0:T(8,128)(2,1)S(1)} collective-permute-done((bf16[432,256]{1,0:T(8,128)(2,1)S(1)}, bf16[432,256]{1,0:T(8,128)(2,1)S(1)}, u32[]{:S(2)}, u32[]{:S(2)}) %collective-permute-start.26) | collective-permute-done | bytes 221216 | tf_op jit(solution)/shard_map/ppermute | solution.py:443
  58.2 2.8 %collective-permute-start.27 = (bf16[432,256]{1,0:T(8,128)(2,1)S(1)}, bf16[432,256]{1,0:T(8,128)(2,1)S(1)}, u32[]{:S(2)}, u32[]{:S(2)}) collective-permute-start(bf16[432,256]{1,0:T(8,128)(2,1)S(1)} %add_convert_fusion), channel_id=1, source_target_pairs={{0,16},{8,24},{16,0},{24,8},{1,17},{9,25},{17,1},{25,9},{2,18},{10... | collective-permute-start | bytes 663560 | tf_op jit(solution)/shard_map/ppermute | solution.py:443
  61.0 1.2 %collective-permute-done.17 = bf16[2,256,256]{2,1,0:T(8,128)(2,1)S(1)} collective-permute-done((bf16[2,256,256]{2,1,0:T(8,128)(2,1)S(1)}, bf16[2,256,256]{2,1,0:T(8,128)(2,1)S(1)}, u32[]{:S(2)}, u32[]{:S(2)}) %collective-permute-start.17) | collective-permute-done | bytes 262176 | tf_op jit(solution)/shard_map/ppermute | solution.py:443
  62.2 4.8 %collective-permute-done.19 = bf16[2,256,256]{2,1,0:T(8,128)(2,1)S(1)} collective-permute-done((bf16[2,256,256]{2,1,0:T(8,128)(2,1)S(1)}, bf16[2,256,256]{2,1,0:T(8,128)(2,1)S(1)}, u32[]{:S(2)}, u32[]{:S(2)}) %collective-permute-start.19) | collective-permute-done | bytes 262176 | tf_op jit(solution)/shard_map/ppermute | solution.py:443
  67.0 0.5 collective-permute-start.22
  67.5 2.4 %collective-permute-done.27 = bf16[432,256]{1,0:T(8,128)(2,1)S(1)} collective-permute-done((bf16[432,256]{1,0:T(8,128)(2,1)S(1)}, bf16[432,256]{1,0:T(8,128)(2,1)S(1)}, u32[]{:S(2)}, u32[]{:S(2)}) %collective-permute-start.27) | collective-permute-done | bytes 221216 | tf_op jit(solution)/shard_map/ppermute | solution.py:443
  69.9 0.8 %convert_add_fusion = f32[432,256]{1,0:T(8,128)} fusion(bf16[432,256]{1,0:T(8,128)(2,1)S(1)} %collective-permute-done.27, bf16[432,256]{1,0:T(8,128)(2,1)S(1)} %add_convert_fusion), kind=kLoop, calls=%fused_computation | loop fusion | flops 331776 | bytes 884736 | tf_op jit(solution)/shard_map/add | solution.py:490
  70.8 1.0 %place_latents.1 = bf16[16,8,16,256]{3,2,1,0:T(8,128)(2,1)} custom-call(s32[1]{0:T(128)} %bitcast.me_ref, bf16[2,16,16,256]{3,2,1,0:T(8,128)(2,1)S(1)} %bitcast.14, bf16[2,16,16,256]{3,2,1,0:T(8,128)(2,1)S(1)} %bitcast.18, bf16[2,16,16,256]{3,2,1,0:T(8,128)(2,1)S(1)} %bitcast.15, bf16[2,16,16,256]{3,2,1,0:T(8,128)(2,1)S(1)} %bitcast.19, ...), custom_call_target="tpu_custom_call" | custom-call | bytes 2000000 | tf_op jit(solution)/shard_map/place_latents/pallas_call | solution.py:430
  (44 shorter events, 0.8 us)
Async XLA Ops:
  1.6 12.2 %collective-permute-start.8 = (bf16[4,2,8,16,128]{4,3,2,1,0:T(8,128)(2,1)S(1)}, bf16[4,2,8,16,128]{4,3,2,1,0:T(8,128)(2,1)S(1)}, u32[]{:S(2)}, u32[]{:S(2)}) collective-permute-start(bf16[4,2,8,16,128]{4,3,2,1,0:T(8,128)(2,1)S(1)} %cut_tails.1.refs_0_), channel_id=1, source_target_pairs={{0,6},{1,7},{2,4},{3,5},{4,2},{5,3},{6,0},{7,1},{8,14},{9,15},{10,... | collective-permute-start | bytes 786440 | tf_op jit(solution)/shard_map/ppermute | solution.py:443
  5.6 11.9 %collective-permute-start.7 = (bf16[4,2,8,16,128]{4,3,2,1,0:T(8,128)(2,1)S(1)}, bf16[4,2,8,16,128]{4,3,2,1,0:T(8,128)(2,1)S(1)}, u32[]{:S(2)}, u32[]{:S(2)}) collective-permute-start(bf16[4,2,8,16,128]{4,3,2,1,0:T(8,128)(2,1)S(1)} %cut_tails.1.refs_0_), channel_id=1, source_target_pairs={{0,4},{1,5},{2,6},{3,7},{4,0},{5,1},{6,2},{7,3},{8,12},{9,13},{10,... | collective-permute-start | bytes 786440 | tf_op jit(solution)/shard_map/ppermute | solution.py:443
  6.1 11.7 %collective-permute-start.6 = (bf16[4,2,8,16,128]{4,3,2,1,0:T(8,128)(2,1)S(1)}, bf16[4,2,8,16,128]{4,3,2,1,0:T(8,128)(2,1)S(1)}, u32[]{:S(2)}, u32[]{:S(2)}) collective-permute-start(bf16[4,2,8,16,128]{4,3,2,1,0:T(8,128)(2,1)S(1)} %cut_tails.1.refs_0_), channel_id=1, source_target_pairs={{0,2},{1,3},{2,0},{3,1},{4,6},{5,7},{6,4},{7,5},{8,10},{9,11},{10,... | collective-permute-start | bytes 786440 | tf_op jit(solution)/shard_map/ppermute | solution.py:443
  6.2 17.1 %collective-permute-start.4 = (bf16[4,8,8,16,128]{4,3,2,1,0:T(8,128)(2,1)}, bf16[4,8,8,16,128]{4,3,2,1,0:T(8,128)(2,1)S(1)}, u32[]{:S(2)}, u32[]{:S(2)}) collective-permute-start(bf16[4,8,8,16,128]{4,3,2,1,0:T(8,128)(2,1)} %bitcast.1.x_ref.xs_ref), channel_id=1, source_target_pairs={{0,1},{1,0},{2,3},{3,2},{4,5},{5,4},{6,7},{7,6},{8,9},{9,8},{10,11... | collective-permute-start | bytes 3145736 | tf_op jit(solution)/shard_map/ppermute | solution.py:443
  6.2 17.1 %collective-permute-start.5 = (bf16[4,4,128,256]{3,2,1,0:T(8,128)(2,1)}, bf16[4,4,128,256]{3,2,1,0:T(8,128)(2,1)S(1)}, u32[]{:S(2)}, u32[]{:S(2)}) collective-permute-start(bf16[4,4,128,256]{3,2,1,0:T(8,128)(2,1)} %bitcast.12), channel_id=1, source_target_pairs={{0,1},{1,0},{2,3},{3,2},{4,5},{5,4},{6,7},{7,6},{8,9},{9,8},{10,11... | collective-permute-start | bytes 3145736 | tf_op jit(solution)/shard_map/ppermute | solution.py:443
  6.7 16.6 %copy-start.4 = (s32[4]{0:T(128)S(1)}, s32[4]{0:T(128)}, u32[]{:S(2)}) copy-start(s32[4]{0:T(128)} %counts.3) | copy-start | bytes 52
  17.8 1.5 %collective-permute-start.9 = (bf16[4,2,8,16,128]{4,3,2,1,0:T(8,128)(2,1)S(1)}, bf16[4,2,8,16,128]{4,3,2,1,0:T(8,128)(2,1)S(1)}, u32[]{:S(2)}, u32[]{:S(2)}) collective-permute-start(bf16[4,2,8,16,128]{4,3,2,1,0:T(8,128)(2,1)S(1)} %cut_tails.1.refs_0_), channel_id=1, source_target_pairs={{0,1},{1,0},{2,3},{3,2},{4,5},{5,4},{6,7},{7,6},{8,9},{9,8},{10,11... | collective-permute-start | bytes 786440 | tf_op jit(solution)/shard_map/ppermute | solution.py:443
  17.8 1.9 %collective-permute-start.10 = (bf16[4,2,8,16,128]{4,3,2,1,0:T(8,128)(2,1)S(1)}, bf16[4,2,8,16,128]{4,3,2,1,0:T(8,128)(2,1)S(1)}, u32[]{:S(2)}, u32[]{:S(2)}) collective-permute-start(bf16[4,2,8,16,128]{4,3,2,1,0:T(8,128)(2,1)S(1)} %collective-permute-done.6.refs_2_), channel_id=1, source_target_pairs={{0,1},{1,0},{2,3},{3,2},{4,5},{5,4},{6,7},{7,6},{8,9},{9,8},{10,11... | collective-permute-start | bytes 786440 | tf_op jit(solution)/shard_map/ppermute | solution.py:443
  18.3 2.9 %collective-permute-start.11 = (bf16[4,2,8,16,128]{4,3,2,1,0:T(8,128)(2,1)S(1)}, bf16[4,2,8,16,128]{4,3,2,1,0:T(8,128)(2,1)S(1)}, u32[]{:S(2)}, u32[]{:S(2)}) collective-permute-start(bf16[4,2,8,16,128]{4,3,2,1,0:T(8,128)(2,1)S(1)} %collective-permute-done.7.refs_4_), channel_id=1, source_target_pairs={{0,1},{1,0},{2,3},{3,2},{4,5},{5,4},{6,7},{7,6},{8,9},{9,8},{10,11... | collective-permute-start | bytes 786440 | tf_op jit(solution)/shard_map/ppermute | solution.py:443
  19.3 2.5 %collective-permute-start.12 = (bf16[4,2,8,16,128]{4,3,2,1,0:T(8,128)(2,1)S(1)}, bf16[4,2,8,16,128]{4,3,2,1,0:T(8,128)(2,1)S(1)}, u32[]{:S(2)}, u32[]{:S(2)}) collective-permute-start(bf16[4,2,8,16,128]{4,3,2,1,0:T(8,128)(2,1)S(1)} %collective-permute-done.8.refs_6_), channel_id=1, source_target_pairs={{0,1},{1,0},{2,3},{3,2},{4,5},{5,4},{6,7},{7,6},{8,9},{9,8},{10,11... | collective-permute-start | bytes 786440 | tf_op jit(solution)/shard_map/ppermute | solution.py:443
  19.7 15.1 %collective-permute-start.1 = (bf16[2,320,256]{2,1,0:T(8,128)(2,1)S(1)}, bf16[2,320,256]{2,1,0:T(8,128)(2,1)S(1)}, u32[]{:S(2)}, u32[]{:S(2)}) collective-permute-start(bf16[2,320,256]{2,1,0:T(8,128)(2,1)S(1)} %get-tuple-element.25), channel_id=1, source_target_pairs={{0,2},{1,3},{2,0},{3,1},{4,6},{5,7},{6,4},{7,5},{8,10},{9,11},{10,... | collective-permute-start | bytes 983048 | tf_op jit(solution)/shard_map/ppermute | solution.py:443
  21.2 16.5 %collective-permute-start.2 = (bf16[2,320,256]{2,1,0:T(8,128)(2,1)S(1)}, bf16[2,320,256]{2,1,0:T(8,128)(2,1)S(1)}, u32[]{:S(2)}, u32[]{:S(2)}) collective-permute-start(bf16[2,320,256]{2,1,0:T(8,128)(2,1)S(1)} %get-tuple-element.26), channel_id=1, source_target_pairs={{0,4},{1,5},{2,6},{3,7},{4,0},{5,1},{6,2},{7,3},{8,12},{9,13},{10,... | collective-permute-start | bytes 983048 | tf_op jit(solution)/shard_map/ppermute | solution.py:443
  21.8 19.9 %copy-start.1 = (bf16[256,768]{1,0:T(8,128)(2,1)S(1)}, bf16[256,768]{1,0:T(8,128)(2,1)}, u32[]{:S(2)}) copy-start(bf16[256,768]{1,0:T(8,128)(2,1)} %qkv_ref.1) | copy-start | bytes 1179652
  21.8 19.9 %copy-start.2 = (bf16[256,256]{1,0:T(8,128)(2,1)S(1)}, bf16[256,256]{1,0:T(8,128)(2,1)}, u32[]{:S(2)}) copy-start(bf16[256,256]{1,0:T(8,128)(2,1)} %last_ref.1) | copy-start | bytes 393220
  21.8 19.9 %copy-start.5 = (f32[4]{0:T(128)S(1)}, f32[4]{0:T(128)}, u32[]{:S(2)}) copy-start(f32[4]{0:T(128)} %scale.1) | copy-start | bytes 52
  21.8 15.9 %collective-permute-start.3 = (bf16[2,320,256]{2,1,0:T(8,128)(2,1)S(1)}, bf16[2,320,256]{2,1,0:T(8,128)(2,1)S(1)}, u32[]{:S(2)}, u32[]{:S(2)}) collective-permute-start(bf16[2,320,256]{2,1,0:T(8,128)(2,1)S(1)} %get-tuple-element.27), channel_id=1, source_target_pairs={{0,6},{1,7},{2,4},{3,5},{4,2},{5,3},{6,0},{7,1},{8,14},{9,15},{10,... | collective-permute-start | bytes 983048 | tf_op jit(solution)/shard_map/ppermute | solution.py:443
  23.3 15.6 %collective-permute-start = (bf16[2,320,256]{2,1,0:T(8,128)(2,1)S(1)}, bf16[2,320,256]{2,1,0:T(8,128)(2,1)S(1)}, u32[]{:S(2)}, u32[]{:S(2)}) collective-permute-start(bf16[2,320,256]{2,1,0:T(8,128)(2,1)S(1)} %get-tuple-element.24.refs_0_), channel_id=1, source_target_pairs={{0,1},{1,0},{2,3},{3,2},{4,5},{5,4},{6,7},{7,6},{8,9},{9,8},{10,11... | collective-permute-start | bytes 983048 | tf_op jit(solution)/shard_map/ppermute | solution.py:443
  37.7 2.5 %collective-permute-start.13 = (bf16[2,320,256]{2,1,0:T(8,128)(2,1)S(1)}, bf16[2,320,256]{2,1,0:T(8,128)(2,1)S(1)}, u32[]{:S(2)}, u32[]{:S(2)}) collective-permute-start(bf16[2,320,256]{2,1,0:T(8,128)(2,1)S(1)} %collective-permute-done.1.refs_2_), channel_id=1, source_target_pairs={{0,1},{1,0},{2,3},{3,2},{4,5},{5,4},{6,7},{7,6},{8,9},{9,8},{10,11... | collective-permute-start | bytes 983048 | tf_op jit(solution)/shard_map/ppermute | solution.py:443
  37.7 4.0 %collective-permute-start.14 = (bf16[2,320,256]{2,1,0:T(8,128)(2,1)S(1)}, bf16[2,320,256]{2,1,0:T(8,128)(2,1)S(1)}, u32[]{:S(2)}, u32[]{:S(2)}) collective-permute-start(bf16[2,320,256]{2,1,0:T(8,128)(2,1)S(1)} %collective-permute-done.2.refs_4_), channel_id=1, source_target_pairs={{0,1},{1,0},{2,3},{3,2},{4,5},{5,4},{6,7},{7,6},{8,9},{9,8},{10,11... | collective-permute-start | bytes 983048 | tf_op jit(solution)/shard_map/ppermute | solution.py:443
  38.2 3.5 %collective-permute-start.15 = (bf16[2,320,256]{2,1,0:T(8,128)(2,1)S(1)}, bf16[2,320,256]{2,1,0:T(8,128)(2,1)S(1)}, u32[]{:S(2)}, u32[]{:S(2)}) collective-permute-start(bf16[2,320,256]{2,1,0:T(8,128)(2,1)S(1)} %collective-permute-done.3.refs_6_), channel_id=1, source_target_pairs={{0,1},{1,0},{2,3},{3,2},{4,5},{5,4},{6,7},{7,6},{8,9},{9,8},{10,11... | collective-permute-start | bytes 983048 | tf_op jit(solution)/shard_map/ppermute | solution.py:443
  38.2 10.6 %collective-permute-start.23 = (bf16[432,256]{1,0:T(8,128)(2,1)S(1)}, bf16[432,256]{1,0:T(8,128)(2,1)S(1)}, u32[]{:S(2)}, u32[]{:S(2)}) collective-permute-start(bf16[432,256]{1,0:T(8,128)(2,1)S(1)} %get-tuple-element.32), channel_id=1, source_target_pairs={{0,2},{1,3},{2,0},{3,1},{4,6},{5,7},{6,4},{7,5},{8,10},{9,11},{10,... | collective-permute-start | bytes 663560 | tf_op jit(solution)/shard_map/ppermute | solution.py:443
  38.9 12.3 %collective-permute-start.24 = (bf16[432,256]{1,0:T(8,128)(2,1)S(1)}, bf16[432,256]{1,0:T(8,128)(2,1)S(1)}, u32[]{:S(2)}, u32[]{:S(2)}) collective-permute-start(bf16[432,256]{1,0:T(8,128)(2,1)S(1)} %get-tuple-element.33), channel_id=1, source_target_pairs={{0,4},{1,5},{2,6},{3,7},{4,0},{5,1},{6,2},{7,3},{8,12},{9,13},{10,... | collective-permute-start | bytes 663560 | tf_op jit(solution)/shard_map/ppermute | solution.py:443
  40.2 11.0 %collective-permute-start.25 = (bf16[432,256]{1,0:T(8,128)(2,1)S(1)}, bf16[432,256]{1,0:T(8,128)(2,1)S(1)}, u32[]{:S(2)}, u32[]{:S(2)}) collective-permute-start(bf16[432,256]{1,0:T(8,128)(2,1)S(1)} %get-tuple-element.34), channel_id=1, source_target_pairs={{0,6},{1,7},{2,4},{3,5},{4,2},{5,3},{6,0},{7,1},{8,14},{9,15},{10,... | collective-permute-start | bytes 663560 | tf_op jit(solution)/shard_map/ppermute | solution.py:443
  51.3 6.8 %collective-permute-start.26 = (bf16[432,256]{1,0:T(8,128)(2,1)S(1)}, bf16[432,256]{1,0:T(8,128)(2,1)S(1)}, u32[]{:S(2)}, u32[]{:S(2)}) collective-permute-start(bf16[432,256]{1,0:T(8,128)(2,1)S(1)} %add_convert_fusion.1), channel_id=1, source_target_pairs={{0,8},{8,0},{16,24},{24,16},{1,9},{9,1},{17,25},{25,17},{2,10},{10... | collective-permute-start | bytes 663560 | tf_op jit(solution)/shard_map/ppermute | solution.py:443
  52.9 9.2 %collective-permute-start.17 = (bf16[2,256,256]{2,1,0:T(8,128)(2,1)S(1)}, bf16[2,256,256]{2,1,0:T(8,128)(2,1)S(1)}, u32[]{:S(2)}, u32[]{:S(2)}) collective-permute-start(bf16[2,256,256]{2,1,0:T(8,128)(2,1)S(1)} %get-tuple-element.39), channel_id=1, source_target_pairs={{0,2},{1,3},{2,0},{3,1},{4,6},{5,7},{6,4},{7,5},{8,10},{9,11},{10,... | collective-permute-start | bytes 786440 | tf_op jit(solution)/shard_map/ppermute | solution.py:443
  54.3 12.7 %collective-permute-start.19 = (bf16[2,256,256]{2,1,0:T(8,128)(2,1)S(1)}, bf16[2,256,256]{2,1,0:T(8,128)(2,1)S(1)}, u32[]{:S(2)}, u32[]{:S(2)}) collective-permute-start(bf16[2,256,256]{2,1,0:T(8,128)(2,1)S(1)} %get-tuple-element.40), channel_id=1, source_target_pairs={{0,4},{1,5},{2,6},{3,7},{4,0},{5,1},{6,2},{7,3},{8,12},{9,13},{10,... | collective-permute-start | bytes 786440 | tf_op jit(solution)/shard_map/ppermute | solution.py:443
  55.0 12.0 %collective-permute-start.21 = (bf16[2,256,256]{2,1,0:T(8,128)(2,1)S(1)}, bf16[2,256,256]{2,1,0:T(8,128)(2,1)S(1)}, u32[]{:S(2)}, u32[]{:S(2)}) collective-permute-start(bf16[2,256,256]{2,1,0:T(8,128)(2,1)S(1)} %get-tuple-element.41), channel_id=1, source_target_pairs={{0,6},{1,7},{2,4},{3,5},{4,2},{5,3},{6,0},{7,1},{8,14},{9,15},{10,... | collective-permute-start | bytes 786440 | tf_op jit(solution)/shard_map/ppermute | solution.py:443
  58.2 11.7 %collective-permute-start.27 = (bf16[432,256]{1,0:T(8,128)(2,1)S(1)}, bf16[432,256]{1,0:T(8,128)(2,1)S(1)}, u32[]{:S(2)}, u32[]{:S(2)}) collective-permute-start(bf16[432,256]{1,0:T(8,128)(2,1)S(1)} %add_convert_fusion), channel_id=1, source_target_pairs={{0,16},{8,24},{16,0},{24,8},{1,17},{9,25},{17,1},{25,9},{2,18},{10... | collective-permute-start | bytes 663560 | tf_op jit(solution)/shard_map/ppermute | solution.py:443
  60.9 9.8 %collective-permute-start.16 = (bf16[2,256,256]{2,1,0:T(8,128)(2,1)S(1)}, bf16[2,256,256]{2,1,0:T(8,128)(2,1)S(1)}, u32[]{:S(2)}, u32[]{:S(2)}) collective-permute-start(bf16[2,256,256]{2,1,0:T(8,128)(2,1)S(1)} %get-tuple-element.38), channel_id=1, source_target_pairs={{0,1},{1,0},{2,3},{3,2},{4,5},{5,4},{6,7},{7,6},{8,9},{9,8},{10,11... | collective-permute-start | bytes 786440 | tf_op jit(solution)/shard_map/ppermute | solution.py:443
  62.2 8.6 %collective-permute-start.18 = (bf16[2,256,256]{2,1,0:T(8,128)(2,1)S(1)}, bf16[2,256,256]{2,1,0:T(8,128)(2,1)S(1)}, u32[]{:S(2)}, u32[]{:S(2)}) collective-permute-start(bf16[2,256,256]{2,1,0:T(8,128)(2,1)S(1)} %collective-permute-done.17), channel_id=1, source_target_pairs={{0,1},{1,0},{2,3},{3,2},{4,5},{5,4},{6,7},{7,6},{8,9},{9,8},{10,11... | collective-permute-start | bytes 786440 | tf_op jit(solution)/shard_map/ppermute | solution.py:443
  67.0 3.8 %collective-permute-start.20 = (bf16[2,256,256]{2,1,0:T(8,128)(2,1)S(1)}, bf16[2,256,256]{2,1,0:T(8,128)(2,1)S(1)}, u32[]{:S(2)}, u32[]{:S(2)}) collective-permute-start(bf16[2,256,256]{2,1,0:T(8,128)(2,1)S(1)} %collective-permute-done.19), channel_id=1, source_target_pairs={{0,1},{1,0},{2,3},{3,2},{4,5},{5,4},{6,7},{7,6},{8,9},{9,8},{10,11... | collective-permute-start | bytes 786440 | tf_op jit(solution)/shard_map/ppermute | solution.py:443
  67.0 3.8 %collective-permute-start.22 = (bf16[2,256,256]{2,1,0:T(8,128)(2,1)S(1)}, bf16[2,256,256]{2,1,0:T(8,128)(2,1)S(1)}, u32[]{:S(2)}, u32[]{:S(2)}) collective-permute-start(bf16[2,256,256]{2,1,0:T(8,128)(2,1)S(1)} %collective-permute-done.21), channel_id=1, source_target_pairs={{0,1},{1,0},{2,3},{3,2},{4,5},{5,4},{6,7},{7,6},{8,9},{9,8},{10,11... | collective-permute-start | bytes 786440 | tf_op jit(solution)/shard_map/ppermute | solution.py:443
  (2 other events, 33.1 us)

commit v5 on v4

--- a/solution.py
+++ b/solution.py
@@ -368,7 +368,7 @@
                 q_ref[part, cell, :, lanes] = mixed.reshape(block // FRAMES, FRAMES, 128)
         return carry
 
-    lax.fori_loop(0, cells, mix, 0, unroll=8 if total == block else 1)
+    lax.fori_loop(0, cells, mix, 0, unroll=cells if total == block else 1)
 
     turn = swap_matrix(cells, FRAMES)
 

time: 72 us -> 72 us (level)
  transfers between devices with their start and end apart: 28 -> 28, of which waited for: 10 -> 10; matrix products, arithmetic and copies ran while one was open for 1% -> 1% of each run, Pallas kernels for 36% -> 35%
where the time goes in v5:
time: 72 us; the launch traced here: 71.8 us
  Pallas kernels  27.2 us (38%)
  starting transfers between devices  21.7 us (30%)
  waiting for transfers between devices  21.1 us (29%)
  other arithmetic  1 us (1%)
  between operations  0.78 us (1%)
    ppermute x28, starting transfers between devices, flip(): return lax.ppermute(value, axis, [(i, i ^ bits) for i in range(size)])  21.7 us
    ppermute x28, waiting for transfers between devices, flip(): return lax.ppermute(value, axis, [(i, i ^ bits) for i in range(size)])  21.1 us
    pallas_call x1, Pallas kernels, run_grad(): pl.pallas_call(functools.partial(grad_kernel, chips), out_shape=[jax.Shap...  11.5 us
    pallas_call x1, Pallas kernels, run_conv(): pl.pallas_call(functools.partial(conv_kernel, cells), out_shape=[jax.Shap...  7.07 us
    pallas_call x1, Pallas kernels, run_attend(): pl.pallas_call(functools.partial(attend_kernel, cells, ctx), grid=(1,), o...  6.62 us
  transfers between devices with their start and end apart: 28, of which 10 were waited for; matrix products, arithmetic and copies ran while one was open for 1% of the time, Pallas kernels for 35%

profile of v5, /device:TPU:0, one launch (start us, length us, event | category | flops | bytes accessed | tf_op | source)
XLA Modules:
  0.0 71.8 jit_solution(8590564098892816915)
XLA Ops:
  0.6 1.0 %cut_tails.1.refs_0_ = bf16[4,2,8,16,128]{4,3,2,1,0:T(8,128)(2,1)S(1)} custom-call(bf16[4,8,8,16,128]{4,3,2,1,0:T(8,128)(2,1)} %bitcast.1.x_ref.xs_ref), custom_call_target="tpu_custom_call" | custom-call | bytes 500000 | tf_op jit(solution)/shard_map/cut_tails/pallas_call | solution.py:177
  1.6 4.0 %collective-permute-start.8 = (bf16[4,2,8,16,128]{4,3,2,1,0:T(8,128)(2,1)S(1)}, bf16[4,2,8,16,128]{4,3,2,1,0:T(8,128)(2,1)S(1)}, u32[]{:S(2)}, u32[]{:S(2)}) collective-permute-start(bf16[4,2,8,16,128]{4,3,2,1,0:T(8,128)(2,1)S(1)} %cut_tails.1.refs_0_), channel_id=1, source_target_pairs={{0,6},{1,7},{2,4},{3,5},{4,2},{5,3},{6,0},{7,1},{8,14},{9,15},{10,... | collective-permute-start | bytes 786440 | tf_op jit(solution)/shard_map/ppermute | solution.py:443
  5.6 0.5 collective-permute-start.7
  6.2 0.5 collective-permute-start.5
  6.7 7.1 %conv_forward.1 = (bf16[2,320,256]{2,1,0:T(8,128)(2,1)S(1)}, bf16[2,320,256]{2,1,0:T(8,128)(2,1)S(1)}, bf16[2,320,256]{2,1,0:T(8,128)(2,1)S(1)}, bf16[2,320,256]{2,1,0:T(8,128)(2,1)S(1)}) custom-call(s32[1]{0:T(128)} %bitcast.me_ref, bf16[4,8,8,16,128]{4,3,2,1,0:T(8,128)(2,1)} %bitcast.1.x_ref.xs_ref, bf16[3456,256]{1,0:T(8,128)(2,1)} %w_ref.1), custom_call_target="tpu_custom_call" | custom-call | flops 4800000000 | bytes 4000000 | tf_op jit(solution)/shard_map/conv_forward/pallas_call | solution.py:150
  13.8 3.7 %collective-permute-done.7.refs_4_ = bf16[4,2,8,16,128]{4,3,2,1,0:T(8,128)(2,1)S(1)} collective-permute-done((bf16[4,2,8,16,128]{4,3,2,1,0:T(8,128)(2,1)S(1)}, bf16[4,2,8,16,128]{4,3,2,1,0:T(8,128)(2,1)S(1)}, u32[]{:S(2)}, u32[]{:S(2)}) %collective-permute-start.7) | collective-permute-done | bytes 262176 | tf_op jit(solution)/shard_map/ppermute | solution.py:443
  17.5 0.3 collective-permute-done.6.refs_2_
  17.8 0.5 collective-permute-start.10
  18.3 1.0 %collective-permute-done.9.refs_1_ = bf16[4,2,8,16,128]{4,3,2,1,0:T(8,128)(2,1)S(1)} collective-permute-done((bf16[4,2,8,16,128]{4,3,2,1,0:T(8,128)(2,1)S(1)}, bf16[4,2,8,16,128]{4,3,2,1,0:T(8,128)(2,1)S(1)}, u32[]{:S(2)}, u32[]{:S(2)}) %collective-permute-start.9) | collective-permute-done | bytes 262176 | tf_op jit(solution)/shard_map/ppermute | solution.py:443
  19.7 1.5 %collective-permute-start.1 = (bf16[2,320,256]{2,1,0:T(8,128)(2,1)S(1)}, bf16[2,320,256]{2,1,0:T(8,128)(2,1)S(1)}, u32[]{:S(2)}, u32[]{:S(2)}) collective-permute-start(bf16[2,320,256]{2,1,0:T(8,128)(2,1)S(1)} %get-tuple-element.25), channel_id=1, source_target_pairs={{0,2},{1,3},{2,0},{3,1},{4,6},{5,7},{6,4},{7,5},{8,10},{9,11},{10,... | collective-permute-start | bytes 983048 | tf_op jit(solution)/shard_map/ppermute | solution.py:443
  21.2 0.6 collective-permute-start.2
  21.8 1.5 %collective-permute-start.3 = (bf16[2,320,256]{2,1,0:T(8,128)(2,1)S(1)}, bf16[2,320,256]{2,1,0:T(8,128)(2,1)S(1)}, u32[]{:S(2)}, u32[]{:S(2)}) collective-permute-start(bf16[2,320,256]{2,1,0:T(8,128)(2,1)S(1)} %get-tuple-element.27), channel_id=1, source_target_pairs={{0,6},{1,7},{2,4},{3,5},{4,2},{5,3},{6,0},{7,1},{8,14},{9,15},{10,... | collective-permute-start | bytes 983048 | tf_op jit(solution)/shard_map/ppermute | solution.py:443
  23.3 11.5 %conv_gradient.1 = (f32[432,256]{1,0:T(8,128)S(1)}, bf16[432,256]{1,0:T(8,128)(2,1)S(1)}, bf16[432,256]{1,0:T(8,128)(2,1)S(1)}, bf16[432,256]{1,0:T(8,128)(2,1)S(1)}) custom-call(s32[32]{0:T(128)S(1)} %copy-done.3, s32[4]{0:T(128)S(1)} %copy-done.4, s32[1]{0:T(128)} %bitcast.me_ref, bf16[4,8,8,16,128]{4,3,2,1,0:T(8,128)(2,1)} %bitcast.1.x_ref.xs_ref, ...), custom_call_target="tpu_custom_call" | custom-call | flops 1000 | bytes 1000 | tf_op jit(solution)/shard_map/conv_gradient/pallas_call | solution.py:257
  34.8 2.9 %collective-permute-done.2.refs_4_ = bf16[2,320,256]{2,1,0:T(8,128)(2,1)S(1)} collective-permute-done((bf16[2,320,256]{2,1,0:T(8,128)(2,1)S(1)}, bf16[2,320,256]{2,1,0:T(8,128)(2,1)S(1)}, u32[]{:S(2)}, u32[]{:S(2)}) %collective-permute-start.2) | collective-permute-done | bytes 327712 | tf_op jit(solution)/shard_map/ppermute | solution.py:443
  37.7 0.5 collective-permute-start.14
  38.2 0.6 collective-permute-start.23
  38.9 1.3 %collective-permute-start.24 = (bf16[432,256]{1,0:T(8,128)(2,1)S(1)}, bf16[432,256]{1,0:T(8,128)(2,1)S(1)}, u32[]{:S(2)}, u32[]{:S(2)}) collective-permute-start(bf16[432,256]{1,0:T(8,128)(2,1)S(1)} %get-tuple-element.33), channel_id=1, source_target_pairs={{0,4},{1,5},{2,6},{3,7},{4,0},{5,1},{6,2},{7,3},{8,12},{9,13},{10,... | collective-permute-start | bytes 663560 | tf_op jit(solution)/shard_map/ppermute | solution.py:443
  40.2 1.5 %collective-permute-start.25 = (bf16[432,256]{1,0:T(8,128)(2,1)S(1)}, bf16[432,256]{1,0:T(8,128)(2,1)S(1)}, u32[]{:S(2)}, u32[]{:S(2)}) collective-permute-start(bf16[432,256]{1,0:T(8,128)(2,1)S(1)} %get-tuple-element.34), channel_id=1, source_target_pairs={{0,6},{1,7},{2,4},{3,5},{4,2},{5,3},{6,0},{7,1},{8,14},{9,15},{10,... | collective-permute-start | bytes 663560 | tf_op jit(solution)/shard_map/ppermute | solution.py:443
  41.7 6.6 %attend.1 = (bf16[2,256,256]{2,1,0:T(8,128)(2,1)S(1)}, bf16[2,256,256]{2,1,0:T(8,128)(2,1)S(1)}, bf16[2,256,256]{2,1,0:T(8,128)(2,1)S(1)}, bf16[2,256,256]{2,1,0:T(8,128)(2,1)S(1)}) custom-call(s32[32]{0:T(128)S(1)} %copy-done.3, s32[4]{0:T(128)S(1)} %copy-done.4, f32[4]{0:T(128)S(1)} %copy-done.5, s32[1]{0:T(128)} %bitcast.me_ref, ...), custom_call_target="tpu_custom_call" | custom-call | flops 1000 | bytes 1000 | tf_op jit(solution)/shard_map/attend/pallas_call | solution.py:395
  48.4 2.8 %collective-permute-done.24 = bf16[432,256]{1,0:T(8,128)(2,1)S(1)} collective-permute-done((bf16[432,256]{1,0:T(8,128)(2,1)S(1)}, bf16[432,256]{1,0:T(8,128)(2,1)S(1)}, u32[]{:S(2)}, u32[]{:S(2)}) %collective-permute-start.24) | collective-permute-done | bytes 221216 | tf_op jit(solution)/shard_map/ppermute | solution.py:443
  51.3 1.6 %collective-permute-start.26 = (bf16[432,256]{1,0:T(8,128)(2,1)S(1)}, bf16[432,256]{1,0:T(8,128)(2,1)S(1)}, u32[]{:S(2)}, u32[]{:S(2)}) collective-permute-start(bf16[432,256]{1,0:T(8,128)(2,1)S(1)} %add_convert_fusion.1), channel_id=1, source_target_pairs={{0,8},{8,0},{16,24},{24,16},{1,9},{9,1},{17,25},{25,17},{2,10},{10... | collective-permute-start | bytes 663560 | tf_op jit(solution)/shard_map/ppermute | solution.py:443
  52.9 1.4 %collective-permute-start.17 = (bf16[2,256,256]{2,1,0:T(8,128)(2,1)S(1)}, bf16[2,256,256]{2,1,0:T(8,128)(2,1)S(1)}, u32[]{:S(2)}, u32[]{:S(2)}) collective-permute-start(bf16[2,256,256]{2,1,0:T(8,128)(2,1)S(1)} %get-tuple-element.39), channel_id=1, source_target_pairs={{0,2},{1,3},{2,0},{3,1},{4,6},{5,7},{6,4},{7,5},{8,10},{9,11},{10,... | collective-permute-start | bytes 786440 | tf_op jit(solution)/shard_map/ppermute | solution.py:443
  54.3 0.7 %collective-permute-start.19 = (bf16[2,256,256]{2,1,0:T(8,128)(2,1)S(1)}, bf16[2,256,256]{2,1,0:T(8,128)(2,1)S(1)}, u32[]{:S(2)}, u32[]{:S(2)}) collective-permute-start(bf16[2,256,256]{2,1,0:T(8,128)(2,1)S(1)} %get-tuple-element.40), channel_id=1, source_target_pairs={{0,4},{1,5},{2,6},{3,7},{4,0},{5,1},{6,2},{7,3},{8,12},{9,13},{10,... | collective-permute-start | bytes 786440 | tf_op jit(solution)/shard_map/ppermute | solution.py:443
  55.0 1.4 %collective-permute-start.21 = (bf16[2,256,256]{2,1,0:T(8,128)(2,1)S(1)}, bf16[2,256,256]{2,1,0:T(8,128)(2,1)S(1)}, u32[]{:S(2)}, u32[]{:S(2)}) collective-permute-start(bf16[2,256,256]{2,1,0:T(8,128)(2,1)S(1)} %get-tuple-element.41), channel_id=1, source_target_pairs={{0,6},{1,7},{2,4},{3,5},{4,2},{5,3},{6,0},{7,1},{8,14},{9,15},{10,... | collective-permute-start | bytes 786440 | tf_op jit(solution)/shard_map/ppermute | solution.py:443
  56.4 1.7 %collective-permute-done.26 = bf16[432,256]{1,0:T(8,128)(2,1)S(1)} collective-permute-done((bf16[432,256]{1,0:T(8,128)(2,1)S(1)}, bf16[432,256]{1,0:T(8,128)(2,1)S(1)}, u32[]{:S(2)}, u32[]{:S(2)}) %collective-permute-start.26) | collective-permute-done | bytes 221216 | tf_op jit(solution)/shard_map/ppermute | solution.py:443
  58.2 2.8 %collective-permute-start.27 = (bf16[432,256]{1,0:T(8,128)(2,1)S(1)}, bf16[432,256]{1,0:T(8,128)(2,1)S(1)}, u32[]{:S(2)}, u32[]{:S(2)}) collective-permute-start(bf16[432,256]{1,0:T(8,128)(2,1)S(1)} %add_convert_fusion), channel_id=1, source_target_pairs={{0,16},{8,24},{16,0},{24,8},{1,17},{9,25},{17,1},{25,9},{2,18},{10... | collective-permute-start | bytes 663560 | tf_op jit(solution)/shard_map/ppermute | solution.py:443
  61.0 1.2 %collective-permute-done.17 = bf16[2,256,256]{2,1,0:T(8,128)(2,1)S(1)} collective-permute-done((bf16[2,256,256]{2,1,0:T(8,128)(2,1)S(1)}, bf16[2,256,256]{2,1,0:T(8,128)(2,1)S(1)}, u32[]{:S(2)}, u32[]{:S(2)}) %collective-permute-start.17) | collective-permute-done | bytes 262176 | tf_op jit(solution)/shard_map/ppermute | solution.py:443
  62.2 4.8 %collective-permute-done.19 = bf16[2,256,256]{2,1,0:T(8,128)(2,1)S(1)} collective-permute-done((bf16[2,256,256]{2,1,0:T(8,128)(2,1)S(1)}, bf16[2,256,256]{2,1,0:T(8,128)(2,1)S(1)}, u32[]{:S(2)}, u32[]{:S(2)}) %collective-permute-start.19) | collective-permute-done | bytes 262176 | tf_op jit(solution)/shard_map/ppermute | solution.py:443
  67.0 0.5 collective-permute-start.22
  67.5 2.4 %collective-permute-done.27 = bf16[432,256]{1,0:T(8,128)(2,1)S(1)} collective-permute-done((bf16[432,256]{1,0:T(8,128)(2,1)S(1)}, bf16[432,256]{1,0:T(8,128)(2,1)S(1)}, u32[]{:S(2)}, u32[]{:S(2)}) %collective-permute-start.27) | collective-permute-done | bytes 221216 | tf_op jit(solution)/shard_map/ppermute | solution.py:443
  69.9 0.8 %convert_add_fusion = f32[432,256]{1,0:T(8,128)} fusion(bf16[432,256]{1,0:T(8,128)(2,1)S(1)} %collective-permute-done.27, bf16[432,256]{1,0:T(8,128)(2,1)S(1)} %add_convert_fusion), kind=kLoop, calls=%fused_computation | loop fusion | flops 331776 | bytes 884736 | tf_op jit(solution)/shard_map/add | solution.py:490
  70.8 1.0 %place_latents.1 = bf16[16,8,16,256]{3,2,1,0:T(8,128)(2,1)} custom-call(s32[1]{0:T(128)} %bitcast.me_ref, bf16[2,16,16,256]{3,2,1,0:T(8,128)(2,1)S(1)} %bitcast.14, bf16[2,16,16,256]{3,2,1,0:T(8,128)(2,1)S(1)} %bitcast.18, bf16[2,16,16,256]{3,2,1,0:T(8,128)(2,1)S(1)} %bitcast.15, bf16[2,16,16,256]{3,2,1,0:T(8,128)(2,1)S(1)} %bitcast.19, ...), custom_call_target="tpu_custom_call" | custom-call | bytes 2000000 | tf_op jit(solution)/shard_map/place_latents/pallas_call | solution.py:430
  (44 shorter events, 0.8 us)
Async XLA Ops:
  1.6 12.2 %collective-permute-start.8 = (bf16[4,2,8,16,128]{4,3,2,1,0:T(8,128)(2,1)S(1)}, bf16[4,2,8,16,128]{4,3,2,1,0:T(8,128)(2,1)S(1)}, u32[]{:S(2)}, u32[]{:S(2)}) collective-permute-start(bf16[4,2,8,16,128]{4,3,2,1,0:T(8,128)(2,1)S(1)} %cut_tails.1.refs_0_), channel_id=1, source_target_pairs={{0,6},{1,7},{2,4},{3,5},{4,2},{5,3},{6,0},{7,1},{8,14},{9,15},{10,... | collective-permute-start | bytes 786440 | tf_op jit(solution)/shard_map/ppermute | solution.py:443
  5.6 11.9 %collective-permute-start.7 = (bf16[4,2,8,16,128]{4,3,2,1,0:T(8,128)(2,1)S(1)}, bf16[4,2,8,16,128]{4,3,2,1,0:T(8,128)(2,1)S(1)}, u32[]{:S(2)}, u32[]{:S(2)}) collective-permute-start(bf16[4,2,8,16,128]{4,3,2,1,0:T(8,128)(2,1)S(1)} %cut_tails.1.refs_0_), channel_id=1, source_target_pairs={{0,4},{1,5},{2,6},{3,7},{4,0},{5,1},{6,2},{7,3},{8,12},{9,13},{10,... | collective-permute-start | bytes 786440 | tf_op jit(solution)/shard_map/ppermute | solution.py:443
  6.1 11.7 %collective-permute-start.6 = (bf16[4,2,8,16,128]{4,3,2,1,0:T(8,128)(2,1)S(1)}, bf16[4,2,8,16,128]{4,3,2,1,0:T(8,128)(2,1)S(1)}, u32[]{:S(2)}, u32[]{:S(2)}) collective-permute-start(bf16[4,2,8,16,128]{4,3,2,1,0:T(8,128)(2,1)S(1)} %cut_tails.1.refs_0_), channel_id=1, source_target_pairs={{0,2},{1,3},{2,0},{3,1},{4,6},{5,7},{6,4},{7,5},{8,10},{9,11},{10,... | collective-permute-start | bytes 786440 | tf_op jit(solution)/shard_map/ppermute | solution.py:443
  6.2 17.1 %collective-permute-start.4 = (bf16[4,8,8,16,128]{4,3,2,1,0:T(8,128)(2,1)}, bf16[4,8,8,16,128]{4,3,2,1,0:T(8,128)(2,1)S(1)}, u32[]{:S(2)}, u32[]{:S(2)}) collective-permute-start(bf16[4,8,8,16,128]{4,3,2,1,0:T(8,128)(2,1)} %bitcast.1.x_ref.xs_ref), channel_id=1, source_target_pairs={{0,1},{1,0},{2,3},{3,2},{4,5},{5,4},{6,7},{7,6},{8,9},{9,8},{10,11... | collective-permute-start | bytes 3145736 | tf_op jit(solution)/shard_map/ppermute | solution.py:443
  6.2 17.1 %collective-permute-start.5 = (bf16[4,4,128,256]{3,2,1,0:T(8,128)(2,1)}, bf16[4,4,128,256]{3,2,1,0:T(8,128)(2,1)S(1)}, u32[]{:S(2)}, u32[]{:S(2)}) collective-permute-start(bf16[4,4,128,256]{3,2,1,0:T(8,128)(2,1)} %bitcast.12), channel_id=1, source_target_pairs={{0,1},{1,0},{2,3},{3,2},{4,5},{5,4},{6,7},{7,6},{8,9},{9,8},{10,11... | collective-permute-start | bytes 3145736 | tf_op jit(solution)/shard_map/ppermute | solution.py:443
  6.7 16.6 %copy-start.4 = (s32[4]{0:T(128)S(1)}, s32[4]{0:T(128)}, u32[]{:S(2)}) copy-start(s32[4]{0:T(128)} %counts.3) | copy-start | bytes 52
  17.8 1.5 %collective-permute-start.9 = (bf16[4,2,8,16,128]{4,3,2,1,0:T(8,128)(2,1)S(1)}, bf16[4,2,8,16,128]{4,3,2,1,0:T(8,128)(2,1)S(1)}, u32[]{:S(2)}, u32[]{:S(2)}) collective-permute-start(bf16[4,2,8,16,128]{4,3,2,1,0:T(8,128)(2,1)S(1)} %cut_tails.1.refs_0_), channel_id=1, source_target_pairs={{0,1},{1,0},{2,3},{3,2},{4,5},{5,4},{6,7},{7,6},{8,9},{9,8},{10,11... | collective-permute-start | bytes 786440 | tf_op jit(solution)/shard_map/ppermute | solution.py:443
  17.8 1.9 %collective-permute-start.10 = (bf16[4,2,8,16,128]{4,3,2,1,0:T(8,128)(2,1)S(1)}, bf16[4,2,8,16,128]{4,3,2,1,0:T(8,128)(2,1)S(1)}, u32[]{:S(2)}, u32[]{:S(2)}) collective-permute-start(bf16[4,2,8,16,128]{4,3,2,1,0:T(8,128)(2,1)S(1)} %collective-permute-done.6.refs_2_), channel_id=1, source_target_pairs={{0,1},{1,0},{2,3},{3,2},{4,5},{5,4},{6,7},{7,6},{8,9},{9,8},{10,11... | collective-permute-start | bytes 786440 | tf_op jit(solution)/shard_map/ppermute | solution.py:443
  18.3 2.9 %collective-permute-start.11 = (bf16[4,2,8,16,128]{4,3,2,1,0:T(8,128)(2,1)S(1)}, bf16[4,2,8,16,128]{4,3,2,1,0:T(8,128)(2,1)S(1)}, u32[]{:S(2)}, u32[]{:S(2)}) collective-permute-start(bf16[4,2,8,16,128]{4,3,2,1,0:T(8,128)(2,1)S(1)} %collective-permute-done.7.refs_4_), channel_id=1, source_target_pairs={{0,1},{1,0},{2,3},{3,2},{4,5},{5,4},{6,7},{7,6},{8,9},{9,8},{10,11... | collective-permute-start | bytes 786440 | tf_op jit(solution)/shard_map/ppermute | solution.py:443
  19.3 2.5 %collective-permute-start.12 = (bf16[4,2,8,16,128]{4,3,2,1,0:T(8,128)(2,1)S(1)}, bf16[4,2,8,16,128]{4,3,2,1,0:T(8,128)(2,1)S(1)}, u32[]{:S(2)}, u32[]{:S(2)}) collective-permute-start(bf16[4,2,8,16,128]{4,3,2,1,0:T(8,128)(2,1)S(1)} %collective-permute-done.8.refs_6_), channel_id=1, source_target_pairs={{0,1},{1,0},{2,3},{3,2},{4,5},{5,4},{6,7},{7,6},{8,9},{9,8},{10,11... | collective-permute-start | bytes 786440 | tf_op jit(solution)/shard_map/ppermute | solution.py:443
  19.7 15.1 %collective-permute-start.1 = (bf16[2,320,256]{2,1,0:T(8,128)(2,1)S(1)}, bf16[2,320,256]{2,1,0:T(8,128)(2,1)S(1)}, u32[]{:S(2)}, u32[]{:S(2)}) collective-permute-start(bf16[2,320,256]{2,1,0:T(8,128)(2,1)S(1)} %get-tuple-element.25), channel_id=1, source_target_pairs={{0,2},{1,3},{2,0},{3,1},{4,6},{5,7},{6,4},{7,5},{8,10},{9,11},{10,... | collective-permute-start | bytes 983048 | tf_op jit(solution)/shard_map/ppermute | solution.py:443
  21.2 16.5 %collective-permute-start.2 = (bf16[2,320,256]{2,1,0:T(8,128)(2,1)S(1)}, bf16[2,320,256]{2,1,0:T(8,128)(2,1)S(1)}, u32[]{:S(2)}, u32[]{:S(2)}) collective-permute-start(bf16[2,320,256]{2,1,0:T(8,128)(2,1)S(1)} %get-tuple-element.26), channel_id=1, source_target_pairs={{0,4},{1,5},{2,6},{3,7},{4,0},{5,1},{6,2},{7,3},{8,12},{9,13},{10,... | collective-permute-start | bytes 983048 | tf_op jit(solution)/shard_map/ppermute | solution.py:443
  21.8 19.9 %copy-start.1 = (bf16[256,768]{1,0:T(8,128)(2,1)S(1)}, bf16[256,768]{1,0:T(8,128)(2,1)}, u32[]{:S(2)}) copy-start(bf16[256,768]{1,0:T(8,128)(2,1)} %qkv_ref.1) | copy-start | bytes 1179652
  21.8 19.9 %copy-start.2 = (bf16[256,256]{1,0:T(8,128)(2,1)S(1)}, bf16[256,256]{1,0:T(8,128)(2,1)}, u32[]{:S(2)}) copy-start(bf16[256,256]{1,0:T(8,128)(2,1)} %last_ref.1) | copy-start | bytes 393220
  21.8 19.9 %copy-start.5 = (f32[4]{0:T(128)S(1)}, f32[4]{0:T(128)}, u32[]{:S(2)}) copy-start(f32[4]{0:T(128)} %scale.1) | copy-start | bytes 52
  21.8 15.9 %collective-permute-start.3 = (bf16[2,320,256]{2,1,0:T(8,128)(2,1)S(1)}, bf16[2,320,256]{2,1,0:T(8,128)(2,1)S(1)}, u32[]{:S(2)}, u32[]{:S(2)}) collective-permute-start(bf16[2,320,256]{2,1,0:T(8,128)(2,1)S(1)} %get-tuple-element.27), channel_id=1, source_target_pairs={{0,6},{1,7},{2,4},{3,5},{4,2},{5,3},{6,0},{7,1},{8,14},{9,15},{10,... | collective-permute-start | bytes 983048 | tf_op jit(solution)/shard_map/ppermute | solution.py:443
  23.3 15.6 %collective-permute-start = (bf16[2,320,256]{2,1,0:T(8,128)(2,1)S(1)}, bf16[2,320,256]{2,1,0:T(8,128)(2,1)S(1)}, u32[]{:S(2)}, u32[]{:S(2)}) collective-permute-start(bf16[2,320,256]{2,1,0:T(8,128)(2,1)S(1)} %get-tuple-element.24.refs_0_), channel_id=1, source_target_pairs={{0,1},{1,0},{2,3},{3,2},{4,5},{5,4},{6,7},{7,6},{8,9},{9,8},{10,11... | collective-permute-start | bytes 983048 | tf_op jit(solution)/shard_map/ppermute | solution.py:443
  37.7 2.5 %collective-permute-start.13 = (bf16[2,320,256]{2,1,0:T(8,128)(2,1)S(1)}, bf16[2,320,256]{2,1,0:T(8,128)(2,1)S(1)}, u32[]{:S(2)}, u32[]{:S(2)}) collective-permute-start(bf16[2,320,256]{2,1,0:T(8,128)(2,1)S(1)} %collective-permute-done.1.refs_2_), channel_id=1, source_target_pairs={{0,1},{1,0},{2,3},{3,2},{4,5},{5,4},{6,7},{7,6},{8,9},{9,8},{10,11... | collective-permute-start | bytes 983048 | tf_op jit(solution)/shard_map/ppermute | solution.py:443
  37.7 4.0 %collective-permute-start.14 = (bf16[2,320,256]{2,1,0:T(8,128)(2,1)S(1)}, bf16[2,320,256]{2,1,0:T(8,128)(2,1)S(1)}, u32[]{:S(2)}, u32[]{:S(2)}) collective-permute-start(bf16[2,320,256]{2,1,0:T(8,128)(2,1)S(1)} %collective-permute-done.2.refs_4_), channel_id=1, source_target_pairs={{0,1},{1,0},{2,3},{3,2},{4,5},{5,4},{6,7},{7,6},{8,9},{9,8},{10,11... | collective-permute-start | bytes 983048 | tf_op jit(solution)/shard_map/ppermute | solution.py:443
  38.2 3.5 %collective-permute-start.15 = (bf16[2,320,256]{2,1,0:T(8,128)(2,1)S(1)}, bf16[2,320,256]{2,1,0:T(8,128)(2,1)S(1)}, u32[]{:S(2)}, u32[]{:S(2)}) collective-permute-start(bf16[2,320,256]{2,1,0:T(8,128)(2,1)S(1)} %collective-permute-done.3.refs_6_), channel_id=1, source_target_pairs={{0,1},{1,0},{2,3},{3,2},{4,5},{5,4},{6,7},{7,6},{8,9},{9,8},{10,11... | collective-permute-start | bytes 983048 | tf_op jit(solution)/shard_map/ppermute | solution.py:443
  38.2 10.2 %collective-permute-start.23 = (bf16[432,256]{1,0:T(8,128)(2,1)S(1)}, bf16[432,256]{1,0:T(8,128)(2,1)S(1)}, u32[]{:S(2)}, u32[]{:S(2)}) collective-permute-start(bf16[432,256]{1,0:T(8,128)(2,1)S(1)} %get-tuple-element.32), channel_id=1, source_target_pairs={{0,2},{1,3},{2,0},{3,1},{4,6},{5,7},{6,4},{7,5},{8,10},{9,11},{10,... | collective-permute-start | bytes 663560 | tf_op jit(solution)/shard_map/ppermute | solution.py:443
  38.9 12.3 %collective-permute-start.24 = (bf16[432,256]{1,0:T(8,128)(2,1)S(1)}, bf16[432,256]{1,0:T(8,128)(2,1)S(1)}, u32[]{:S(2)}, u32[]{:S(2)}) collective-permute-start(bf16[432,256]{1,0:T(8,128)(2,1)S(1)} %get-tuple-element.33), channel_id=1, source_target_pairs={{0,4},{1,5},{2,6},{3,7},{4,0},{5,1},{6,2},{7,3},{8,12},{9,13},{10,... | collective-permute-start | bytes 663560 | tf_op jit(solution)/shard_map/ppermute | solution.py:443
  40.2 11.0 %collective-permute-start.25 = (bf16[432,256]{1,0:T(8,128)(2,1)S(1)}, bf16[432,256]{1,0:T(8,128)(2,1)S(1)}, u32[]{:S(2)}, u32[]{:S(2)}) collective-permute-start(bf16[432,256]{1,0:T(8,128)(2,1)S(1)} %get-tuple-element.34), channel_id=1, source_target_pairs={{0,6},{1,7},{2,4},{3,5},{4,2},{5,3},{6,0},{7,1},{8,14},{9,15},{10,... | collective-permute-start | bytes 663560 | tf_op jit(solution)/shard_map/ppermute | solution.py:443
  51.3 6.8 %collective-permute-start.26 = (bf16[432,256]{1,0:T(8,128)(2,1)S(1)}, bf16[432,256]{1,0:T(8,128)(2,1)S(1)}, u32[]{:S(2)}, u32[]{:S(2)}) collective-permute-start(bf16[432,256]{1,0:T(8,128)(2,1)S(1)} %add_convert_fusion.1), channel_id=1, source_target_pairs={{0,8},{8,0},{16,24},{24,16},{1,9},{9,1},{17,25},{25,17},{2,10},{10... | collective-permute-start | bytes 663560 | tf_op jit(solution)/shard_map/ppermute | solution.py:443
  52.9 9.2 %collective-permute-start.17 = (bf16[2,256,256]{2,1,0:T(8,128)(2,1)S(1)}, bf16[2,256,256]{2,1,0:T(8,128)(2,1)S(1)}, u32[]{:S(2)}, u32[]{:S(2)}) collective-permute-start(bf16[2,256,256]{2,1,0:T(8,128)(2,1)S(1)} %get-tuple-element.39), channel_id=1, source_target_pairs={{0,2},{1,3},{2,0},{3,1},{4,6},{5,7},{6,4},{7,5},{8,10},{9,11},{10,... | collective-permute-start | bytes 786440 | tf_op jit(solution)/shard_map/ppermute | solution.py:443
  54.3 12.7 %collective-permute-start.19 = (bf16[2,256,256]{2,1,0:T(8,128)(2,1)S(1)}, bf16[2,256,256]{2,1,0:T(8,128)(2,1)S(1)}, u32[]{:S(2)}, u32[]{:S(2)}) collective-permute-start(bf16[2,256,256]{2,1,0:T(8,128)(2,1)S(1)} %get-tuple-element.40), channel_id=1, source_target_pairs={{0,4},{1,5},{2,6},{3,7},{4,0},{5,1},{6,2},{7,3},{8,12},{9,13},{10,... | collective-permute-start | bytes 786440 | tf_op jit(solution)/shard_map/ppermute | solution.py:443
  55.0 12.0 %collective-permute-start.21 = (bf16[2,256,256]{2,1,0:T(8,128)(2,1)S(1)}, bf16[2,256,256]{2,1,0:T(8,128)(2,1)S(1)}, u32[]{:S(2)}, u32[]{:S(2)}) collective-permute-start(bf16[2,256,256]{2,1,0:T(8,128)(2,1)S(1)} %get-tuple-element.41), channel_id=1, source_target_pairs={{0,6},{1,7},{2,4},{3,5},{4,2},{5,3},{6,0},{7,1},{8,14},{9,15},{10,... | collective-permute-start | bytes 786440 | tf_op jit(solution)/shard_map/ppermute | solution.py:443
  58.2 11.7 %collective-permute-start.27 = (bf16[432,256]{1,0:T(8,128)(2,1)S(1)}, bf16[432,256]{1,0:T(8,128)(2,1)S(1)}, u32[]{:S(2)}, u32[]{:S(2)}) collective-permute-start(bf16[432,256]{1,0:T(8,128)(2,1)S(1)} %add_convert_fusion), channel_id=1, source_target_pairs={{0,16},{8,24},{16,0},{24,8},{1,17},{9,25},{17,1},{25,9},{2,18},{10... | collective-permute-start | bytes 663560 | tf_op jit(solution)/shard_map/ppermute | solution.py:443
  60.9 9.8 %collective-permute-start.16 = (bf16[2,256,256]{2,1,0:T(8,128)(2,1)S(1)}, bf16[2,256,256]{2,1,0:T(8,128)(2,1)S(1)}, u32[]{:S(2)}, u32[]{:S(2)}) collective-permute-start(bf16[2,256,256]{2,1,0:T(8,128)(2,1)S(1)} %get-tuple-element.38), channel_id=1, source_target_pairs={{0,1},{1,0},{2,3},{3,2},{4,5},{5,4},{6,7},{7,6},{8,9},{9,8},{10,11... | collective-permute-start | bytes 786440 | tf_op jit(solution)/shard_map/ppermute | solution.py:443
  62.2 8.6 %collective-permute-start.18 = (bf16[2,256,256]{2,1,0:T(8,128)(2,1)S(1)}, bf16[2,256,256]{2,1,0:T(8,128)(2,1)S(1)}, u32[]{:S(2)}, u32[]{:S(2)}) collective-permute-start(bf16[2,256,256]{2,1,0:T(8,128)(2,1)S(1)} %collective-permute-done.17), channel_id=1, source_target_pairs={{0,1},{1,0},{2,3},{3,2},{4,5},{5,4},{6,7},{7,6},{8,9},{9,8},{10,11... | collective-permute-start | bytes 786440 | tf_op jit(solution)/shard_map/ppermute | solution.py:443
  67.0 3.8 %collective-permute-start.20 = (bf16[2,256,256]{2,1,0:T(8,128)(2,1)S(1)}, bf16[2,256,256]{2,1,0:T(8,128)(2,1)S(1)}, u32[]{:S(2)}, u32[]{:S(2)}) collective-permute-start(bf16[2,256,256]{2,1,0:T(8,128)(2,1)S(1)} %collective-permute-done.19), channel_id=1, source_target_pairs={{0,1},{1,0},{2,3},{3,2},{4,5},{5,4},{6,7},{7,6},{8,9},{9,8},{10,11... | collective-permute-start | bytes 786440 | tf_op jit(solution)/shard_map/ppermute | solution.py:443
  67.0 3.8 %collective-permute-start.22 = (bf16[2,256,256]{2,1,0:T(8,128)(2,1)S(1)}, bf16[2,256,256]{2,1,0:T(8,128)(2,1)S(1)}, u32[]{:S(2)}, u32[]{:S(2)}) collective-permute-start(bf16[2,256,256]{2,1,0:T(8,128)(2,1)S(1)} %collective-permute-done.21), channel_id=1, source_target_pairs={{0,1},{1,0},{2,3},{3,2},{4,5},{5,4},{6,7},{7,6},{8,9},{9,8},{10,11... | collective-permute-start | bytes 786440 | tf_op jit(solution)/shard_map/ppermute | solution.py:443
  (2 other events, 33.1 us)
